TPU v7x, 512 devices: a whole 4x8x8 slice. The times are simulated.
512 devices in a mesh: seq: 32 (over z_hi, y, core), chan: 16 (over x, z_lo).
Axes of the slice: x: 4, y: 8, z: 8 (z_hi: 2, z_lo: 4; z = z_hi * 4 + z_lo), core: 2. Of those that a mesh axis runs over, the one named last changes fastest.
Arguments:
- query: bfloat16 [131072, 256], P(('seq', 'chan')), may hold values from -6 to 6
- keys: bfloat16 [131072, 256], P(('seq', 'chan')), may hold values from -6 to 6
- values: bfloat16 [131072, 256], P(('seq', 'chan')), may hold values from -6 to 6
- decay: float32 [32, 16], P('chan'), may hold values from 3.8146973e-06 to 0.03
- residue: float32 [32, 16], P('chan'), may hold values from -2.5 to 2.5
- skip: float32 [256], P('chan'), may hold values from 0.5 to 1.5
Outputs:
- gated: bfloat16 [131072, 256], P(('seq', 'chan'))
All inputs are finite; a program needn't handle non-finite values.
Results may differ from a plain program's by a relative error of at most 0.0085.
Values may be sent and summed in bfloat16 or wider, within the bound.
No kernel may reach another device: no remote copies, remote signals or barrier semaphores. Data moves between devices by JAX's collectives and lax.ppermute only.
A program may use at most 128 MiB of HBM per device.

v0:
```python
import functools

import jax
import jax.numpy as jnp
from jax import lax
from jax.experimental import pallas as pl
from jax.experimental.pallas import tpu as pltpu
from jax.sharding import PartitionSpec as P

F32 = jnp.float32
BF16 = jnp.bfloat16
VMEM = pl.BlockSpec(memory_space=pltpu.VMEM)
SMEM = pl.BlockSpec(memory_space=pltpu.SMEM)
NT = (((1,), (1,)), ((), ()))


def call(body, out_shape, in_specs, flops, nbytes, **kw):
    return pl.pallas_call(
        body,
        out_shape=out_shape,
        in_specs=in_specs,
        out_specs=jax.tree.map(lambda _: VMEM, out_shape),
        cost_estimate=pl.CostEstimate(flops=flops, bytes_accessed=nbytes, transcendentals=0),
        **kw,
    )


def split(table):
    high = table.astype(BF16)
    return high, (table - high.astype(F32)).astype(BF16)


def dot(a, b):
    return jnp.dot(a, b, preferred_element_type=F32)


def own_group(shape, group_rows, modes):
    row = lax.broadcasted_iota(jnp.int32, shape, len(shape) - 2)
    lane = lax.broadcasted_iota(jnp.int32, shape, len(shape) - 1)
    return (row // group_rows) == (lane // modes)


def gate_in_kernel(keys_ref, values_ref, out_ref):
    z = keys_ref[...].astype(F32) * values_ref[...].astype(F32)
    out_ref[...] = z.T.astype(BF16).reshape(out_ref.shape)


def table_kernel(dims, seq_ref, decay_ref, high_ref, low_ref, step_ref, grow_ref, seq_w_ref):
    blocks, rows, length, modes, group_rows = dims
    decay = decay_ref[...]
    lanes = decay.shape[1]
    back = (length - 1) - lax.broadcasted_iota(jnp.int32, (length, lanes), 0)
    high, low = split(jnp.exp(-decay * back.astype(F32)))
    high_ref[...] = high
    low_ref[...] = low
    step_ref[...] = jnp.exp(-decay * float(length))
    shape = (blocks, rows, lanes)
    block = lax.broadcasted_iota(jnp.int32, shape, 0)
    grow = jnp.exp(-decay[None] * (block * length).astype(F32))
    grow_ref[...] = jnp.where(own_group(shape, group_rows, modes), grow, 0.0)
    shape = seq_w_ref.shape
    gap = seq_ref[0] - 1 - lax.broadcasted_iota(jnp.int32, shape, 0)
    away = jnp.maximum(gap, 0) * (blocks * length)
    seq_w_ref[...] = jnp.where(gap >= 0, jnp.exp(-decay[None] * away.astype(F32)), 0.0)


def state_kernel(dims, z_ref, high_ref, low_ref, step_ref, state_ref, end_ref):
    blocks, rows, length, modes, group_rows = dims
    z = z_ref[...].reshape(blocks * rows, length)
    ends = dot(z, high_ref[...]) + dot(z, low_ref[...])
    lanes = ends.shape[1]
    mine = own_group((rows, lanes), group_rows, modes)
    step = step_ref[...]
    state = jnp.zeros((rows, lanes), F32)
    for b in range(blocks):
        state_ref[b] = state
        state = state * step + jnp.where(mine, ends[b * rows : (b + 1) * rows], 0.0)
    folded = state[:group_rows]
    for g in range(1, rows // group_rows):
        folded = folded + state[g * group_rows : (g + 1) * group_rows]
    end_ref[...] = jnp.broadcast_to(folded[None], end_ref.shape)


def local_kernel(dims, z_ref, state_ref, decay_ref, residue_ref, skip_ref, out_ref, table_ref):
    blocks, rows, length, modes, group_rows = dims
    decay = decay_ref[...]
    lanes = decay.shape[1]
    amplitude = residue_ref[...] * jnp.sqrt(2.0 * decay)
    position = lax.broadcasted_iota(jnp.int32, (length, lanes), 0).astype(F32)
    rise = jnp.exp(decay * position)
    fall = amplitude * jnp.exp(-decay * position)
    after = amplitude * jnp.exp(-decay * (position + 1.0))
    table_ref[...] = after
    z = z_ref[...].reshape(blocks * rows, length)
    row = lax.broadcasted_iota(jnp.int32, (length, length), 0)
    col = lax.broadcasted_iota(jnp.int32, (length, length), 1)
    lane = lax.broadcasted_iota(jnp.int32, (length, lanes), 1)
    groups = rows // group_rows
    parts = []
    for g in range(groups):
        taps = lax.dot_general(
            jnp.where(lane // modes == g, rise, 0.0), fall, NT,
            precision=lax.Precision.HIGHEST, preferred_element_type=F32,
        )
        high, low = split(jnp.where(row <= col, taps, 0.0))
        conv = (dot(z, high) + dot(z, low)).reshape(blocks, groups, group_rows, length)
        parts.append(conv[:, g])
    local = jnp.stack(parts, axis=1).reshape(blocks, rows, length)
    carried = lax.dot_general(
        state_ref[...].reshape(blocks * rows, lanes), after, NT,
        precision=lax.Precision.HIGHEST, preferred_element_type=F32,
    ).reshape(blocks, rows, length)
    out_ref[...] = local + carried + skip_ref[...][None] * z_ref[...].astype(F32)


def carry_kernel(dims, ends_ref, seq_w_ref, grow_ref, table_ref, local_ref, out_ref):
    blocks, rows, length, modes, group_rows = dims
    enter = jnp.sum(ends_ref[...] * seq_w_ref[...], axis=0)
    lanes = enter.shape[1]
    groups = rows // group_rows
    enter = jnp.concatenate([enter] * groups, axis=0)
    state = (grow_ref[...] * enter[None]).reshape(blocks * rows, lanes)
    carried = lax.dot_general(
        state, table_ref[...], NT,
        precision=lax.Precision.HIGHEST, preferred_element_type=F32,
    ).reshape(blocks, rows, length)
    out_ref[...] = (local_ref[...] + carried).astype(BF16)


def gate_out_kernel(query_ref, mixed_ref, out_ref):
    chan, length = out_ref.shape[1], out_ref.shape[0]
    mixed = mixed_ref[...].reshape(chan, length).astype(F32).T
    out_ref[...] = (query_ref[...].astype(F32) * mixed).astype(BF16)


def on_device(query, keys, values, decay, residue, skip):
    seq_count = lax.axis_size("seq")
    blocks = lax.axis_size("chan")
    length, chan = query.shape
    rows = skip.shape[0]
    filters, modes = decay.shape
    group_rows = rows // filters
    lanes = filters * modes
    dims = (blocks, rows, length, modes, group_rows)
    shape = jax.ShapeDtypeStruct
    size = length * chan

    decay_row = decay.reshape(1, lanes)
    residue_row = residue.reshape(1, lanes)
    skip_col = skip.reshape(rows, 1)
    seq_index = lax.axis_index("seq").astype(jnp.int32).reshape(1)

    gated = call(
        gate_in_kernel, shape((blocks, rows, length), BF16), [VMEM] * 2, size, 6 * size
    )(keys, values)
    z = lax.all_to_all(gated, "chan", 0, 0, tiled=True)
    high, low, step, grow, seq_w = call(
        functools.partial(table_kernel, dims),
        (
            shape((length, lanes), BF16),
            shape((length, lanes), BF16),
            shape((1, lanes), F32),
            shape((blocks, rows, lanes), F32),
            shape((seq_count, group_rows, lanes), F32),
        ),
        [SMEM, VMEM], 100 * size, 8 * size,
    )(seq_index, decay_row)
    state, ends = call(
        functools.partial(state_kernel, dims),
        (shape((blocks, rows, lanes), F32), shape((seq_count, group_rows, lanes), F32)),
        [VMEM] * 4, 4 * lanes * size, 4 * size,
    )(z, high, low, step)
    ends = lax.all_to_all(ends, "seq", 0, 0, tiled=True)
    local, table = call(
        functools.partial(local_kernel, dims),
        (shape((blocks, rows, length), F32), shape((length, lanes), F32)),
        [VMEM] * 5, 8 * length * size, 8 * size,
    )(z, state, decay_row, residue_row, skip_col)
    mixed = call(
        functools.partial(carry_kernel, dims),
        shape((blocks, rows, length), BF16),
        [VMEM] * 5, 12 * lanes * size, 8 * size,
    )(ends, seq_w, grow, table, local)
    mixed = lax.all_to_all(mixed, "chan", 0, 0, tiled=True)
    return call(
        gate_out_kernel, shape((length, chan), BF16), [VMEM] * 2, size, 6 * size
    )(query, mixed)


def solution(mesh):
    tokens = P(("seq", "chan"), None)
    return jax.shard_map(
        on_device,
        mesh=mesh,
        in_specs=(tokens, tokens, tokens, P("chan", None), P("chan", None), P("chan")),
        out_specs=tokens,
        check_vma=False,
    )
```

profile of v0, /device:TPU:1, one launch (start us, length us, event | category | flops | bytes accessed | tf_op | source)
XLA Modules:
  0.0 68.0 jit_solution(3203661695219310658)
XLA Ops:
  0.0 1.7 %shard_map.64 = bf16[16,16,256]{2,1,0:T(8,128)(2,1)} custom-call(bf16[256,256]{1,0:T(8,128)(2,1)} %keys_ref.1, bf16[256,256]{1,0:T(8,128)(2,1)} %values_ref.1), custom_call_target="tpu_custom_call" | custom-call | flops 65536 | bytes 393216 | tf_op jit(solution)/shard_map/pallas_call | solution.py:153
  1.7 10.4 %all-to-all-start = ((bf16[16,16,256]{2,1,0:T(8,128)(2,1)}), bf16[16,16,256]{2,1,0:T(8,128)(2,1)S(1)}, u32[]{:S(2)}, u32[]{:S(2)}) async-start(bf16[16,16,256]{2,1,0:T(8,128)(2,1)} %shard_map.64), calls=%async_computation | async-start | bytes 262144 | tf_op jit(solution)/shard_map/all_to_all | solution.py:156
  12.1 0.0 copy-start.2
  12.1 0.7 copy-done.2
  12.8 0.7 reshape.13.decay_ref
  13.5 1.5 %shard_map.65 = (bf16[256,32]{1,0:T(8,128)(2,1)}, bf16[256,32]{1,0:T(8,128)(2,1)}, f32[1,32]{1,0:T(1,128)}, f32[16,16,32]{2,1,0:T(8,128)}, f32[32,8,32]{2,1,0:T(8,128)}) custom-call(s32[1]{0:T(128)} %bitcast.seq_ref, f32[1,32]{1,0:T(1,128)} %reshape.13.decay_ref), custom_call_target="tpu_custom_call" | custom-call | flops 6553600 | bytes 524288 | tf_op jit(solution)/shard_map/pallas_call | solution.py:157
  14.9 4.4 %all-to-all-done.z_ref = bf16[16,16,256]{2,1,0:T(8,128)(2,1)S(1)} async-done(((bf16[16,16,256]{2,1,0:T(8,128)(2,1)}), bf16[16,16,256]{2,1,0:T(8,128)(2,1)S(1)}, u32[]{:S(2)}, u32[]{:S(2)}) %all-to-all-start) | async-done | bytes 131104 | tf_op jit(solution)/shard_map/all_to_all | solution.py:156
  19.4 0.0 copy-start
  19.4 0.7 copy-done
  20.0 1.9 %shard_map.66 = (f32[16,16,32]{2,1,0:T(8,128)}, f32[32,8,32]{2,1,0:T(8,128)}) custom-call(bf16[16,16,256]{2,1,0:T(8,128)(2,1)} %copy-done, bf16[256,32]{1,0:T(8,128)(2,1)} %get-tuple-element.14.high_ref, bf16[256,32]{1,0:T(8,128)(2,1)} %get-tuple-element.15.low_ref, f32[1,32]{1,0:T(1,128)} %get-tuple-element.16.step_ref), custom_call_target="tpu_custom_call" | custom-call | flops 8388608 | bytes 262144 | tf_op jit(solution)/shard_map/pallas_call | solution.py:168
  21.9 1.6 %reshape.16 = f32[32,1,256]{2,1,0:T(1,128)} reshape(f32[32,8,32]{2,1,0:T(8,128)} %get-tuple-element.17) | data formatting | bytes 65536
  23.5 15.2 %all-to-all-start.1 = ((f32[32,1,256]{2,1,0:T(1,128)}), f32[32,1,256]{2,1,0:T(1,128)S(1)}, u32[]{:S(2)}, u32[]{:S(2)}) async-start(f32[32,1,256]{2,1,0:T(1,128)} %reshape.16), calls=%async_computation.1 | async-start | bytes 65536 | tf_op jit(solution)/shard_map/all_to_all | solution.py:173
  38.8 0.0 copy-done.3
  38.8 0.6 reshape.14.residue_ref
  39.4 0.7 copy-done.1
  40.0 0.7 copy.7.skip_ref
  40.7 3.4 %shard_map.67 = (f32[16,16,256]{2,1,0:T(8,128)}, f32[256,32]{1,0:T(8,128)}) custom-call(bf16[16,16,256]{2,1,0:T(8,128)(2,1)} %copy-done, f32[16,16,32]{2,1,0:T(8,128)} %get-tuple-element.20.state_ref, f32[1,32]{1,0:T(1,128)} %reshape.13.decay_ref, f32[1,32]{1,0:T(1,128)} %reshape.14.residue_ref, f32[16,1]{1,0:T(8,128)} %copy.7.skip_ref), custom_call_target="tpu_custom_call" | custom-call | flops 134217728 | bytes 524288 | tf_op jit(solution)/shard_map/pallas_call | solution.py:174
  44.1 6.5 %all-to-all-done.1 = f32[32,1,256]{2,1,0:T(1,128)S(1)} async-done(((f32[32,1,256]{2,1,0:T(1,128)}), f32[32,1,256]{2,1,0:T(1,128)S(1)}, u32[]{:S(2)}, u32[]{:S(2)}) %all-to-all-start.1) | async-done | bytes 32800 | tf_op jit(solution)/shard_map/all_to_all | solution.py:173
  50.6 0.5 broadcast
  51.1 0.7 %reduce = f32[32,256]{1,0:T(8,128)S(1)} reduce(f32[32,1,256]{2,1,0:T(1,128)S(1)} %all-to-all-done.1, f32[]{:T(128)} %broadcast), dimensions={1}, to_apply=%all_to_all.10.reduce_sub_computation | reduce | bytes 65540 | tf_op jit(solution)/shard_map/all_to_all | solution.py:173
  51.8 0.7 %reshape.17.ends_ref = f32[32,8,32]{2,1,0:T(8,128)} reshape(f32[32,256]{1,0:T(8,128)S(1)} %reduce) | data formatting | bytes 65536
  52.6 2.3 %shard_map.68 = bf16[16,16,256]{2,1,0:T(8,128)(2,1)} custom-call(f32[32,8,32]{2,1,0:T(8,128)} %reshape.17.ends_ref, f32[32,8,32]{2,1,0:T(8,128)} %get-tuple-element.18.seq_w_ref, f32[16,16,32]{2,1,0:T(8,128)} %get-tuple-element.19.grow_ref, f32[256,32]{1,0:T(8,128)} %get-tuple-element.21.table_ref, f32[16,16,256]{2,1,0:T(8,128)} %get-tuple-element.22.local_ref), custom_call_target="tpu_custom_call" | custom-call | flops 25165824 | bytes 524288 | tf_op jit(solution)/shard_map/pallas_call | solution.py:179
  54.9 11.4 %all_to_all.15.mixed_ref = bf16[16,16,256]{2,1,0:T(8,128)(2,1)} all-to-all(bf16[16,16,256]{2,1,0:T(8,128)(2,1)} %shard_map.68), channel_id=1, replica_groups=mesh['seq'=32,'chan'=16] {'chan'}, dimensions={0} | all-to-all | bytes 262144 | tf_op jit(solution)/shard_map/all_to_all | solution.py:184
  66.3 1.7 %shard_map.69 = bf16[256,256]{1,0:T(8,128)(2,1)} custom-call(bf16[256,256]{1,0:T(8,128)(2,1)} %query_ref.1, bf16[16,16,256]{2,1,0:T(8,128)(2,1)} %all_to_all.15.mixed_ref), custom_call_target="tpu_custom_call" | custom-call | flops 65536 | bytes 393216 | tf_op jit(solution)/shard_map/pallas_call | solution.py:185
  (2 shorter events, 0.0 us)
Async XLA Ops:
  1.7 17.6 %all-to-all-start = ((bf16[16,16,256]{2,1,0:T(8,128)(2,1)}), bf16[16,16,256]{2,1,0:T(8,128)(2,1)S(1)}, u32[]{:S(2)}, u32[]{:S(2)}) async-start(bf16[16,16,256]{2,1,0:T(8,128)(2,1)} %shard_map.64), calls=%async_computation | async-start | bytes 262144 | tf_op jit(solution)/shard_map/all_to_all | solution.py:156
  12.1 0.7 %copy-start.2 = (f32[2,16]{1,0:T(2,128)S(1)}, f32[2,16]{1,0:T(2,128)}, u32[]{:S(2)}) copy-start(f32[2,16]{1,0:T(2,128)} %param.9) | copy-start | bytes 388
  19.4 0.7 copy-start
  23.5 15.3 %copy-start.3 = (f32[2,16]{1,0:T(2,128)S(1)}, f32[2,16]{1,0:T(2,128)}, u32[]{:S(2)}) copy-start(f32[2,16]{1,0:T(2,128)} %param.10) | copy-start | bytes 388
  23.5 27.1 %all-to-all-start.1 = ((f32[32,1,256]{2,1,0:T(1,128)}), f32[32,1,256]{2,1,0:T(1,128)S(1)}, u32[]{:S(2)}, u32[]{:S(2)}) async-start(f32[32,1,256]{2,1,0:T(1,128)} %reshape.16), calls=%async_computation.1 | async-start | bytes 65536 | tf_op jit(solution)/shard_map/all_to_all | solution.py:173
  39.3 0.7 copy-start.1
where the time goes:
time: 68.5 us; the launch traced here: 68 us
  starting transfers between devices  25.6 us (37%)
  Pallas kernels  12.4 us (18%)
  blocking collectives  11.4 us (17%)
  waiting for transfers between devices  11 us (16%)
  local copies, waits for them, and re-layouts  6.77 us (10%)
  other arithmetic  0.72 us (1%)
    all_to_all x1, starting transfers between devices, on_device(): ends = lax.all_to_all(ends, 'seq', 0, 0, tiled=True)  15.2 us
    all_to_all x1, blocking collectives, on_device(): mixed = lax.all_to_all(mixed, 'chan', 0, 0, tiled=True)  11.4 us
    all_to_all x1, starting transfers between devices, on_device(): z = lax.all_to_all(gated, 'chan', 0, 0, tiled=True)  10.4 us
    all_to_all x1, waiting for transfers between devices, on_device(): ends = lax.all_to_all(ends, 'seq', 0, 0, tiled=True)  6.54 us
    all_to_all x1, waiting for transfers between devices, on_device(): z = lax.all_to_all(gated, 'chan', 0, 0, tiled=True)  4.45 us
    unnamed x10, local copies, waits for them, and re-layouts  4.37 us
    pallas_call x1, Pallas kernels, on_device(): call(functools.partial(local_kernel, dims), (shape((blocks, rows, length)...  3.39 us
    pallas_call x1, Pallas kernels, on_device(): call(functools.partial(carry_kernel, dims), shape((blocks, rows, length),...  2.27 us
  transfers between devices with their start and end apart: 2, of which 2 were waited for; matrix products, arithmetic and copies ran while one was open for 3% of the time, Pallas kernels for 7%

commit v1 on v0

--- a/solution.py
+++ b/solution.py
@@ -21,6 +21,7 @@
         in_specs=in_specs,
         out_specs=jax.tree.map(lambda _: VMEM, out_shape),
         cost_estimate=pl.CostEstimate(flops=flops, bytes_accessed=nbytes, transcendentals=0),
+        compiler_params=pltpu.CompilerParams(vmem_limit_bytes=16 << 20),
         **kw,
     )
 
@@ -78,7 +79,8 @@
     folded = state[:group_rows]
     for g in range(1, rows // group_rows):
         folded = folded + state[g * group_rows : (g + 1) * group_rows]
-    end_ref[...] = jnp.broadcast_to(folded[None], end_ref.shape)
+    spare = jnp.zeros((group_rows, end_ref.shape[2] - lanes), F32)
+    end_ref[...] = jnp.broadcast_to(jnp.concatenate([folded, spare], axis=1)[None], end_ref.shape)
 
 
 def local_kernel(dims, z_ref, state_ref, decay_ref, residue_ref, skip_ref, out_ref, table_ref):
@@ -115,8 +117,8 @@
 
 def carry_kernel(dims, ends_ref, seq_w_ref, grow_ref, table_ref, local_ref, out_ref):
     blocks, rows, length, modes, group_rows = dims
-    enter = jnp.sum(ends_ref[...] * seq_w_ref[...], axis=0)
-    lanes = enter.shape[1]
+    lanes = grow_ref.shape[2]
+    enter = jnp.sum(ends_ref[:, :, :lanes] * seq_w_ref[...], axis=0)
     groups = rows // group_rows
     enter = jnp.concatenate([enter] * groups, axis=0)
     state = (grow_ref[...] * enter[None]).reshape(blocks * rows, lanes)
@@ -167,7 +169,7 @@
     )(seq_index, decay_row)
     state, ends = call(
         functools.partial(state_kernel, dims),
-        (shape((blocks, rows, lanes), F32), shape((seq_count, group_rows, lanes), F32)),
+        (shape((blocks, rows, lanes), F32), shape((seq_count, group_rows, 128), F32)),
         [VMEM] * 4, 4 * lanes * size, 4 * size,
     )(z, high, low, step)
     ends = lax.all_to_all(ends, "seq", 0, 0, tiled=True)

time: 68.5 us -> 61.4 us (0.90)
  Pallas kernels: 12.4 us -> 4.63 us
  waiting for transfers between devices: 11 us -> 16.8 us
  local copies, waits for them, and re-layouts: 6.77 us -> 3.39 us
  blocking collectives: 11.4 us -> 9.95 us
  other arithmetic: 0.72 us -> 0 us
    all_to_all x1, waiting for transfers between devices: 6.54 us -> 10.4 us  [on_device(): ends = lax.all_to_all(ends, 'seq', 0, 0, tiled=True)]
    all_to_all x1, waiting for transfers between devices: 4.45 us -> 6.37 us  [on_device(): z = lax.all_to_all(gated, 'chan', 0, 0, tiled=True)]
    pallas_call x1, Pallas kernels: 2.27 us -> 0.4 us  [on_device(): call(functools.partial(carry_kernel, dims), shape((blocks, rows, length),...]
    pallas_call x1, Pallas kernels: 3.39 us -> 1.71 us  [on_device(): call(functools.partial(local_kernel, dims), (shape((blocks, rows, length)...]
    all_to_all x1, blocking collectives: 11.4 us -> 9.95 us  [on_device(): mixed = lax.all_to_all(mixed, 'chan', 0, 0, tiled=True)]
    pallas_call x1, Pallas kernels: 1.46 us -> 0.11 us  [on_device(): call(functools.partial(table_kernel, dims), (shape((length, lanes), BF16)...]
    unnamed x10 -> x12, local copies, waits for them, and re-layouts: 4.37 us -> 3.15 us
    pallas_call x1, Pallas kernels: 1.86 us -> 0.88 us  [on_device(): call(functools.partial(state_kernel, dims), (shape((blocks, rows, lanes),...]
  transfers between devices with their start and end apart: 2 -> 2, of which waited for: 2 -> 2; matrix products, arithmetic and copies ran while one was open for 3% -> 0% of each run, Pallas kernels for 7% -> 3%
where the time goes in v1:
time: 61.4 us; the launch traced here: 60.5 us
  starting transfers between devices  25.6 us (42%)
  waiting for transfers between devices  16.8 us (27%)
  blocking collectives  9.95 us (16%)
  Pallas kernels  4.63 us (8%)
  local copies, waits for them, and re-layouts  3.39 us (6%)
    all_to_all x1, starting transfers between devices, on_device(): ends = lax.all_to_all(ends, 'seq', 0, 0, tiled=True)  15.2 us
    all_to_all x1, waiting for transfers between devices, on_device(): ends = lax.all_to_all(ends, 'seq', 0, 0, tiled=True)  10.4 us
    all_to_all x1, starting transfers between devices, on_device(): z = lax.all_to_all(gated, 'chan', 0, 0, tiled=True)  10.4 us
    all_to_all x1, blocking collectives, on_device(): mixed = lax.all_to_all(mixed, 'chan', 0, 0, tiled=True)  9.95 us
    all_to_all x1, waiting for transfers between devices, on_device(): z = lax.all_to_all(gated, 'chan', 0, 0, tiled=True)  6.37 us
    unnamed x12, local copies, waits for them, and re-layouts  3.15 us
    pallas_call x1, Pallas kernels, on_device(): call(functools.partial(local_kernel, dims), (shape((blocks, rows, length)...  1.71 us
  transfers between devices with their start and end apart: 2, of which 2 were waited for; matrix products, arithmetic and copies ran while one was open for 0% of the time, Pallas kernels for 3%

profile of v1, /device:TPU:1, one launch (start us, length us, event | category | flops | bytes accessed | tf_op | source)
XLA Modules:
  0.0 60.5 jit_solution(4237989033598997354)
XLA Ops:
  0.0 0.0 copy-start
  0.0 0.9 %copy-done = bf16[256,256]{1,0:T(8,128)(2,1)S(1)} copy-done((bf16[256,256]{1,0:T(8,128)(2,1)S(1)}, bf16[256,256]{1,0:T(8,128)(2,1)}, u32[]{:S(2)}) %copy-start) | copy-done | bytes 131096
  0.9 0.0 copy-start.1
  0.9 0.9 %copy-done.1 = bf16[256,256]{1,0:T(8,128)(2,1)S(1)} copy-done((bf16[256,256]{1,0:T(8,128)(2,1)S(1)}, bf16[256,256]{1,0:T(8,128)(2,1)}, u32[]{:S(2)}) %copy-start.1) | copy-done | bytes 131096
  1.8 0.8 %shard_map.64 = bf16[16,16,256]{2,1,0:T(8,128)(2,1)} custom-call(bf16[256,256]{1,0:T(8,128)(2,1)S(1)} %copy-done, bf16[256,256]{1,0:T(8,128)(2,1)S(1)} %copy-done.1), custom_call_target="tpu_custom_call" | custom-call | flops 65536 | bytes 393216 | tf_op jit(solution)/shard_map/pallas_call | solution.py:155
  2.6 10.4 %all-to-all-start = ((bf16[16,16,256]{2,1,0:T(8,128)(2,1)}), bf16[16,16,256]{2,1,0:T(8,128)(2,1)S(1)}, u32[]{:S(2)}, u32[]{:S(2)}) async-start(bf16[16,16,256]{2,1,0:T(8,128)(2,1)} %shard_map.64), calls=%async_computation | async-start | bytes 262144 | tf_op jit(solution)/shard_map/all_to_all | solution.py:158
  13.0 0.0 copy-start.4
  13.0 0.7 %copy-done.4 = f32[2,16]{1,0:T(2,128)S(1)} copy-done((f32[2,16]{1,0:T(2,128)S(1)}, f32[2,16]{1,0:T(2,128)}, u32[]{:S(2)}) %copy-start.4) | copy-done | bytes 152
  13.6 0.1 reshape.13.decay_ref
  13.7 0.1 shard_map.65
  13.8 6.4 %all-to-all-done.z_ref = bf16[16,16,256]{2,1,0:T(8,128)(2,1)S(1)} async-done(((bf16[16,16,256]{2,1,0:T(8,128)(2,1)}), bf16[16,16,256]{2,1,0:T(8,128)(2,1)S(1)}, u32[]{:S(2)}, u32[]{:S(2)}) %all-to-all-start) | async-done | bytes 131104 | tf_op jit(solution)/shard_map/all_to_all | solution.py:158
  20.2 0.9 %shard_map.66 = (f32[16,16,32]{2,1,0:T(8,128)S(1)}, f32[32,8,128]{2,1,0:T(8,128)}) custom-call(bf16[16,16,256]{2,1,0:T(8,128)(2,1)S(1)} %all-to-all-done.z_ref, bf16[256,32]{1,0:T(8,128)(2,1)S(1)} %get-tuple-element.14.high_ref, bf16[256,32]{1,0:T(8,128)(2,1)S(1)} %get-tuple-element.15.low_ref, f32[1,32]{1,0:T(1,128)S(1)} %get-tuple-element.16.step_ref), custom_call_target="tpu_custom_call" | custom-call | flops 8388608 | bytes 262144 | tf_op jit(solution)/shard_map/pallas_call | solution.py:170
  21.1 15.2 %all-to-all-start.1 = ((f32[32,8,128]{2,1,0:T(8,128)}), f32[32,8,128]{2,1,0:T(8,128)S(1)}, u32[]{:S(2)}, u32[]{:S(2)}) async-start(f32[32,8,128]{2,1,0:T(8,128)} %get-tuple-element.17), calls=%async_computation.1 | async-start | bytes 262144 | tf_op jit(solution)/shard_map/all_to_all | solution.py:175
  36.3 0.0 copy-done.5
  36.4 0.1 reshape.14.residue_ref
  36.4 0.7 %copy-done.3 = f32[16]{0:T(128)S(1)} copy-done((f32[16]{0:T(128)S(1)}, f32[16]{0:T(128)}, u32[]{:S(2)}) %copy-start.3) | copy-done | bytes 88
  37.1 0.1 copy.7.skip_ref
  37.2 1.7 %shard_map.67 = (f32[16,16,256]{2,1,0:T(8,128)S(1)}, f32[256,32]{1,0:T(8,128)S(1)}) custom-call(bf16[16,16,256]{2,1,0:T(8,128)(2,1)S(1)} %all-to-all-done.z_ref, f32[16,16,32]{2,1,0:T(8,128)S(1)} %get-tuple-element.20.state_ref, f32[1,32]{1,0:T(1,128)S(1)} %reshape.13.decay_ref, f32[1,32]{1,0:T(1,128)S(1)} %reshape.14.residue_ref, f32[16,1]{1,0:T(8,128)S(1)} %copy.7.skip_ref), custom_call_target="tpu_custom_call" | custom-call | flops 134217728 | bytes 524288 | tf_op jit(solution)/shard_map/pallas_call | solution.py:176
  38.9 10.4 %all-to-all-done.1.ends_ref = f32[32,8,128]{2,1,0:T(8,128)S(1)} async-done(((f32[32,8,128]{2,1,0:T(8,128)}), f32[32,8,128]{2,1,0:T(8,128)S(1)}, u32[]{:S(2)}, u32[]{:S(2)}) %all-to-all-start.1) | async-done | bytes 131104 | tf_op jit(solution)/shard_map/all_to_all | solution.py:175
  49.3 0.4 shard_map.68
  49.7 0.0 copy-start.2
  49.7 9.9 %all_to_all.15.mixed_ref = bf16[16,16,256]{2,1,0:T(8,128)(2,1)S(1)} all-to-all(bf16[16,16,256]{2,1,0:T(8,128)(2,1)S(1)} %shard_map.68), channel_id=1, replica_groups=mesh['seq'=32,'chan'=16] {'chan'}, dimensions={0} | all-to-all | bytes 262144 | tf_op jit(solution)/shard_map/all_to_all | solution.py:186
  59.7 0.0 copy-done.2
  59.7 0.8 %shard_map.69 = bf16[256,256]{1,0:T(8,128)(2,1)} custom-call(bf16[256,256]{1,0:T(8,128)(2,1)S(1)} %copy-done.2, bf16[16,16,256]{2,1,0:T(8,128)(2,1)S(1)} %all_to_all.15.mixed_ref), custom_call_target="tpu_custom_call" | custom-call | flops 65536 | bytes 393216 | tf_op jit(solution)/shard_map/pallas_call | solution.py:187
  (2 shorter events, 0.0 us)
Async XLA Ops:
  0.0 0.9 %copy-start = (bf16[256,256]{1,0:T(8,128)(2,1)S(1)}, bf16[256,256]{1,0:T(8,128)(2,1)}, u32[]{:S(2)}) copy-start(bf16[256,256]{1,0:T(8,128)(2,1)} %keys_ref.1) | copy-start | bytes 393220
  0.9 0.9 %copy-start.1 = (bf16[256,256]{1,0:T(8,128)(2,1)S(1)}, bf16[256,256]{1,0:T(8,128)(2,1)}, u32[]{:S(2)}) copy-start(bf16[256,256]{1,0:T(8,128)(2,1)} %values_ref.1) | copy-start | bytes 393220
  2.6 17.6 %all-to-all-start = ((bf16[16,16,256]{2,1,0:T(8,128)(2,1)}), bf16[16,16,256]{2,1,0:T(8,128)(2,1)S(1)}, u32[]{:S(2)}, u32[]{:S(2)}) async-start(bf16[16,16,256]{2,1,0:T(8,128)(2,1)} %shard_map.64), calls=%async_computation | async-start | bytes 262144 | tf_op jit(solution)/shard_map/all_to_all | solution.py:158
  13.0 0.7 %copy-start.4 = (f32[2,16]{1,0:T(2,128)S(1)}, f32[2,16]{1,0:T(2,128)}, u32[]{:S(2)}) copy-start(f32[2,16]{1,0:T(2,128)} %param.9) | copy-start | bytes 388
  21.1 15.3 %copy-start.5 = (f32[2,16]{1,0:T(2,128)S(1)}, f32[2,16]{1,0:T(2,128)}, u32[]{:S(2)}) copy-start(f32[2,16]{1,0:T(2,128)} %param.10) | copy-start | bytes 388
  21.1 28.2 %all-to-all-start.1 = ((f32[32,8,128]{2,1,0:T(8,128)}), f32[32,8,128]{2,1,0:T(8,128)S(1)}, u32[]{:S(2)}, u32[]{:S(2)}) async-start(f32[32,8,128]{2,1,0:T(8,128)} %get-tuple-element.17), calls=%async_computation.1 | async-start | bytes 262144 | tf_op jit(solution)/shard_map/all_to_all | solution.py:175
  36.4 0.7 %copy-start.3 = (f32[16]{0:T(128)S(1)}, f32[16]{0:T(128)}, u32[]{:S(2)}) copy-start(f32[16]{0:T(128)} %param.11) | copy-start | bytes 196
  49.7 10.0 %copy-start.2 = (bf16[256,256]{1,0:T(8,128)(2,1)S(1)}, bf16[256,256]{1,0:T(8,128)(2,1)}, u32[]{:S(2)}) copy-start(bf16[256,256]{1,0:T(8,128)(2,1)} %query_ref.1) | copy-start | bytes 393220

commit v2 on v0

v2 whole, which is shorter than its diff:
```python
import functools

import jax
import jax.numpy as jnp
from jax import lax
from jax.experimental import pallas as pl
from jax.experimental.pallas import tpu as pltpu
from jax.sharding import PartitionSpec as P

F32 = jnp.float32
BF16 = jnp.bfloat16
VMEM = pl.BlockSpec(memory_space=pltpu.VMEM)
SMEM = pl.BlockSpec(memory_space=pltpu.SMEM)
HBM = pl.BlockSpec(memory_space=pltpu.HBM)
NT = (((1,), (1,)), ((), ()))


def call(body, out_shape, in_specs, flops, nbytes, vmem=16, **kw):
    return pl.pallas_call(
        body,
        out_shape=out_shape,
        in_specs=in_specs,
        out_specs=jax.tree.map(lambda _: VMEM, out_shape),
        cost_estimate=pl.CostEstimate(flops=flops, bytes_accessed=nbytes, transcendentals=0),
        compiler_params=pltpu.CompilerParams(vmem_limit_bytes=vmem << 20),
        **kw,
    )


def split(table):
    high = table.astype(BF16)
    return high, (table - high.astype(F32)).astype(BF16)


def dot(a, b):
    return jnp.dot(a, b, preferred_element_type=F32)


def dot_nt(a, b):
    return lax.dot_general(
        a, b, NT, precision=lax.Precision.HIGHEST, preferred_element_type=F32
    )


def own_lanes(shape, modes):
    row = lax.broadcasted_iota(jnp.int32, shape, len(shape) - 2)
    lane = lax.broadcasted_iota(jnp.int32, shape, len(shape) - 1)
    return row == lane // modes


def gate_in_kernel(keys_ref, values_ref, out_ref, keys_buf, values_buf, sems):
    half = keys_buf.shape[1]
    copies = []
    for h in range(2):
        part = pl.ds(h * half, half)
        copies.append(
            [
                pltpu.make_async_copy(keys_ref.at[part], keys_buf.at[h], sems.at[h, 0]),
                pltpu.make_async_copy(values_ref.at[part], values_buf.at[h], sems.at[h, 1]),
            ]
        )
        for copy in copies[h]:
            copy.start()
    blocks, rows, _ = out_ref.shape
    for h in range(2):
        for copy in copies[h]:
            copy.wait()
        z = keys_buf[h].astype(F32) * values_buf[h].astype(F32)
        out_ref[:, :, h * half : (h + 1) * half] = z.T.astype(BF16).reshape(blocks, rows, half)


def table_kernel(dims, seq_ref, decay_ref, high_ref, low_ref, step_ref, grow_ref, seq_w_ref):
    blocks, groups, size, length, modes = dims
    decay = decay_ref[...]
    lanes = decay.shape[1]
    back = (length - 1) - lax.broadcasted_iota(jnp.int32, (length, lanes), 0)
    for g in range(groups):
        high, low = split(jnp.exp(-decay[g : g + 1] * back.astype(F32)))
        high_ref[:, g * lanes : (g + 1) * lanes] = high
        low_ref[:, g * lanes : (g + 1) * lanes] = low
    step_ref[...] = jnp.exp(-decay * float(length))
    shape = (blocks, size, lanes)
    block = lax.broadcasted_iota(jnp.int32, shape, 0)
    for g in range(groups):
        grow = jnp.exp(-decay[g : g + 1][None] * (block * length).astype(F32))
        grow_ref[:, g] = jnp.where(own_lanes(shape, modes), grow, 0.0)
    shape = seq_w_ref.shape
    gap = seq_ref[0] - 1 - lax.broadcasted_iota(jnp.int32, shape, 0)
    away = jnp.maximum(gap, 0) * (blocks * length)
    seq_w_ref[...] = jnp.where(gap >= 0, jnp.exp(-decay[None] * away.astype(F32)), 0.0)


def state_kernel(dims, z_ref, high_ref, low_ref, step_ref, state_ref, end_ref):
    blocks, groups, size, length, modes = dims
    z = z_ref[...].reshape(blocks * groups * size, length)
    ends = dot(z, high_ref[...]) + dot(z, low_ref[...])
    lanes = step_ref.shape[1]
    ends = ends.reshape(blocks, groups, size, groups * lanes)
    mine = own_lanes((size, lanes), modes)
    packed = []
    for g in range(groups):
        step = step_ref[g : g + 1]
        state = jnp.zeros((size, lanes), F32)
        for b in range(blocks):
            state_ref[b, g] = state
            state = state * step + jnp.where(mine, ends[b, g, :, g * lanes : (g + 1) * lanes], 0.0)
        packed.append(jnp.sum(state, axis=0, keepdims=True))
    packed = jnp.concatenate(packed, axis=0)
    end_ref[...] = jnp.broadcast_to(packed[None], end_ref.shape)


def local_kernel(dims, z_ref, state_ref, decay_ref, residue_ref, skip_ref, out_ref, table_ref):
    blocks, groups, size, length, modes = dims
    lanes = decay_ref.shape[1]
    z = z_ref[...].reshape(blocks * groups * size, length)
    skipped = skip_ref[...][None] * z_ref[...].astype(F32)
    skipped = skipped.reshape(blocks, groups, size, length)
    row = lax.broadcasted_iota(jnp.int32, (length, length), 0)
    col = lax.broadcasted_iota(jnp.int32, (length, length), 1)
    position = lax.broadcasted_iota(jnp.int32, (length, lanes), 0).astype(F32)
    first = lax.broadcasted_iota(jnp.int32, (length, lanes), 1) < modes
    for g in range(groups):
        decay = decay_ref[g : g + 1]
        amplitude = residue_ref[g : g + 1] * jnp.sqrt(2.0 * decay)
        rise = jnp.where(first, jnp.exp(decay * position), 0.0)
        fall = amplitude * jnp.exp(-decay * position)
        after = amplitude * jnp.exp(-decay * (position + 1.0))
        table_ref[g] = after
        high, low = split(jnp.where(row <= col, dot_nt(rise, fall), 0.0))
        conv = (dot(z, high) + dot(z, low)).reshape(blocks, groups, size, length)[:, g]
        carried = dot_nt(state_ref[:, g].reshape(blocks * size, lanes), after)
        out_ref[:, g] = conv + carried.reshape(blocks, size, length) + skipped[:, g]


def carry_kernel(dims, ends_ref, seq_w_ref, grow_ref, table_ref, local_ref, out_ref):
    blocks, groups, size, length, modes = dims
    enter = jnp.sum(ends_ref[...] * seq_w_ref[...], axis=0)
    lanes = enter.shape[1]
    mixed = []
    for g in range(groups):
        state = (grow_ref[:, g] * enter[g : g + 1][None]).reshape(blocks * size, lanes)
        carried = dot_nt(state, table_ref[g]).reshape(blocks, size, length)
        mixed.append(local_ref[:, g] + carried)
    mixed = jnp.stack(mixed, axis=1).reshape(blocks, groups * size, length)
    out_ref[...] = mixed.astype(BF16)


def gate_out_kernel(query_ref, mixed_ref, out_ref):
    chan, length = out_ref.shape[1], out_ref.shape[0]
    mixed = mixed_ref[...].reshape(chan, length).astype(F32).T
    out_ref[...] = (query_ref[...].astype(F32) * mixed).astype(BF16)


def on_device(query, keys, values, decay, residue, skip):
    seq_count = lax.axis_size("seq")
    blocks = lax.axis_size("chan")
    length, chan = query.shape
    rows = skip.shape[0]
    groups, modes = decay.shape
    size = rows // groups
    lanes = size * modes
    dims = (blocks, groups, size, length, modes)
    shape = jax.ShapeDtypeStruct
    whole = length * chan

    decay_row = jnp.tile(decay, (1, size))
    residue_row = jnp.tile(residue, (1, size))
    skip_col = skip.reshape(rows, 1)
    seq_index = lax.axis_index("seq").astype(jnp.int32).reshape(1)

    gated = call(
        gate_in_kernel, shape((blocks, rows, length), BF16), [HBM] * 2, whole, 6 * whole, 60,
        scratch_shapes=[
            pltpu.VMEM((2, length // 2, chan), BF16),
            pltpu.VMEM((2, length // 2, chan), BF16),
            pltpu.SemaphoreType.DMA((2, 2)),
        ],
    )(keys, values)
    z = lax.all_to_all(gated, "chan", 0, 0, tiled=True)
    high, low, step, grow, seq_w = call(
        functools.partial(table_kernel, dims),
        (
            shape((length, groups * lanes), BF16),
            shape((length, groups * lanes), BF16),
            shape((groups, lanes), F32),
            shape((blocks, groups, size, lanes), F32),
            shape((seq_count, groups, lanes), F32),
        ),
        [SMEM, VMEM], 100 * whole, 8 * whole,
    )(seq_index, decay_row)
    state, ends = call(
        functools.partial(state_kernel, dims),
        (shape((blocks, groups, size, lanes), F32), shape((seq_count, groups, lanes), F32)),
        [VMEM] * 4, 4 * lanes * whole, 4 * whole,
    )(z, high, low, step)
    ends = lax.all_to_all(ends, "seq", 0, 0, tiled=True)
    local, table = call(
        functools.partial(local_kernel, dims),
        (shape((blocks, groups, size, length), F32), shape((groups, length, lanes), F32)),
        [VMEM] * 5, 8 * length * whole, 8 * whole,
    )(z, state, decay_row, residue_row, skip_col)
    mixed = call(
        functools.partial(carry_kernel, dims),
        shape((blocks, rows, length), BF16),
        [VMEM] * 5, 12 * lanes * whole, 8 * whole,
    )(ends, seq_w, grow, table, local)
    mixed = lax.all_to_all(mixed, "chan", 0, 0, tiled=True)
    return call(
        gate_out_kernel, shape((length, chan), BF16), [VMEM] * 2, whole, 6 * whole
    )(query, mixed)


def solution(mesh):
    tokens = P(("seq", "chan"), None)
    return jax.shard_map(
        on_device,
        mesh=mesh,
        in_specs=(tokens, tokens, tokens, P("chan", None), P("chan", None), P("chan")),
        out_specs=tokens,
        check_vma=False,
    )
```

time: 68.5 us -> 58.9 us (0.86)
  Pallas kernels: 12.4 us -> 5.87 us
  local copies, waits for them, and re-layouts: 6.77 us -> 1.59 us
  waiting for transfers between devices: 11 us -> 15.4 us
  blocking collectives: 11.4 us -> 9.95 us
  other arithmetic: 0.72 us -> 0 us
    pallas_call x5, Pallas kernels: 10.2 us -> 5.45 us  [the longest x1 1.89 us: on_device(): call(functools.partial(local_kernel, dims), (shape((blocks, groups, size,...]
    unnamed x10 -> x8, local copies, waits for them, and re-layouts: 4.37 us -> 1.34 us
    all_to_all x1, waiting for transfers between devices: 6.54 us -> 9.09 us  [on_device(): ends = lax.all_to_all(ends, 'seq', 0, 0, tiled=True)]
    all_to_all x1, waiting for transfers between devices: 4.45 us -> 6.32 us  [on_device(): z = lax.all_to_all(gated, 'chan', 0, 0, tiled=True)]
    pallas_call x1, Pallas kernels: 2.27 us -> 0.42 us  [on_device(): call(functools.partial(carry_kernel, dims), shape((blocks, rows, length),...]
    all_to_all x1, blocking collectives: 11.4 us -> 9.95 us  [on_device(): mixed = lax.all_to_all(mixed, 'chan', 0, 0, tiled=True)]
    reshape x2 -> x0, local copies, waits for them, and re-layouts: 1.22 us -> none  [the longest x1 0.65 us: on_device(): decay_row = decay.reshape(1, lanes)]
    all_to_all x1 -> x0, other arithmetic: 0.72 us -> none  [on_device(): ends = lax.all_to_all(ends, 'seq', 0, 0, tiled=True)]
  transfers between devices with their start and end apart: 2 -> 2, of which waited for: 2 -> 2; matrix products, arithmetic and copies ran while one was open for 3% -> 0% of each run, Pallas kernels for 7% -> 4%
where the time goes in v2:
time: 58.9 us; the launch traced here: 58.5 us
  starting transfers between devices  25.6 us (43%)
  waiting for transfers between devices  15.4 us (26%)
  blocking collectives  9.95 us (17%)
  Pallas kernels  5.87 us (10%)
  local copies, waits for them, and re-layouts  1.59 us (3%)
    all_to_all x1, starting transfers between devices, on_device(): ends = lax.all_to_all(ends, 'seq', 0, 0, tiled=True)  15.2 us
    all_to_all x1, starting transfers between devices, on_device(): z = lax.all_to_all(gated, 'chan', 0, 0, tiled=True)  10.4 us
    all_to_all x1, blocking collectives, on_device(): mixed = lax.all_to_all(mixed, 'chan', 0, 0, tiled=True)  9.95 us
    all_to_all x1, waiting for transfers between devices, on_device(): ends = lax.all_to_all(ends, 'seq', 0, 0, tiled=True)  9.09 us
    all_to_all x1, waiting for transfers between devices, on_device(): z = lax.all_to_all(gated, 'chan', 0, 0, tiled=True)  6.32 us
    pallas_call x1, Pallas kernels, on_device(): call(functools.partial(local_kernel, dims), (shape((blocks, groups, size,...  1.89 us
    pallas_call x1, Pallas kernels, on_device(): call(gate_in_kernel, shape((blocks, rows, length), BF16), [HBM] * 2, whol...  1.77 us
    unnamed x8, local copies, waits for them, and re-layouts  1.34 us
  transfers between devices with their start and end apart: 2, of which 2 were waited for; matrix products, arithmetic and copies ran while one was open for 0% of the time, Pallas kernels for 4%

profile of v2, /device:TPU:1, one launch (start us, length us, event | category | flops | bytes accessed | tf_op | source)
XLA Modules:
  0.0 58.5 jit_solution(13217518642947638583)
XLA Ops:
  0.0 1.8 %shard_map.64 = bf16[16,16,256]{2,1,0:T(8,128)(2,1)} custom-call(bf16[256,256]{1,0:T(8,128)(2,1)} %keys_ref.1, bf16[256,256]{1,0:T(8,128)(2,1)} %values_ref.1), custom_call_target="tpu_custom_call" | custom-call | flops 65536 | bytes 393216 | tf_op jit(solution)/shard_map/pallas_call | solution.py:171
  1.8 10.4 %all-to-all-start = ((bf16[16,16,256]{2,1,0:T(8,128)(2,1)}), bf16[16,16,256]{2,1,0:T(8,128)(2,1)S(1)}, u32[]{:S(2)}, u32[]{:S(2)}) async-start(bf16[16,16,256]{2,1,0:T(8,128)(2,1)} %shard_map.64), calls=%async_computation | async-start | bytes 262144 | tf_op jit(solution)/shard_map/all_to_all | solution.py:179
  12.2 0.0 copy-start.1
  12.2 0.7 %copy-done.1 = f32[2,16]{1,0:T(2,128)S(1)} copy-done((f32[2,16]{1,0:T(2,128)S(1)}, f32[2,16]{1,0:T(2,128)}, u32[]{:S(2)}) %copy-start.1) | copy-done | bytes 152
  12.9 0.1 tile.9.decay_ref
  13.0 0.2 shard_map.65
  13.1 6.3 %all-to-all-done.z_ref = bf16[16,16,256]{2,1,0:T(8,128)(2,1)S(1)} async-done(((bf16[16,16,256]{2,1,0:T(8,128)(2,1)}), bf16[16,16,256]{2,1,0:T(8,128)(2,1)S(1)}, u32[]{:S(2)}, u32[]{:S(2)}) %all-to-all-start) | async-done | bytes 131104 | tf_op jit(solution)/shard_map/all_to_all | solution.py:179
  19.4 0.9 %shard_map.66 = (f32[16,2,8,128]{3,2,1,0:T(8,128)S(1)}, f32[32,2,128]{2,1,0:T(2,128)}) custom-call(bf16[16,16,256]{2,1,0:T(8,128)(2,1)S(1)} %all-to-all-done.z_ref, bf16[256,256]{1,0:T(8,128)(2,1)S(1)} %get-tuple-element.14.high_ref, bf16[256,256]{1,0:T(8,128)(2,1)S(1)} %get-tuple-element.15.low_ref, f32[2,128]{1,0:T(2,128)S(1)} %get-tuple-element.16.step_ref), custom_call_target="tpu_custom_call" | custom-call | flops 33554432 | bytes 262144 | tf_op jit(solution)/shard_map/pallas_call | solution.py:191
  20.3 0.0 copy-start.2
  20.3 15.2 %all-to-all-start.1 = ((f32[32,2,128]{2,1,0:T(2,128)}), f32[32,2,128]{2,1,0:T(2,128)S(1)}, u32[]{:S(2)}, u32[]{:S(2)}) async-start(f32[32,2,128]{2,1,0:T(2,128)} %get-tuple-element.17), calls=%async_computation.1 | async-start | bytes 65536 | tf_op jit(solution)/shard_map/all_to_all | solution.py:196
  35.5 0.0 copy-done.2
  35.6 0.1 tile.21.residue_ref
  35.6 0.0 copy-start.3
  35.6 0.7 %copy-done.3 = f32[16]{0:T(128)S(1)} copy-done((f32[16]{0:T(128)S(1)}, f32[16]{0:T(128)}, u32[]{:S(2)}) %copy-start.3) | copy-done | bytes 88
  36.3 0.1 copy.7.skip_ref
  36.4 1.9 %shard_map.67 = (f32[16,2,8,256]{3,2,1,0:T(8,128)S(1)}, f32[2,256,128]{2,1,0:T(8,128)S(1)}) custom-call(bf16[16,16,256]{2,1,0:T(8,128)(2,1)S(1)} %all-to-all-done.z_ref, f32[16,2,8,128]{3,2,1,0:T(8,128)S(1)} %get-tuple-element.20.state_ref, f32[2,128]{1,0:T(2,128)S(1)} %tile.9.decay_ref, f32[2,128]{1,0:T(2,128)S(1)} %tile.21.residue_ref, ...), custom_call_target="tpu_custom_call" | custom-call | flops 134217728 | bytes 524288 | tf_op jit(solution)/shard_map/pallas_call | solution.py:197
  38.3 9.1 %all-to-all-done.1.ends_ref = f32[32,2,128]{2,1,0:T(2,128)S(1)} async-done(((f32[32,2,128]{2,1,0:T(2,128)}), f32[32,2,128]{2,1,0:T(2,128)S(1)}, u32[]{:S(2)}, u32[]{:S(2)}) %all-to-all-start.1) | async-done | bytes 32800 | tf_op jit(solution)/shard_map/all_to_all | solution.py:196
  47.4 0.4 shard_map.68
  47.8 0.0 copy-start
  47.8 9.9 %all_to_all.15.mixed_ref = bf16[16,16,256]{2,1,0:T(8,128)(2,1)S(1)} all-to-all(bf16[16,16,256]{2,1,0:T(8,128)(2,1)S(1)} %shard_map.68), channel_id=1, replica_groups=mesh['seq'=32,'chan'=16] {'chan'}, dimensions={0} | all-to-all | bytes 262144 | tf_op jit(solution)/shard_map/all_to_all | solution.py:207
  57.8 0.0 copy-done
  57.8 0.8 %shard_map.69 = bf16[256,256]{1,0:T(8,128)(2,1)} custom-call(bf16[256,256]{1,0:T(8,128)(2,1)S(1)} %copy-done, bf16[16,16,256]{2,1,0:T(8,128)(2,1)S(1)} %all_to_all.15.mixed_ref), custom_call_target="tpu_custom_call" | custom-call | flops 65536 | bytes 393216 | tf_op jit(solution)/shard_map/pallas_call | solution.py:208
  (2 shorter events, 0.0 us)
Async XLA Ops:
  1.8 17.6 %all-to-all-start = ((bf16[16,16,256]{2,1,0:T(8,128)(2,1)}), bf16[16,16,256]{2,1,0:T(8,128)(2,1)S(1)}, u32[]{:S(2)}, u32[]{:S(2)}) async-start(bf16[16,16,256]{2,1,0:T(8,128)(2,1)} %shard_map.64), calls=%async_computation | async-start | bytes 262144 | tf_op jit(solution)/shard_map/all_to_all | solution.py:179
  12.2 0.7 %copy-start.1 = (f32[2,16]{1,0:T(2,128)S(1)}, f32[2,16]{1,0:T(2,128)}, u32[]{:S(2)}) copy-start(f32[2,16]{1,0:T(2,128)} %param.9) | copy-start | bytes 388
  20.3 15.2 %copy-start.2 = (f32[2,16]{1,0:T(2,128)S(1)}, f32[2,16]{1,0:T(2,128)}, u32[]{:S(2)}) copy-start(f32[2,16]{1,0:T(2,128)} %param.10) | copy-start | bytes 388
  20.3 27.1 %all-to-all-start.1 = ((f32[32,2,128]{2,1,0:T(2,128)}), f32[32,2,128]{2,1,0:T(2,128)S(1)}, u32[]{:S(2)}, u32[]{:S(2)}) async-start(f32[32,2,128]{2,1,0:T(2,128)} %get-tuple-element.17), calls=%async_computation.1 | async-start | bytes 65536 | tf_op jit(solution)/shard_map/all_to_all | solution.py:196
  35.6 0.7 %copy-start.3 = (f32[16]{0:T(128)S(1)}, f32[16]{0:T(128)}, u32[]{:S(2)}) copy-start(f32[16]{0:T(128)} %param.11) | copy-start | bytes 196
  47.8 10.0 %copy-start = (bf16[256,256]{1,0:T(8,128)(2,1)S(1)}, bf16[256,256]{1,0:T(8,128)(2,1)}, u32[]{:S(2)}) copy-start(bf16[256,256]{1,0:T(8,128)(2,1)} %query_ref.1) | copy-start | bytes 393220

commit v3 on v2

v3 whole, which is shorter than its diff:
```python
import functools

import jax
import jax.numpy as jnp
from jax import lax
from jax.experimental import pallas as pl
from jax.experimental.pallas import tpu as pltpu
from jax.sharding import Mesh
from jax.sharding import PartitionSpec as P

F32 = jnp.float32
BF16 = jnp.bfloat16
VMEM = pl.BlockSpec(memory_space=pltpu.VMEM)
SMEM = pl.BlockSpec(memory_space=pltpu.SMEM)
HBM = pl.BlockSpec(memory_space=pltpu.HBM)
NT = (((1,), (1,)), ((), ()))
HALVES = 2


def call(body, out_shape, in_specs, flops, nbytes, vmem=16, **kw):
    return pl.pallas_call(
        body,
        out_shape=out_shape,
        in_specs=in_specs,
        out_specs=jax.tree.map(lambda _: VMEM, out_shape),
        cost_estimate=pl.CostEstimate(flops=flops, bytes_accessed=nbytes, transcendentals=0),
        compiler_params=pltpu.CompilerParams(vmem_limit_bytes=vmem << 20),
        **kw,
    )


def split(table):
    high = table.astype(BF16)
    return high, (table - high.astype(F32)).astype(BF16)


def dot(a, b):
    return jnp.dot(a, b, preferred_element_type=F32)


def dot_nt(a, b):
    return lax.dot_general(
        a, b, NT, precision=lax.Precision.HIGHEST, preferred_element_type=F32
    )


def own_lanes(shape, modes):
    row = lax.broadcasted_iota(jnp.int32, shape, len(shape) - 2)
    lane = lax.broadcasted_iota(jnp.int32, shape, len(shape) - 1)
    return row == lane // modes


def unpack(message_ref, size):
    message = message_ref[...].astype(F32)
    return jnp.concatenate([message[:, :size], message[:, size:]], axis=2)


def pack(data):
    half = data.shape[2] // 2
    return jnp.concatenate([data[:, :, :half], data[:, :, half:]], axis=1).astype(BF16)


def swap(data, outer):
    return data.reshape(outer, -1, *data.shape[1:]).swapaxes(0, 1).reshape(data.shape)


def gate_in_kernel(size, keys_ref, values_ref, out_ref, keys_buf, values_buf, sems):
    half = keys_buf.shape[1]
    copies = []
    for h in range(2):
        part = pl.ds(h * half, half)
        copies.append(
            [
                pltpu.make_async_copy(keys_ref.at[part], keys_buf.at[h], sems.at[h, 0]),
                pltpu.make_async_copy(values_ref.at[part], values_buf.at[h], sems.at[h, 1]),
            ]
        )
        for copy in copies[h]:
            copy.start()
    filters = out_ref.shape[0]
    parts = []
    for h in range(2):
        for copy in copies[h]:
            copy.wait()
        z = keys_buf[h].astype(F32) * values_buf[h].astype(F32)
        parts.append(z.T.reshape(filters, size, half))
    z = swap(jnp.concatenate(parts, axis=1), filters // HALVES)
    out_ref[...] = z.astype(BF16)


def own_filter(place_ref, table):
    rows = table.shape[0] // HALVES
    return jnp.where(place_ref[0] == 0, table[:rows], table[rows:])


def table_kernel(dims, place_ref, decay_ref, high_ref, low_ref, step_ref, grow_ref, away_ref):
    blocks, size, length, modes = dims
    decay = own_filter(place_ref, decay_ref[...])
    lanes = decay.shape[1]
    back = (length - 1) - lax.broadcasted_iota(jnp.int32, (length, lanes), 0)
    high, low = split(jnp.exp(-decay * back.astype(F32)))
    high_ref[...] = high
    low_ref[...] = low
    step_ref[...] = jnp.exp(-decay * float(length))
    shape = (blocks, size, lanes)
    block = lax.broadcasted_iota(jnp.int32, shape, 0)
    grow = jnp.exp(-decay[None] * (block * length).astype(F32))
    grow_ref[...] = jnp.where(own_lanes(shape, modes), grow, 0.0)
    shape = away_ref.shape
    gap = place_ref[1] - 1 - lax.broadcasted_iota(jnp.int32, shape, 0)
    gap = gap + shape[0] * lax.broadcasted_iota(jnp.int32, shape, 1)
    away = jnp.maximum(gap, 0) * (blocks * length)
    away_ref[...] = jnp.where(gap >= 0, jnp.exp(-decay[None] * away.astype(F32)), 0.0)


def state_kernel(dims, z_ref, high_ref, low_ref, step_ref, state_ref, end_ref):
    blocks, size, length, modes = dims
    z = unpack(z_ref, size).reshape(HALVES * blocks * size, length).astype(BF16)
    ends = dot(z, high_ref[...]) + dot(z, low_ref[...])
    lanes = step_ref.shape[1]
    ends = ends.reshape(HALVES, blocks, size, lanes)
    mine = own_lanes((size, lanes), modes)
    step = step_ref[...]
    packed = []
    for h in range(HALVES):
        state = jnp.zeros((size, lanes), F32)
        for b in range(blocks):
            state_ref[h, b] = state
            state = state * step + jnp.where(mine, ends[h, b], 0.0)
        packed.append(jnp.sum(state, axis=0, keepdims=True))
    packed = jnp.concatenate(packed, axis=0)
    end_ref[...] = jnp.broadcast_to(packed[None], end_ref.shape)


def local_kernel(
    dims, place_ref, z_ref, state_ref, decay_ref, residue_ref, skip_ref, out_ref, table_ref
):
    blocks, size, length, modes = dims
    decay = own_filter(place_ref, decay_ref[...])
    lanes = decay.shape[1]
    z = unpack(z_ref, size)
    skipped = own_filter(place_ref, skip_ref[...])[None] * z
    z = z.reshape(HALVES * blocks * size, length).astype(BF16)
    row = lax.broadcasted_iota(jnp.int32, (length, length), 0)
    col = lax.broadcasted_iota(jnp.int32, (length, length), 1)
    position = lax.broadcasted_iota(jnp.int32, (length, lanes), 0).astype(F32)
    first = lax.broadcasted_iota(jnp.int32, (length, lanes), 1) < modes
    amplitude = own_filter(place_ref, residue_ref[...]) * jnp.sqrt(2.0 * decay)
    rise = jnp.where(first, jnp.exp(decay * position), 0.0)
    fall = amplitude * jnp.exp(-decay * position)
    after = amplitude * jnp.exp(-decay * (position + 1.0))
    table_ref[...] = after
    high, low = split(jnp.where(row <= col, dot_nt(rise, fall), 0.0))
    states = state_ref[...].reshape(HALVES * blocks * size, lanes)
    local = dot(z, high) + dot(z, low) + dot_nt(states, after)
    out_ref[...] = local.reshape(HALVES * blocks, size, length) + skipped


def carry_kernel(dims, ends_ref, away_ref, grow_ref, table_ref, local_ref, out_ref):
    blocks, size, length, modes = dims
    first, second = ends_ref[:, 0], ends_ref[:, 1]
    same, across = away_ref[:, 0], away_ref[:, 1]
    enter = [
        jnp.sum(first * same, axis=0, keepdims=True),
        jnp.sum(first * across + second * same, axis=0, keepdims=True),
    ]
    lanes = same.shape[1]
    state = jnp.concatenate([grow_ref[...] * e[None] for e in enter], axis=0)
    carried = dot_nt(state.reshape(HALVES * blocks * size, lanes), table_ref[...])
    out_ref[...] = pack(local_ref[...] + carried.reshape(HALVES * blocks, size, length))


def gate_out_kernel(size, query_ref, mixed_ref, out_ref):
    length, chan = out_ref.shape
    half = length // 2
    mixed = swap(mixed_ref[...].astype(F32), HALVES)
    for h in range(2):
        part = mixed[:, h * size : (h + 1) * size].reshape(chan, half).T
        rows = slice(h * half, (h + 1) * half)
        out_ref[rows] = (query_ref[rows].astype(F32) * part).astype(BF16)


def on_device(query, keys, values, decay, residue, skip):
    seq_count = lax.axis_size("yc")
    blocks = lax.axis_size("chan")
    length, chan = query.shape
    modes = decay.shape[1]
    size = skip.shape[0] // HALVES
    lanes = size * modes
    count = HALVES * blocks
    dims = (blocks, size, length, modes)
    shape = jax.ShapeDtypeStruct
    whole = length * chan

    decay_row = jnp.tile(decay, (1, size))
    residue_row = jnp.tile(residue, (1, size))
    skip_col = skip.reshape(HALVES * size, 1)
    place = jnp.stack([lax.axis_index("zh"), lax.axis_index("yc")]).astype(jnp.int32)
    message = shape((count, 2 * size, length // 2), BF16)

    gated = call(
        functools.partial(gate_in_kernel, size), message, [HBM] * 2, whole, 6 * whole, 60,
        scratch_shapes=[
            pltpu.VMEM((2, length // 2, chan), BF16),
            pltpu.VMEM((2, length // 2, chan), BF16),
            pltpu.SemaphoreType.DMA((2, 2)),
        ],
    )(keys, values)
    z = lax.all_to_all(gated, ("zh", "chan"), 0, 0, tiled=True)
    high, low, step, grow, away = call(
        functools.partial(table_kernel, dims),
        (
            shape((length, lanes), BF16),
            shape((length, lanes), BF16),
            shape((1, lanes), F32),
            shape((blocks, size, lanes), F32),
            shape((seq_count, HALVES, lanes), F32),
        ),
        [SMEM, VMEM], 100 * whole, 8 * whole,
    )(place, decay_row)
    state, ends = call(
        functools.partial(state_kernel, dims),
        (shape((HALVES, blocks, size, lanes), F32), shape((seq_count, HALVES, lanes), F32)),
        [VMEM] * 4, 4 * lanes * whole, 4 * whole,
    )(z, high, low, step)
    ends = lax.all_to_all(ends, "yc", 0, 0, tiled=True)
    local, table = call(
        functools.partial(local_kernel, dims),
        (shape((count, size, length), F32), shape((length, lanes), F32)),
        [SMEM] + [VMEM] * 5, 8 * length * whole, 8 * whole,
    )(place, z, state, decay_row, residue_row, skip_col)
    mixed = call(
        functools.partial(carry_kernel, dims), message,
        [VMEM] * 5, 12 * lanes * whole, 8 * whole,
    )(ends, away, grow, table, local)
    mixed = lax.all_to_all(mixed, ("zh", "chan"), 0, 0, tiled=True)
    return call(
        functools.partial(gate_out_kernel, size), shape((length, chan), BF16),
        [VMEM] * 2, whole, 6 * whole,
    )(query, mixed)


def solution(mesh):
    chan = mesh.shape["chan"]
    cut = Mesh(mesh.devices.reshape(HALVES, -1, chan), ("zh", "yc", "chan"))
    tokens = P(("zh", "yc", "chan"), None)
    return jax.shard_map(
        on_device,
        mesh=cut,
        in_specs=(tokens, tokens, tokens, P("chan", None), P("chan", None), P("chan")),
        out_specs=tokens,
        check_vma=False,
    )
```

time: 58.9 us -> 57.5 us (0.976)
  blocking collectives: 9.95 us -> 13.2 us
  starting transfers between devices: 25.6 us -> 23 us
  waiting for transfers between devices: 15.4 us -> 13.1 us
    all_to_all x1, blocking collectives: 9.95 us -> 13.2 us  [on_device(): mixed = lax.all_to_all(mixed, ('zh', 'chan'), 0, 0, tiled=True)]
    all_to_all x2, starting transfers between devices: 25.6 us -> 23 us  [the longest x1 13.7 us: on_device(): z = lax.all_to_all(gated, ('zh', 'chan'), 0, 0, tiled=True)]
    all_to_all x2, waiting for transfers between devices: 15.4 us -> 13.1 us  [the longest x1 8.34 us: on_device(): z = lax.all_to_all(gated, ('zh', 'chan'), 0, 0, tiled=True)]
  transfers between devices with their start and end apart: 2 -> 2, of which waited for: 2 -> 2; matrix products, arithmetic and copies ran while one was open for 0% -> 1% of each run, Pallas kernels for 4% -> 4%
where the time goes in v3:
time: 57.5 us; the launch traced here: 57.2 us
  starting transfers between devices  23 us (40%)
  blocking collectives  13.2 us (23%)
  waiting for transfers between devices  13.1 us (23%)
  Pallas kernels  6.09 us (11%)
  local copies, waits for them, and re-layouts  1.59 us (3%)
    all_to_all x1, starting transfers between devices, on_device(): z = lax.all_to_all(gated, ('zh', 'chan'), 0, 0, tiled=True)  13.7 us
    all_to_all x1, blocking collectives, on_device(): mixed = lax.all_to_all(mixed, ('zh', 'chan'), 0, 0, tiled=True)  13.2 us
    all_to_all x1, starting transfers between devices, on_device(): ends = lax.all_to_all(ends, 'yc', 0, 0, tiled=True)  9.3 us
    all_to_all x1, waiting for transfers between devices, on_device(): z = lax.all_to_all(gated, ('zh', 'chan'), 0, 0, tiled=True)  8.34 us
    all_to_all x1, waiting for transfers between devices, on_device(): ends = lax.all_to_all(ends, 'yc', 0, 0, tiled=True)  4.77 us
    pallas_call x1, Pallas kernels, on_device(): call(functools.partial(gate_in_kernel, size), message, [HBM] * 2, whole,...  1.77 us
    pallas_call x1, Pallas kernels, on_device(): call(functools.partial(local_kernel, dims), (shape((count, size, length),...  1.72 us
    unnamed x8, local copies, waits for them, and re-layouts  1.34 us
  transfers between devices with their start and end apart: 2, of which 2 were waited for; matrix products, arithmetic and copies ran while one was open for 1% of the time, Pallas kernels for 4%

profile of v3, /device:TPU:1, one launch (start us, length us, event | category | flops | bytes accessed | tf_op | source)
XLA Modules:
  0.0 57.2 jit_solution(8347804896763113353)
XLA Ops:
  0.0 1.8 %shard_map.64 = bf16[32,16,128]{2,1,0:T(8,128)(2,1)} custom-call(bf16[256,256]{1,0:T(8,128)(2,1)} %keys_ref.1, bf16[256,256]{1,0:T(8,128)(2,1)} %values_ref.1), custom_call_target="tpu_custom_call" | custom-call | flops 65536 | bytes 393216 | tf_op jit(solution)/shard_map/pallas_call | solution.py:201
  1.8 13.7 %all-to-all-start = ((bf16[32,16,128]{2,1,0:T(8,128)(2,1)}), bf16[32,16,128]{2,1,0:T(8,128)(2,1)S(1)}, u32[]{:S(2)}, u32[]{:S(2)}) async-start(bf16[32,16,128]{2,1,0:T(8,128)(2,1)} %shard_map.64), calls=%async_computation | async-start | bytes 262144 | tf_op jit(solution)/shard_map/all_to_all | solution.py:209
  15.5 0.0 copy-start.1
  15.5 0.7 %copy-done.1 = f32[2,16]{1,0:T(2,128)S(1)} copy-done((f32[2,16]{1,0:T(2,128)S(1)}, f32[2,16]{1,0:T(2,128)}, u32[]{:S(2)}) %copy-start.1) | copy-done | bytes 152
  16.2 0.1 tile.9.decay_ref
  16.3 0.1 pad_add_fusion.place_ref
  16.4 0.6 %shard_map.65 = (bf16[256,128]{1,0:T(8,128)(2,1)S(1)}, bf16[256,128]{1,0:T(8,128)(2,1)S(1)}, f32[1,128]{1,0:T(1,128)S(1)}, f32[16,8,128]{2,1,0:T(8,128)S(1)}, f32[16,2,128]{2,1,0:T(2,128)S(1)}) custom-call(s32[2]{0:T(128)S(1)} %pad_add_fusion.place_ref, f32[2,128]{1,0:T(2,128)S(1)} %tile.9.decay_ref), custom_call_target="tpu_custom_call" | custom-call | flops 6553600 | bytes 524288 | tf_op jit(solution)/shard_map/pallas_call | solution.py:210
  17.0 8.3 %all-to-all-done.z_ref = bf16[32,16,128]{2,1,0:T(8,128)(2,1)S(1)} async-done(((bf16[32,16,128]{2,1,0:T(8,128)(2,1)}), bf16[32,16,128]{2,1,0:T(8,128)(2,1)S(1)}, u32[]{:S(2)}, u32[]{:S(2)}) %all-to-all-start) | async-done | bytes 131104 | tf_op jit(solution)/shard_map/all_to_all | solution.py:209
  25.3 0.8 %shard_map.66 = (f32[2,16,8,128]{3,2,1,0:T(8,128)S(1)}, f32[16,2,128]{2,1,0:T(2,128)}) custom-call(bf16[32,16,128]{2,1,0:T(8,128)(2,1)S(1)} %all-to-all-done.z_ref, bf16[256,128]{1,0:T(8,128)(2,1)S(1)} %get-tuple-element.14.high_ref, bf16[256,128]{1,0:T(8,128)(2,1)S(1)} %get-tuple-element.15.low_ref, f32[1,128]{1,0:T(1,128)S(1)} %get-tuple-element.16.step_ref), custom_call_target="tpu_custom_call" | custom-call | flops 33554432 | bytes 262144 | tf_op jit(solution)/shard_map/pallas_call | solution.py:221
  26.2 0.0 copy-start.2
  26.2 9.3 %all-to-all-start.1 = ((f32[16,2,128]{2,1,0:T(2,128)}), f32[16,2,128]{2,1,0:T(2,128)S(1)}, u32[]{:S(2)}, u32[]{:S(2)}) async-start(f32[16,2,128]{2,1,0:T(2,128)} %get-tuple-element.17), calls=%async_computation.1 | async-start | bytes 32768 | tf_op jit(solution)/shard_map/all_to_all | solution.py:226
  35.5 0.0 copy-done.2
  35.5 0.1 tile.21.residue_ref
  35.6 0.0 copy-start.3
  35.6 0.7 %copy-done.3 = f32[16]{0:T(128)S(1)} copy-done((f32[16]{0:T(128)S(1)}, f32[16]{0:T(128)}, u32[]{:S(2)}) %copy-start.3) | copy-done | bytes 88
  36.2 0.1 copy.7.skip_ref
  36.3 1.7 %shard_map.67 = (f32[32,8,256]{2,1,0:T(8,128)S(1)}, f32[256,128]{1,0:T(8,128)S(1)}) custom-call(s32[2]{0:T(128)S(1)} %pad_add_fusion.place_ref, bf16[32,16,128]{2,1,0:T(8,128)(2,1)S(1)} %all-to-all-done.z_ref, f32[2,16,8,128]{3,2,1,0:T(8,128)S(1)} %get-tuple-element.20.state_ref, f32[2,128]{1,0:T(2,128)S(1)} %tile.9.decay_ref, ...), custom_call_target="tpu_custom_call" | custom-call | flops 134217728 | bytes 524288 | tf_op jit(solution)/shard_map/pallas_call | solution.py:227
  38.0 4.8 %all-to-all-done.1.ends_ref = f32[16,2,128]{2,1,0:T(2,128)S(1)} async-done(((f32[16,2,128]{2,1,0:T(2,128)}), f32[16,2,128]{2,1,0:T(2,128)S(1)}, u32[]{:S(2)}, u32[]{:S(2)}) %all-to-all-start.1) | async-done | bytes 16416 | tf_op jit(solution)/shard_map/all_to_all | solution.py:226
  42.8 0.4 shard_map.68
  43.2 0.0 copy-start
  43.2 13.2 %all_to_all.15.mixed_ref = bf16[32,16,128]{2,1,0:T(8,128)(2,1)S(1)} all-to-all(bf16[32,16,128]{2,1,0:T(8,128)(2,1)S(1)} %shard_map.68), channel_id=1, replica_groups=mesh['zh'=2,'yc'=16,'chan'=16] {'zh','chan'}, dimensions={0} | all-to-all | bytes 262144 | tf_op jit(solution)/shard_map/all_to_all | solution.py:236
  56.4 0.0 copy-done
  56.4 0.8 %shard_map.69 = bf16[256,256]{1,0:T(8,128)(2,1)} custom-call(bf16[256,256]{1,0:T(8,128)(2,1)S(1)} %copy-done, bf16[32,16,128]{2,1,0:T(8,128)(2,1)S(1)} %all_to_all.15.mixed_ref), custom_call_target="tpu_custom_call" | custom-call | flops 65536 | bytes 393216 | tf_op jit(solution)/shard_map/pallas_call | solution.py:237
  (2 shorter events, 0.0 us)
Async XLA Ops:
  1.8 23.6 %all-to-all-start = ((bf16[32,16,128]{2,1,0:T(8,128)(2,1)}), bf16[32,16,128]{2,1,0:T(8,128)(2,1)S(1)}, u32[]{:S(2)}, u32[]{:S(2)}) async-start(bf16[32,16,128]{2,1,0:T(8,128)(2,1)} %shard_map.64), calls=%async_computation | async-start | bytes 262144 | tf_op jit(solution)/shard_map/all_to_all | solution.py:209
  15.5 0.7 %copy-start.1 = (f32[2,16]{1,0:T(2,128)S(1)}, f32[2,16]{1,0:T(2,128)}, u32[]{:S(2)}) copy-start(f32[2,16]{1,0:T(2,128)} %param.9) | copy-start | bytes 388
  26.2 9.3 %copy-start.2 = (f32[2,16]{1,0:T(2,128)S(1)}, f32[2,16]{1,0:T(2,128)}, u32[]{:S(2)}) copy-start(f32[2,16]{1,0:T(2,128)} %param.10) | copy-start | bytes 388
  26.2 16.6 %all-to-all-start.1 = ((f32[16,2,128]{2,1,0:T(2,128)}), f32[16,2,128]{2,1,0:T(2,128)S(1)}, u32[]{:S(2)}, u32[]{:S(2)}) async-start(f32[16,2,128]{2,1,0:T(2,128)} %get-tuple-element.17), calls=%async_computation.1 | async-start | bytes 32768 | tf_op jit(solution)/shard_map/all_to_all | solution.py:226
  35.6 0.7 %copy-start.3 = (f32[16]{0:T(128)S(1)}, f32[16]{0:T(128)}, u32[]{:S(2)}) copy-start(f32[16]{0:T(128)} %param.11) | copy-start | bytes 196
  43.2 13.2 %copy-start = (bf16[256,256]{1,0:T(8,128)(2,1)S(1)}, bf16[256,256]{1,0:T(8,128)(2,1)}, u32[]{:S(2)}) copy-start(bf16[256,256]{1,0:T(8,128)(2,1)} %query_ref.1) | copy-start | bytes 393220

commit v4 on v2

--- a/solution.py
+++ b/solution.py
@@ -5,6 +5,7 @@
 from jax import lax
 from jax.experimental import pallas as pl
 from jax.experimental.pallas import tpu as pltpu
+from jax.sharding import Mesh
 from jax.sharding import PartitionSpec as P
 
 F32 = jnp.float32
@@ -13,6 +14,7 @@
 SMEM = pl.BlockSpec(memory_space=pltpu.SMEM)
 HBM = pl.BlockSpec(memory_space=pltpu.HBM)
 NT = (((1,), (1,)), ((), ()))
+HALVES = 2
 
 
 def call(body, out_shape, in_specs, flops, nbytes, vmem=16, **kw):
@@ -69,7 +71,9 @@
         out_ref[:, :, h * half : (h + 1) * half] = z.T.astype(BF16).reshape(blocks, rows, half)
 
 
-def table_kernel(dims, seq_ref, decay_ref, high_ref, low_ref, step_ref, grow_ref, seq_w_ref):
+def table_kernel(
+    dims, place_ref, decay_ref, high_ref, low_ref, step_ref, grow_ref, inside_ref, whole_ref, cross_ref
+):
     blocks, groups, size, length, modes = dims
     decay = decay_ref[...]
     lanes = decay.shape[1]
@@ -84,10 +88,16 @@
     for g in range(groups):
         grow = jnp.exp(-decay[g : g + 1][None] * (block * length).astype(F32))
         grow_ref[:, g] = jnp.where(own_lanes(shape, modes), grow, 0.0)
-    shape = seq_w_ref.shape
-    gap = seq_ref[0] - 1 - lax.broadcasted_iota(jnp.int32, shape, 0)
-    away = jnp.maximum(gap, 0) * (blocks * length)
-    seq_w_ref[...] = jnp.where(gap >= 0, jnp.exp(-decay[None] * away.astype(F32)), 0.0)
+    shape = inside_ref.shape
+    span = blocks * length
+    place = place_ref[0]
+    index = lax.broadcasted_iota(jnp.int32, shape, 0)
+    gap = place - 1 - index
+    away = jnp.maximum(gap, 0) * span
+    inside_ref[...] = jnp.where(gap >= 0, jnp.exp(-decay[None] * away.astype(F32)), 0.0)
+    left = (shape[0] - 1 - index) * span
+    whole_ref[...] = jnp.exp(-decay[None] * left.astype(F32))
+    cross_ref[...] = jnp.exp(-decay * (place * span).astype(F32))
 
 
 def state_kernel(dims, z_ref, high_ref, low_ref, step_ref, state_ref, end_ref):
@@ -132,9 +142,17 @@
         out_ref[:, g] = conv + carried.reshape(blocks, size, length) + skipped[:, g]
 
 
-def carry_kernel(dims, ends_ref, seq_w_ref, grow_ref, table_ref, local_ref, out_ref):
-    blocks, groups, size, length, modes = dims
-    enter = jnp.sum(ends_ref[...] * seq_w_ref[...], axis=0)
+def join_kernel(ends_ref, inside_ref, whole_ref, enter_ref, total_ref):
+    ends = ends_ref[...]
+    enter_ref[...] = jnp.sum(ends * inside_ref[...], axis=0)
+    total_ref[...] = jnp.sum(ends * whole_ref[...], axis=0)
+
+
+def carry_kernel(
+    dims, enter_ref, before_ref, cross_ref, grow_ref, table_ref, local_ref, out_ref
+):
+    blocks, groups, size, length, modes = dims
+    enter = enter_ref[...] + before_ref[...] * cross_ref[...]
     lanes = enter.shape[1]
     mixed = []
     for g in range(groups):
@@ -152,7 +170,7 @@
 
 
 def on_device(query, keys, values, decay, residue, skip):
-    seq_count = lax.axis_size("seq")
+    seq_count = lax.axis_size("yc")
     blocks = lax.axis_size("chan")
     length, chan = query.shape
     rows = skip.shape[0]
@@ -166,7 +184,7 @@
     decay_row = jnp.tile(decay, (1, size))
     residue_row = jnp.tile(residue, (1, size))
     skip_col = skip.reshape(rows, 1)
-    seq_index = lax.axis_index("seq").astype(jnp.int32).reshape(1)
+    place = lax.axis_index("yc").astype(jnp.int32).reshape(1)
 
     gated = call(
         gate_in_kernel, shape((blocks, rows, length), BF16), [HBM] * 2, whole, 6 * whole, 60,
@@ -177,7 +195,7 @@
         ],
     )(keys, values)
     z = lax.all_to_all(gated, "chan", 0, 0, tiled=True)
-    high, low, step, grow, seq_w = call(
+    high, low, step, grow, inside, whole_w, cross = call(
         functools.partial(table_kernel, dims),
         (
             shape((length, groups * lanes), BF16),
@@ -185,25 +203,32 @@
             shape((groups, lanes), F32),
             shape((blocks, groups, size, lanes), F32),
             shape((seq_count, groups, lanes), F32),
+            shape((seq_count, groups, lanes), F32),
+            shape((groups, lanes), F32),
         ),
         [SMEM, VMEM], 100 * whole, 8 * whole,
-    )(seq_index, decay_row)
+    )(place, decay_row)
     state, ends = call(
         functools.partial(state_kernel, dims),
         (shape((blocks, groups, size, lanes), F32), shape((seq_count, groups, lanes), F32)),
         [VMEM] * 4, 4 * lanes * whole, 4 * whole,
     )(z, high, low, step)
-    ends = lax.all_to_all(ends, "seq", 0, 0, tiled=True)
+    ends = lax.all_to_all(ends, "yc", 0, 0, tiled=True)
     local, table = call(
         functools.partial(local_kernel, dims),
         (shape((blocks, groups, size, length), F32), shape((groups, length, lanes), F32)),
         [VMEM] * 5, 8 * length * whole, 8 * whole,
     )(z, state, decay_row, residue_row, skip_col)
+    enter, total = call(
+        join_kernel, (shape((groups, lanes), F32), shape((groups, lanes), F32)),
+        [VMEM] * 3, 4 * seq_count * groups * lanes, 12 * seq_count * groups * lanes,
+    )(ends, inside, whole_w)
+    before = lax.ppermute(total, "zh", [(0, 1)])
     mixed = call(
         functools.partial(carry_kernel, dims),
         shape((blocks, rows, length), BF16),
-        [VMEM] * 5, 12 * lanes * whole, 8 * whole,
-    )(ends, seq_w, grow, table, local)
+        [VMEM] * 6, 12 * lanes * whole, 8 * whole,
+    )(enter, before, cross, grow, table, local)
     mixed = lax.all_to_all(mixed, "chan", 0, 0, tiled=True)
     return call(
         gate_out_kernel, shape((length, chan), BF16), [VMEM] * 2, whole, 6 * whole
@@ -211,10 +236,12 @@
 
 
 def solution(mesh):
-    tokens = P(("seq", "chan"), None)
+    chan = mesh.shape["chan"]
+    cut = Mesh(mesh.devices.reshape(HALVES, -1, chan), ("zh", "yc", "chan"))
+    tokens = P(("zh", "yc", "chan"), None)
     return jax.shard_map(
         on_device,
-        mesh=mesh,
+        mesh=cut,
         in_specs=(tokens, tokens, tokens, P("chan", None), P("chan", None), P("chan")),
         out_specs=tokens,
         check_vma=False,

time: 58.9 us -> 58.3 us (0.990)
  waiting for transfers between devices: 15.4 us -> 12.8 us
  starting transfers between devices: 25.6 us -> 27.7 us
    ppermute x0 -> x1, starting transfers between devices: none -> 7.93 us  [on_device(): before = lax.ppermute(total, 'zh', [(0, 1)])]
    all_to_all x1, starting transfers between devices: 15.2 us -> 9.35 us  [on_device(): ends = lax.all_to_all(ends, 'yc', 0, 0, tiled=True)]
    all_to_all x1, waiting for transfers between devices: 9.09 us -> 6.49 us  [on_device(): ends = lax.all_to_all(ends, 'yc', 0, 0, tiled=True)]
  transfers between devices with their start and end apart: 2 -> 3, of which waited for: 2 -> 2; matrix products, arithmetic and copies ran while one was open for 0% -> 0% of each run, Pallas kernels for 4% -> 4%
where the time goes in v4:
time: 58.3 us; the launch traced here: 57.9 us
  starting transfers between devices  27.7 us (48%)
  waiting for transfers between devices  12.8 us (22%)
  blocking collectives  9.95 us (17%)
  Pallas kernels  5.82 us (10%)
  local copies, waits for them, and re-layouts  1.59 us (3%)
    all_to_all x1, starting transfers between devices, on_device(): z = lax.all_to_all(gated, 'chan', 0, 0, tiled=True)  10.4 us
    all_to_all x1, blocking collectives, on_device(): mixed = lax.all_to_all(mixed, 'chan', 0, 0, tiled=True)  9.95 us
    all_to_all x1, starting transfers between devices, on_device(): ends = lax.all_to_all(ends, 'yc', 0, 0, tiled=True)  9.35 us
    ppermute x1, starting transfers between devices, on_device(): before = lax.ppermute(total, 'zh', [(0, 1)])  7.93 us
    all_to_all x1, waiting for transfers between devices, on_device(): ends = lax.all_to_all(ends, 'yc', 0, 0, tiled=True)  6.49 us
    all_to_all x1, waiting for transfers between devices, on_device(): z = lax.all_to_all(gated, 'chan', 0, 0, tiled=True)  6.33 us
    pallas_call x1, Pallas kernels, on_device(): call(functools.partial(local_kernel, dims), (shape((blocks, groups, size,...  1.9 us
    pallas_call x1, Pallas kernels, on_device(): call(gate_in_kernel, shape((blocks, rows, length), BF16), [HBM] * 2, whol...  1.77 us
  transfers between devices with their start and end apart: 3, of which 2 were waited for; matrix products, arithmetic and copies ran while one was open for 0% of the time, Pallas kernels for 4%

profile of v4, /device:TPU:1, one launch (start us, length us, event | category | flops | bytes accessed | tf_op | source)
XLA Modules:
  0.0 57.9 jit_solution(14274719986338064850)
XLA Ops:
  0.0 1.8 %shard_map.64 = bf16[16,16,256]{2,1,0:T(8,128)(2,1)} custom-call(bf16[256,256]{1,0:T(8,128)(2,1)} %keys_ref.1, bf16[256,256]{1,0:T(8,128)(2,1)} %values_ref.1), custom_call_target="tpu_custom_call" | custom-call | flops 65536 | bytes 393216 | tf_op jit(solution)/shard_map/pallas_call | solution.py:189
  1.8 10.4 %all-to-all-start = ((bf16[16,16,256]{2,1,0:T(8,128)(2,1)}), bf16[16,16,256]{2,1,0:T(8,128)(2,1)S(1)}, u32[]{:S(2)}, u32[]{:S(2)}) async-start(bf16[16,16,256]{2,1,0:T(8,128)(2,1)} %shard_map.64), calls=%async_computation | async-start | bytes 262144 | tf_op jit(solution)/shard_map/all_to_all | solution.py:197
  12.2 0.0 copy-start.1
  12.2 0.7 %copy-done.1 = f32[2,16]{1,0:T(2,128)S(1)} copy-done((f32[2,16]{1,0:T(2,128)S(1)}, f32[2,16]{1,0:T(2,128)}, u32[]{:S(2)}) %copy-start.1) | copy-done | bytes 152
  12.9 0.1 tile.9.decay_ref
  13.0 0.1 shard_map.65
  13.1 6.3 %all-to-all-done.z_ref = bf16[16,16,256]{2,1,0:T(8,128)(2,1)S(1)} async-done(((bf16[16,16,256]{2,1,0:T(8,128)(2,1)}), bf16[16,16,256]{2,1,0:T(8,128)(2,1)S(1)}, u32[]{:S(2)}, u32[]{:S(2)}) %all-to-all-start) | async-done | bytes 131104 | tf_op jit(solution)/shard_map/all_to_all | solution.py:197
  19.4 0.8 %shard_map.66 = (f32[16,2,8,128]{3,2,1,0:T(8,128)S(1)}, f32[16,2,128]{2,1,0:T(2,128)}) custom-call(bf16[16,16,256]{2,1,0:T(8,128)(2,1)S(1)} %all-to-all-done.z_ref, bf16[256,256]{1,0:T(8,128)(2,1)S(1)} %get-tuple-element.18.high_ref, bf16[256,256]{1,0:T(8,128)(2,1)S(1)} %get-tuple-element.19.low_ref, f32[2,128]{1,0:T(2,128)S(1)} %get-tuple-element.20.step_ref), custom_call_target="tpu_custom_call" | custom-call | flops 33554432 | bytes 262144 | tf_op jit(solution)/shard_map/pallas_call | solution.py:211
  20.3 0.0 copy-start.2
  20.3 9.3 %all-to-all-start.1 = ((f32[16,2,128]{2,1,0:T(2,128)}), f32[16,2,128]{2,1,0:T(2,128)S(1)}, u32[]{:S(2)}, u32[]{:S(2)}) async-start(f32[16,2,128]{2,1,0:T(2,128)} %get-tuple-element.21), calls=%async_computation.1 | async-start | bytes 32768 | tf_op jit(solution)/shard_map/all_to_all | solution.py:216
  29.6 0.0 copy-done.2
  29.6 0.1 tile.21.residue_ref
  29.7 0.0 copy-start.3
  29.7 0.7 %copy-done.3 = f32[16]{0:T(128)S(1)} copy-done((f32[16]{0:T(128)S(1)}, f32[16]{0:T(128)}, u32[]{:S(2)}) %copy-start.3) | copy-done | bytes 88
  30.4 0.1 copy.7.skip_ref
  30.5 6.5 %all-to-all-done.1.ends_ref = f32[16,2,128]{2,1,0:T(2,128)S(1)} async-done(((f32[16,2,128]{2,1,0:T(2,128)}), f32[16,2,128]{2,1,0:T(2,128)S(1)}, u32[]{:S(2)}, u32[]{:S(2)}) %all-to-all-start.1) | async-done | bytes 16416 | tf_op jit(solution)/shard_map/all_to_all | solution.py:216
  37.0 7.9 %collective-permute-start = (f32[2,128]{1,0:T(2,128)S(1)}, f32[2,128]{1,0:T(2,128)S(1)}, u32[]{:S(2)}, u32[]{:S(2)}) collective-permute-start(f32[2,128]{1,0:T(2,128)S(1)} %get-tuple-element.25), channel_id=1, source_target_pairs={{0,256},{1,257},{2,258},{3,259},{4,260},{5,261},{6,262},{7,263},{8... | collective-permute-start | bytes 3080 | tf_op jit(solution)/shard_map/ppermute | solution.py:226
  44.9 1.9 %shard_map.68 = (f32[16,2,8,256]{3,2,1,0:T(8,128)S(1)}, f32[2,256,128]{2,1,0:T(8,128)S(1)}) custom-call(bf16[16,16,256]{2,1,0:T(8,128)(2,1)S(1)} %all-to-all-done.z_ref, f32[16,2,8,128]{3,2,1,0:T(8,128)S(1)} %get-tuple-element.28.state_ref, f32[2,128]{1,0:T(2,128)S(1)} %tile.9.decay_ref, f32[2,128]{1,0:T(2,128)S(1)} %tile.21.residue_ref, ...), custom_call_target="tpu_custom_call" | custom-call | flops 134217728 | bytes 524288 | tf_op jit(solution)/shard_map/pallas_call | solution.py:217
  46.8 0.0 collective-permute-done.before_ref
  46.8 0.4 shard_map.69
  47.2 0.0 copy-start
  47.2 9.9 %all_to_all.15.mixed_ref = bf16[16,16,256]{2,1,0:T(8,128)(2,1)S(1)} all-to-all(bf16[16,16,256]{2,1,0:T(8,128)(2,1)S(1)} %shard_map.69), channel_id=1, replica_groups=mesh['zh'=2,'yc'=16,'chan'=16] {'chan'}, dimensions={0} | all-to-all | bytes 262144 | tf_op jit(solution)/shard_map/all_to_all | solution.py:232
  57.2 0.0 copy-done
  57.2 0.8 %shard_map.70 = bf16[256,256]{1,0:T(8,128)(2,1)} custom-call(bf16[256,256]{1,0:T(8,128)(2,1)S(1)} %copy-done, bf16[16,16,256]{2,1,0:T(8,128)(2,1)S(1)} %all_to_all.15.mixed_ref), custom_call_target="tpu_custom_call" | custom-call | flops 65536 | bytes 393216 | tf_op jit(solution)/shard_map/pallas_call | solution.py:233
  (3 shorter events, 0.0 us)
Async XLA Ops:
  1.8 17.6 %all-to-all-start = ((bf16[16,16,256]{2,1,0:T(8,128)(2,1)}), bf16[16,16,256]{2,1,0:T(8,128)(2,1)S(1)}, u32[]{:S(2)}, u32[]{:S(2)}) async-start(bf16[16,16,256]{2,1,0:T(8,128)(2,1)} %shard_map.64), calls=%async_computation | async-start | bytes 262144 | tf_op jit(solution)/shard_map/all_to_all | solution.py:197
  12.2 0.7 %copy-start.1 = (f32[2,16]{1,0:T(2,128)S(1)}, f32[2,16]{1,0:T(2,128)}, u32[]{:S(2)}) copy-start(f32[2,16]{1,0:T(2,128)} %param.9) | copy-start | bytes 388
  20.3 9.4 %copy-start.2 = (f32[2,16]{1,0:T(2,128)S(1)}, f32[2,16]{1,0:T(2,128)}, u32[]{:S(2)}) copy-start(f32[2,16]{1,0:T(2,128)} %param.10) | copy-start | bytes 388
  20.3 16.7 %all-to-all-start.1 = ((f32[16,2,128]{2,1,0:T(2,128)}), f32[16,2,128]{2,1,0:T(2,128)S(1)}, u32[]{:S(2)}, u32[]{:S(2)}) async-start(f32[16,2,128]{2,1,0:T(2,128)} %get-tuple-element.21), calls=%async_computation.1 | async-start | bytes 32768 | tf_op jit(solution)/shard_map/all_to_all | solution.py:216
  29.7 0.7 %copy-start.3 = (f32[16]{0:T(128)S(1)}, f32[16]{0:T(128)}, u32[]{:S(2)}) copy-start(f32[16]{0:T(128)} %param.11) | copy-start | bytes 196
  37.0 9.8 %collective-permute-start = (f32[2,128]{1,0:T(2,128)S(1)}, f32[2,128]{1,0:T(2,128)S(1)}, u32[]{:S(2)}, u32[]{:S(2)}) collective-permute-start(f32[2,128]{1,0:T(2,128)S(1)} %get-tuple-element.25), channel_id=1, source_target_pairs={{0,256},{1,257},{2,258},{3,259},{4,260},{5,261},{6,262},{7,263},{8... | collective-permute-start | bytes 3080 | tf_op jit(solution)/shard_map/ppermute | solution.py:226
  47.2 10.0 %copy-start = (bf16[256,256]{1,0:T(8,128)(2,1)S(1)}, bf16[256,256]{1,0:T(8,128)(2,1)}, u32[]{:S(2)}) copy-start(bf16[256,256]{1,0:T(8,128)(2,1)} %query_ref.1) | copy-start | bytes 393220

commit v5 on v4

v5 whole, which is shorter than its diff:
```python
import functools

import jax
import jax.numpy as jnp
from jax import lax
from jax.experimental import pallas as pl
from jax.experimental.pallas import tpu as pltpu
from jax.sharding import Mesh
from jax.sharding import PartitionSpec as P

F32 = jnp.float32
BF16 = jnp.bfloat16
VMEM = pl.BlockSpec(memory_space=pltpu.VMEM)
SMEM = pl.BlockSpec(memory_space=pltpu.SMEM)
HBM = pl.BlockSpec(memory_space=pltpu.HBM)
NT = (((1,), (1,)), ((), ()))
HALVES = 2


def call(body, out_shape, in_specs, flops, nbytes, vmem=16, **kw):
    return pl.pallas_call(
        body,
        out_shape=out_shape,
        in_specs=in_specs,
        out_specs=jax.tree.map(lambda _: VMEM, out_shape),
        cost_estimate=pl.CostEstimate(flops=flops, bytes_accessed=nbytes, transcendentals=0),
        compiler_params=pltpu.CompilerParams(vmem_limit_bytes=vmem << 20),
        **kw,
    )


def split(table):
    high = table.astype(BF16)
    return high, (table - high.astype(F32)).astype(BF16)


def dot(a, b):
    return jnp.dot(a, b, preferred_element_type=F32)


def dot_nt(a, b):
    return lax.dot_general(
        a, b, NT, precision=lax.Precision.HIGHEST, preferred_element_type=F32
    )


def own_lanes(shape, modes):
    row = lax.broadcasted_iota(jnp.int32, shape, len(shape) - 2)
    lane = lax.broadcasted_iota(jnp.int32, shape, len(shape) - 1)
    return row == lane // modes


def gate_in_kernel(keys_ref, values_ref, out_ref, keys_buf, values_buf, sems):
    half = keys_buf.shape[1]
    copies = []
    for h in range(2):
        part = pl.ds(h * half, half)
        copies.append(
            [
                pltpu.make_async_copy(keys_ref.at[part], keys_buf.at[h], sems.at[h, 0]),
                pltpu.make_async_copy(values_ref.at[part], values_buf.at[h], sems.at[h, 1]),
            ]
        )
        for copy in copies[h]:
            copy.start()
    blocks, rows, _ = out_ref.shape
    for h in range(2):
        for copy in copies[h]:
            copy.wait()
        z = keys_buf[h].astype(F32) * values_buf[h].astype(F32)
        out_ref[:, :, h * half : (h + 1) * half] = z.T.astype(BF16).reshape(blocks, rows, half)


def table_kernel(
    dims, place_ref, decay_ref, residue_ref,
    high_ref, low_ref, step_ref, grow_ref, inside_ref, whole_ref, cross_ref,
    conv_high_ref, conv_low_ref, after_ref,
):
    blocks, groups, size, length, modes = dims
    decay = decay_ref[...]
    lanes = decay.shape[1]
    row = lax.broadcasted_iota(jnp.int32, (length, length), 0)
    col = lax.broadcasted_iota(jnp.int32, (length, length), 1)
    position = lax.broadcasted_iota(jnp.int32, (length, lanes), 0).astype(F32)
    first = lax.broadcasted_iota(jnp.int32, (length, lanes), 1) < modes
    shape = (blocks, size, lanes)
    block = lax.broadcasted_iota(jnp.int32, shape, 0)
    for g in range(groups):
        rate = decay[g : g + 1]
        high, low = split(jnp.exp(-rate * ((length - 1) - position)))
        high_ref[g] = high
        low_ref[g] = low
        grow = jnp.exp(-rate[None] * (block * length).astype(F32))
        grow_ref[:, g] = jnp.where(own_lanes(shape, modes), grow, 0.0)
        amplitude = residue_ref[g : g + 1] * jnp.sqrt(2.0 * rate)
        rise = jnp.where(first, jnp.exp(rate * position), 0.0)
        fall = amplitude * jnp.exp(-rate * position)
        high, low = split(jnp.where(row <= col, dot_nt(rise, fall), 0.0))
        conv_high_ref[g] = high
        conv_low_ref[g] = low
        after_ref[g] = amplitude * jnp.exp(-rate * (position + 1.0))
    step_ref[...] = jnp.exp(-decay * float(length))
    shape = inside_ref.shape
    span = blocks * length
    place = place_ref[0]
    index = lax.broadcasted_iota(jnp.int32, shape, 0)
    gap = place - 1 - index
    away = jnp.maximum(gap, 0) * span
    inside_ref[...] = jnp.where(gap >= 0, jnp.exp(-decay[None] * away.astype(F32)), 0.0)
    left = (shape[0] - 1 - index) * span
    whole_ref[...] = jnp.exp(-decay[None] * left.astype(F32))
    cross_ref[...] = jnp.exp(-decay * (place * span).astype(F32))


def block_kernel(
    dims, z_ref, high_ref, low_ref, step_ref, conv_high_ref, conv_low_ref, after_ref, skip_ref,
    end_ref, out_ref, state_ref,
):
    blocks, groups, size, length, modes = dims
    lanes = step_ref.shape[1]
    z = z_ref[...].astype(F32)
    skipped = (skip_ref[...][None] * z).reshape(blocks, groups, size, length)
    z = z.reshape(blocks, groups, size, length)
    mine = own_lanes((size, lanes), modes)
    packed = []
    for g in range(groups):
        rows = z[:, g].reshape(blocks * size, length).astype(BF16)
        ends = (dot(rows, high_ref[g]) + dot(rows, low_ref[g])).reshape(blocks, size, lanes)
        step = step_ref[g : g + 1]
        state = jnp.zeros((size, lanes), F32)
        for b in range(blocks):
            state_ref[b] = state
            state = state * step + jnp.where(mine, ends[b], 0.0)
        packed.append(jnp.sum(state, axis=0, keepdims=True))
        conv = dot(rows, conv_high_ref[g]) + dot(rows, conv_low_ref[g])
        carried = dot_nt(state_ref[...].reshape(blocks * size, lanes), after_ref[g])
        out_ref[:, g] = (conv + carried).reshape(blocks, size, length) + skipped[:, g]
    packed = jnp.concatenate(packed, axis=0)
    end_ref[...] = jnp.broadcast_to(packed[None], end_ref.shape)


def total_kernel(ends_ref, whole_ref, total_ref):
    total_ref[...] = jnp.sum(ends_ref[...] * whole_ref[...], axis=0)


def carry_kernel(
    dims, ends_ref, inside_ref, before_ref, cross_ref, grow_ref, after_ref, local_ref, out_ref
):
    blocks, groups, size, length, modes = dims
    enter = jnp.sum(ends_ref[...] * inside_ref[...], axis=0)
    enter = enter + before_ref[...] * cross_ref[...]
    lanes = enter.shape[1]
    mixed = []
    for g in range(groups):
        state = (grow_ref[:, g] * enter[g : g + 1][None]).reshape(blocks * size, lanes)
        carried = dot_nt(state, after_ref[g]).reshape(blocks, size, length)
        mixed.append(local_ref[:, g] + carried)
    mixed = jnp.stack(mixed, axis=1).reshape(blocks, groups * size, length)
    out_ref[...] = mixed.astype(BF16)


def gate_out_kernel(query_ref, mixed_ref, out_ref):
    chan, length = out_ref.shape[1], out_ref.shape[0]
    mixed = mixed_ref[...].reshape(chan, length).astype(F32).T
    out_ref[...] = (query_ref[...].astype(F32) * mixed).astype(BF16)


def on_device(query, keys, values, decay, residue, skip):
    seq_count = lax.axis_size("yc")
    blocks = lax.axis_size("chan")
    length, chan = query.shape
    rows = skip.shape[0]
    groups, modes = decay.shape
    size = rows // groups
    lanes = size * modes
    dims = (blocks, groups, size, length, modes)
    shape = jax.ShapeDtypeStruct
    whole = length * chan

    decay_row = jnp.tile(decay, (1, size))
    residue_row = jnp.tile(residue, (1, size))
    skip_col = skip.reshape(rows, 1)
    place = lax.axis_index("yc").astype(jnp.int32).reshape(1)

    gated = call(
        gate_in_kernel, shape((blocks, rows, length), BF16), [HBM] * 2, whole, 6 * whole, 60,
        scratch_shapes=[
            pltpu.VMEM((2, length // 2, chan), BF16),
            pltpu.VMEM((2, length // 2, chan), BF16),
            pltpu.SemaphoreType.DMA((2, 2)),
        ],
    )(keys, values)
    z = lax.all_to_all(gated, "chan", 0, 0, tiled=True)
    table = shape((groups, length, lanes), BF16)
    conv_table = shape((groups, length, length), BF16)
    weights = shape((seq_count, groups, lanes), F32)
    vector = shape((groups, lanes), F32)
    high, low, step, grow, inside, total_w, cross, conv_high, conv_low, after = call(
        functools.partial(table_kernel, dims),
        (
            table, table, vector, shape((blocks, groups, size, lanes), F32),
            weights, weights, vector,
            conv_table, conv_table, shape((groups, length, lanes), F32),
        ),
        [SMEM, VMEM, VMEM], 100 * whole, 16 * whole,
    )(place, decay_row, residue_row)
    ends, local = call(
        functools.partial(block_kernel, dims),
        (weights, shape((blocks, groups, size, length), F32)),
        [VMEM] * 8, 8 * length * whole, 16 * whole,
        scratch_shapes=[pltpu.VMEM((blocks, size, lanes), F32)],
    )(z, high, low, step, conv_high, conv_low, after, skip_col)

    half = lax.axis_index("zh")
    exchange = lambda a: lax.all_to_all(a, "yc", 0, 0, tiled=True)
    keep = lambda a: a
    ends = lax.cond(half == 0, exchange, keep, ends)
    total = call(total_kernel, vector, [VMEM] * 2, whole, whole)(ends, total_w)
    before = lax.ppermute(total, "zh", [(0, 1)])
    ends = lax.cond(half == 1, exchange, keep, ends)
    mixed = call(
        functools.partial(carry_kernel, dims),
        shape((blocks, rows, length), BF16),
        [VMEM] * 7, 12 * lanes * whole, 8 * whole,
    )(ends, inside, before, cross, grow, after, local)
    mixed = lax.all_to_all(mixed, "chan", 0, 0, tiled=True)
    return call(
        gate_out_kernel, shape((length, chan), BF16), [VMEM] * 2, whole, 6 * whole
    )(query, mixed)


def solution(mesh):
    chan = mesh.shape["chan"]
    cut = Mesh(mesh.devices.reshape(HALVES, -1, chan), ("zh", "yc", "chan"))
    tokens = P(("zh", "yc", "chan"), None)
    return jax.shard_map(
        on_device,
        mesh=cut,
        in_specs=(tokens, tokens, tokens, P("chan", None), P("chan", None), P("chan")),
        out_specs=tokens,
        check_vma=False,
    )
```

time: 58.3 us -> 49.9 us (0.86)
  blocking collectives: 9.95 us -> 26.3 us
  starting transfers between devices: 27.7 us -> 11.7 us
  waiting for transfers between devices: 12.8 us -> 4.95 us
  Pallas kernels: 5.82 us -> 4.28 us
  local copies, waits for them, and re-layouts: 1.59 us -> 2.19 us
    all_to_all x0 -> x1, blocking collectives: none -> 16.3 us  [on_device(): exchange = lambda a: lax.all_to_all(a, 'yc', 0, 0, tiled=True)]
    all_to_all x1 -> x0, starting transfers between devices: 9.35 us -> none  [on_device(): ends = lax.all_to_all(ends, 'yc', 0, 0, tiled=True)]
    ppermute x1, starting transfers between devices: 7.93 us -> 1.29 us  [on_device(): before = lax.ppermute(total, 'zh', [(0, 1)])]
    all_to_all x1 -> x0, waiting for transfers between devices: 6.49 us -> none  [on_device(): ends = lax.all_to_all(ends, 'yc', 0, 0, tiled=True)]
    all_to_all x1, waiting for transfers between devices: 6.33 us -> 4.26 us  [on_device(): z = lax.all_to_all(gated, 'chan', 0, 0, tiled=True)]
    pallas_call x4 -> x3, Pallas kernels: 2.91 us -> 1.35 us  [the longest x1 0.78 us: on_device(): call(functools.partial(table_kernel, dims), (table, table, vector, shape(...]
    ppermute x1, waiting for transfers between devices: 0.01 us -> 0.69 us  [on_device(): before = lax.ppermute(total, 'zh', [(0, 1)])]
    unnamed x8, local copies, waits for them, and re-layouts: 1.34 us -> 1.94 us
  transfers between devices with their start and end apart: 3 -> 2, of which waited for: 2 -> 2; matrix products, arithmetic and copies ran while one was open for 0% -> 1% of each run, Pallas kernels for 4% -> 2%
where the time goes in v5:
time: 49.9 us; the launch traced here: 49.5 us
  blocking collectives  26.3 us (53%)
  starting transfers between devices  11.7 us (23%)
  waiting for transfers between devices  4.95 us (10%)
  Pallas kernels  4.28 us (9%)
  local copies, waits for them, and re-layouts  2.19 us (4%)
    all_to_all x1, blocking collectives, on_device(): exchange = lambda a: lax.all_to_all(a, 'yc', 0, 0, tiled=True)  16.3 us
    all_to_all x1, starting transfers between devices, on_device(): z = lax.all_to_all(gated, 'chan', 0, 0, tiled=True)  10.4 us
    all_to_all x1, blocking collectives, on_device(): mixed = lax.all_to_all(mixed, 'chan', 0, 0, tiled=True)  9.95 us
    all_to_all x1, waiting for transfers between devices, on_device(): z = lax.all_to_all(gated, 'chan', 0, 0, tiled=True)  4.26 us
    unnamed x8, local copies, waits for them, and re-layouts  1.94 us
    pallas_call x1, Pallas kernels, on_device(): call(gate_in_kernel, shape((blocks, rows, length), BF16), [HBM] * 2, whol...  1.77 us
    ppermute x1, starting transfers between devices, on_device(): before = lax.ppermute(total, 'zh', [(0, 1)])  1.29 us
  transfers between devices with their start and end apart: 2, of which 2 were waited for; matrix products, arithmetic and copies ran while one was open for 1% of the time, Pallas kernels for 2%

profile of v5, /device:TPU:1, one launch (start us, length us, event | category | flops | bytes accessed | tf_op | source)
XLA Modules:
  0.0 49.5 jit_solution(9442071868073224434)
XLA Ops:
  0.0 1.8 %shard_map.64 = bf16[16,16,256]{2,1,0:T(8,128)(2,1)} custom-call(bf16[256,256]{1,0:T(8,128)(2,1)} %keys_ref.1, bf16[256,256]{1,0:T(8,128)(2,1)} %values_ref.1), custom_call_target="tpu_custom_call" | custom-call | flops 65536 | bytes 393216 | tf_op jit(solution)/shard_map/pallas_call | solution.py:185
  1.8 10.4 %all-to-all-start.2 = ((bf16[16,16,256]{2,1,0:T(8,128)(2,1)}), bf16[16,16,256]{2,1,0:T(8,128)(2,1)S(1)}, u32[]{:S(2)}, u32[]{:S(2)}) async-start(bf16[16,16,256]{2,1,0:T(8,128)(2,1)} %shard_map.64), calls=%async_computation.2 | async-start | bytes 262144 | tf_op jit(solution)/shard_map/all_to_all | solution.py:193
  12.2 0.0 copy-start.1
  12.2 0.7 %copy-done.1 = f32[2,16]{1,0:T(2,128)S(1)} copy-done((f32[2,16]{1,0:T(2,128)S(1)}, f32[2,16]{1,0:T(2,128)}, u32[]{:S(2)}) %copy-start.1) | copy-done | bytes 152
  12.9 0.0 copy-start.2
  12.9 0.1 tile.21.residue_ref
  13.0 0.6 %copy-done.2 = f32[2,16]{1,0:T(2,128)S(1)} copy-done((f32[2,16]{1,0:T(2,128)S(1)}, f32[2,16]{1,0:T(2,128)}, u32[]{:S(2)}) %copy-start.2) | copy-done | bytes 152
  13.6 0.1 tile.9.decay_ref
  13.6 0.0 copy-start.3
  13.6 0.7 %copy-done.3 = f32[16]{0:T(128)S(1)} copy-done((f32[16]{0:T(128)S(1)}, f32[16]{0:T(128)}, u32[]{:S(2)}) %copy-start.3) | copy-done | bytes 88
  14.3 0.1 copy.7.skip_ref
  14.4 0.8 %shard_map.65 = (bf16[2,256,128]{2,1,0:T(8,128)(2,1)S(1)}, bf16[2,256,128]{2,1,0:T(8,128)(2,1)S(1)}, f32[2,128]{1,0:T(2,128)S(1)}, f32[16,2,8,128]{3,2,1,0:T(8,1...) custom-call(s32[1]{0:T(128)} %bitcast.place_ref, ...), custom_call_target="tpu_custom_call" | custom-call | flops 6553600 | bytes 1048576 | tf_op jit(solution)/shard_map/pallas_call | solution.py:198
  15.2 4.3 %all-to-all-done.2.z_ref = bf16[16,16,256]{2,1,0:T(8,128)(2,1)S(1)} async-done(((bf16[16,16,256]{2,1,0:T(8,128)(2,1)}), bf16[16,16,256]{2,1,0:T(8,128)(2,1)S(1)}, u32[]{:S(2)}, u32[]{:S(2)}) %all-to-all-start.2) | async-done | bytes 131104 | tf_op jit(solution)/shard_map/all_to_all | solution.py:193
  19.4 0.5 %shard_map.66 = (f32[16,2,128]{2,1,0:T(2,128)S(1)}, f32[16,2,8,256]{3,2,1,0:T(8,128)S(1)}) custom-call(bf16[16,16,256]{2,1,0:T(8,128)(2,1)S(1)} %all-to-all-done.2.z_ref, bf16[2,256,128]{2,1,0:T(8,128)(2,1)S(1)} %get-tuple-element.27.high_ref, bf16[2,256,128]{2,1,0:T(8,128)(2,1)S(1)} %get-tuple-element.28.low_ref, f32[2,128]{1,0:T(2,128)S(1)} %get-tuple-element.29.step_ref, ...), custom_call_target="tpu_custom_call" | custom-call | flops 134217728 | bytes 1048576 | tf_op jit(solution)/shard_map/pallas_call | solution.py:207
  20.0 16.4 %conditional.2 = (f32[16,2,128]{2,1,0:T(2,128)S(1)}) conditional(s32[]{:T(128)} %convert_element_type.7, f32[16,2,128]{2,1,0:T(2,128)S(1)} %get-tuple-element.33, f32[16,2,128]{2,1,0:T(2,128)S(1)} %get-tuple-element.33), branch_computations={%region_0.0_spmd, %region_1.0_spmd} | conditional | bytes 65544 | solution.py:217
  20.0 16.3 %all_to_all.18 = f32[16,2,128]{2,1,0:T(2,128)S(1)} all-to-all(f32[16,2,128]{2,1,0:T(2,128)S(1)} %copy.12), channel_id=1, replica_groups=mesh['zh'=2,'yc'=16,'chan'=16] {'yc'}, dimensions={0} | all-to-all | bytes 32768 | tf_op jit(solution)/shard_map/cond/branch_1_fun/all_to_all | solution.py:215
  36.4 1.3 %collective-permute-start = (f32[2,128]{1,0:T(2,128)S(1)}, f32[2,128]{1,0:T(2,128)S(1)}, u32[]{:S(2)}, u32[]{:S(2)}) collective-permute-start(f32[2,128]{1,0:T(2,128)S(1)} %shard_map.67), channel_id=1, source_target_pairs={{0,256},{1,257},{2,258},{3,259},{4,260},{5,261},{6,262},{7,263},{8... | collective-permute-start | bytes 3080 | tf_op jit(solution)/shard_map/ppermute | solution.py:219
  37.7 0.7 %collective-permute-done.before_ref = f32[2,128]{1,0:T(2,128)S(1)} collective-permute-done((f32[2,128]{1,0:T(2,128)S(1)}, f32[2,128]{1,0:T(2,128)S(1)}, u32[]{:S(2)}, u32[]{:S(2)}) %collective-permute-start) | collective-permute-done | bytes 1056 | tf_op jit(solution)/shard_map/ppermute | solution.py:219
  38.4 0.4 shard_map.68
  38.8 0.0 copy-start
  38.8 9.9 %all_to_all.20.mixed_ref = bf16[16,16,256]{2,1,0:T(8,128)(2,1)S(1)} all-to-all(bf16[16,16,256]{2,1,0:T(8,128)(2,1)S(1)} %shard_map.68), channel_id=1, replica_groups=mesh['zh'=2,'yc'=16,'chan'=16] {'chan'}, dimensions={0} | all-to-all | bytes 262144 | tf_op jit(solution)/shard_map/all_to_all | solution.py:226
  48.7 0.0 copy-done
  48.7 0.8 %shard_map.69 = bf16[256,256]{1,0:T(8,128)(2,1)} custom-call(bf16[256,256]{1,0:T(8,128)(2,1)S(1)} %copy-done, bf16[16,16,256]{2,1,0:T(8,128)(2,1)S(1)} %all_to_all.20.mixed_ref), custom_call_target="tpu_custom_call" | custom-call | flops 65536 | bytes 393216 | tf_op jit(solution)/shard_map/pallas_call | solution.py:227
  (5 shorter events, 0.0 us)
Async XLA Ops:
  1.8 17.6 %all-to-all-start.2 = ((bf16[16,16,256]{2,1,0:T(8,128)(2,1)}), bf16[16,16,256]{2,1,0:T(8,128)(2,1)S(1)}, u32[]{:S(2)}, u32[]{:S(2)}) async-start(bf16[16,16,256]{2,1,0:T(8,128)(2,1)} %shard_map.64), calls=%async_computation.2 | async-start | bytes 262144 | tf_op jit(solution)/shard_map/all_to_all | solution.py:193
  12.2 0.7 %copy-start.1 = (f32[2,16]{1,0:T(2,128)S(1)}, f32[2,16]{1,0:T(2,128)}, u32[]{:S(2)}) copy-start(f32[2,16]{1,0:T(2,128)} %param.14) | copy-start | bytes 388
  12.9 0.7 %copy-start.2 = (f32[2,16]{1,0:T(2,128)S(1)}, f32[2,16]{1,0:T(2,128)}, u32[]{:S(2)}) copy-start(f32[2,16]{1,0:T(2,128)} %param.13) | copy-start | bytes 388
  13.6 0.7 %copy-start.3 = (f32[16]{0:T(128)S(1)}, f32[16]{0:T(128)}, u32[]{:S(2)}) copy-start(f32[16]{0:T(128)} %param.15) | copy-start | bytes 196
  36.4 2.0 %collective-permute-start = (f32[2,128]{1,0:T(2,128)S(1)}, f32[2,128]{1,0:T(2,128)S(1)}, u32[]{:S(2)}, u32[]{:S(2)}) collective-permute-start(f32[2,128]{1,0:T(2,128)S(1)} %shard_map.67), channel_id=1, source_target_pairs={{0,256},{1,257},{2,258},{3,259},{4,260},{5,261},{6,262},{7,263},{8... | collective-permute-start | bytes 3080 | tf_op jit(solution)/shard_map/ppermute | solution.py:219
  38.8 10.0 %copy-start = (bf16[256,256]{1,0:T(8,128)(2,1)S(1)}, bf16[256,256]{1,0:T(8,128)(2,1)}, u32[]{:S(2)}) copy-start(bf16[256,256]{1,0:T(8,128)(2,1)} %query_ref.1) | copy-start | bytes 393220

commit v6 on v5

--- a/solution.py
+++ b/solution.py
@@ -72,10 +72,12 @@
 
 
 def table_kernel(
-    dims, place_ref, decay_ref, residue_ref,
+    dims, place_ref, decay_ref, residue_ref, query_ref,
     high_ref, low_ref, step_ref, grow_ref, inside_ref, whole_ref, cross_ref,
-    conv_high_ref, conv_low_ref, after_ref,
+    conv_high_ref, conv_low_ref, after_ref, query_out_ref, sem,
 ):
+    fetch = pltpu.make_async_copy(query_ref, query_out_ref, sem)
+    fetch.start()
     blocks, groups, size, length, modes = dims
     decay = decay_ref[...]
     lanes = decay.shape[1]
@@ -110,6 +112,7 @@
     left = (shape[0] - 1 - index) * span
     whole_ref[...] = jnp.exp(-decay[None] * left.astype(F32))
     cross_ref[...] = jnp.exp(-decay * (place * span).astype(F32))
+    fetch.wait()
 
 
 def block_kernel(
@@ -143,12 +146,8 @@
     total_ref[...] = jnp.sum(ends_ref[...] * whole_ref[...], axis=0)
 
 
-def carry_kernel(
-    dims, ends_ref, inside_ref, before_ref, cross_ref, grow_ref, after_ref, local_ref, out_ref
-):
+def add_carried(dims, enter, grow_ref, after_ref, local_ref, out_ref):
     blocks, groups, size, length, modes = dims
-    enter = jnp.sum(ends_ref[...] * inside_ref[...], axis=0)
-    enter = enter + before_ref[...] * cross_ref[...]
     lanes = enter.shape[1]
     mixed = []
     for g in range(groups):
@@ -157,6 +156,15 @@
         mixed.append(local_ref[:, g] + carried)
     mixed = jnp.stack(mixed, axis=1).reshape(blocks, groups * size, length)
     out_ref[...] = mixed.astype(BF16)
+
+
+def carry_first_kernel(dims, ends_ref, inside_ref, *refs):
+    add_carried(dims, jnp.sum(ends_ref[...] * inside_ref[...], axis=0), *refs)
+
+
+def carry_second_kernel(dims, ends_ref, inside_ref, before_ref, cross_ref, *refs):
+    enter = jnp.sum(ends_ref[...] * inside_ref[...], axis=0)
+    add_carried(dims, enter + before_ref[...] * cross_ref[...], *refs)
 
 
 def gate_out_kernel(query_ref, mixed_ref, out_ref):
@@ -195,15 +203,17 @@
     conv_table = shape((groups, length, length), BF16)
     weights = shape((seq_count, groups, lanes), F32)
     vector = shape((groups, lanes), F32)
-    high, low, step, grow, inside, total_w, cross, conv_high, conv_low, after = call(
+    high, low, step, grow, inside, total_w, cross, conv_high, conv_low, after, query_in = call(
         functools.partial(table_kernel, dims),
         (
             table, table, vector, shape((blocks, groups, size, lanes), F32),
             weights, weights, vector,
             conv_table, conv_table, shape((groups, length, lanes), F32),
+            shape((length, chan), BF16),
         ),
-        [SMEM, VMEM, VMEM], 100 * whole, 16 * whole,
-    )(place, decay_row, residue_row)
+        [SMEM, VMEM, VMEM, HBM], 100 * whole, 16 * whole,
+        scratch_shapes=[pltpu.SemaphoreType.DMA],
+    )(place, decay_row, residue_row, query)
     ends, local = call(
         functools.partial(block_kernel, dims),
         (weights, shape((blocks, groups, size, length), F32)),
@@ -213,20 +223,33 @@
 
     half = lax.axis_index("zh")
     exchange = lambda a: lax.all_to_all(a, "yc", 0, 0, tiled=True)
-    keep = lambda a: a
-    ends = lax.cond(half == 0, exchange, keep, ends)
+    ends = lax.cond(half == 0, exchange, lambda a: a, ends)
     total = call(total_kernel, vector, [VMEM] * 2, whole, whole)(ends, total_w)
     before = lax.ppermute(total, "zh", [(0, 1)])
-    ends = lax.cond(half == 1, exchange, keep, ends)
-    mixed = call(
-        functools.partial(carry_kernel, dims),
-        shape((blocks, rows, length), BF16),
-        [VMEM] * 7, 12 * lanes * whole, 8 * whole,
-    )(ends, inside, before, cross, grow, after, local)
-    mixed = lax.all_to_all(mixed, "chan", 0, 0, tiled=True)
+
+    def finish(kernel, args):
+        mixed = call(
+            functools.partial(kernel, dims), shape((blocks, rows, length), BF16),
+            [VMEM] * (len(args) + 3), 12 * lanes * whole, 8 * whole,
+        )(*args, grow, after, local)
+        return lax.all_to_all(mixed, "chan", 0, 0, tiled=True)
+
+    def first_half(ends, mixed):
+        return ends, finish(carry_first_kernel, (ends, inside))
+
+    def second_half(ends, mixed):
+        return exchange(ends), mixed
+
+    ends, mixed = lax.cond(half == 0, first_half, second_half, ends, z)
+    mixed = lax.cond(
+        half == 1,
+        lambda mixed, before: finish(carry_second_kernel, (ends, inside, before, cross)),
+        lambda mixed, before: mixed,
+        mixed, before,
+    )
     return call(
         gate_out_kernel, shape((length, chan), BF16), [VMEM] * 2, whole, 6 * whole
-    )(query, mixed)
+    )(query_in, mixed)
 
 
 def solution(mesh):

time: 49.9 us -> 49.2 us (0.986)
  waiting for transfers between devices: 4.95 us -> 4.09 us
    ppermute x1, waiting for transfers between devices: 0.69 us -> 0.01 us  [on_device(): before = lax.ppermute(total, 'zh', [(0, 1)])]
  transfers between devices with their start and end apart: 2 -> 2, of which waited for: 2 -> 1; matrix products, arithmetic and copies ran while one was open for 1% -> 1% of each run, Pallas kernels for 2% -> 3%
where the time goes in v6:
time: 49.2 us; the launch traced here: 48.8 us
  blocking collectives  26.2 us (53%)
  starting transfers between devices  11.8 us (24%)
  Pallas kernels  4.44 us (9%)
  waiting for transfers between devices  4.09 us (8%)
  local copies, waits for them, and re-layouts  2.19 us (4%)
    all_to_all x1, blocking collectives, on_device(): exchange = lambda a: lax.all_to_all(a, 'yc', 0, 0, tiled=True)  16.3 us
    all_to_all x1, starting transfers between devices, on_device(): z = lax.all_to_all(gated, 'chan', 0, 0, tiled=True)  10.5 us
    all_to_all x1, blocking collectives, finish(): return lax.all_to_all(mixed, 'chan', 0, 0, tiled=True)  9.82 us
    all_to_all x1, waiting for transfers between devices, on_device(): z = lax.all_to_all(gated, 'chan', 0, 0, tiled=True)  4.09 us
    unnamed x8, local copies, waits for them, and re-layouts  1.94 us
    pallas_call x1, Pallas kernels, on_device(): call(gate_in_kernel, shape((blocks, rows, length), BF16), [HBM] * 2, whol...  1.77 us
    ppermute x1, starting transfers between devices, on_device(): before = lax.ppermute(total, 'zh', [(0, 1)])  1.29 us
  transfers between devices with their start and end apart: 2, of which 1 were waited for; matrix products, arithmetic and copies ran while one was open for 1% of the time, Pallas kernels for 3%

profile of v6, /device:TPU:1, one launch (start us, length us, event | category | flops | bytes accessed | tf_op | source)
XLA Modules:
  0.0 48.8 jit_solution(4804812386730113202)
XLA Ops:
  0.0 1.8 %shard_map.65 = bf16[16,16,256]{2,1,0:T(8,128)(2,1)} custom-call(bf16[256,256]{1,0:T(8,128)(2,1)} %keys_ref.1, bf16[256,256]{1,0:T(8,128)(2,1)} %values_ref.1), custom_call_target="tpu_custom_call" | custom-call | flops 65536 | bytes 393216 | tf_op jit(solution)/shard_map/pallas_call | solution.py:193
  1.8 0.0 copy-start
  1.8 10.5 %all-to-all-start.4 = ((bf16[16,16,256]{2,1,0:T(8,128)(2,1)}), bf16[16,16,256]{2,1,0:T(8,128)(2,1)S(1)}, u32[]{:S(2)}, u32[]{:S(2)}) async-start(bf16[16,16,256]{2,1,0:T(8,128)(2,1)} %shard_map.65), calls=%async_computation.4 | async-start | bytes 262144 | tf_op jit(solution)/shard_map/all_to_all | solution.py:201
  12.3 0.0 copy-start.1
  12.3 0.7 %copy-done.1 = f32[2,16]{1,0:T(2,128)S(1)} copy-done((f32[2,16]{1,0:T(2,128)S(1)}, f32[2,16]{1,0:T(2,128)}, u32[]{:S(2)}) %copy-start.1) | copy-done | bytes 152
  13.0 0.0 copy-start.2
  13.0 0.1 tile.21.residue_ref
  13.1 0.6 %copy-done.2 = f32[2,16]{1,0:T(2,128)S(1)} copy-done((f32[2,16]{1,0:T(2,128)S(1)}, f32[2,16]{1,0:T(2,128)}, u32[]{:S(2)}) %copy-start.2) | copy-done | bytes 152
  13.7 0.1 tile.9.decay_ref
  13.8 0.0 copy-start.3
  13.8 0.7 %copy-done.3 = f32[16]{0:T(128)S(1)} copy-done((f32[16]{0:T(128)S(1)}, f32[16]{0:T(128)}, u32[]{:S(2)}) %copy-start.3) | copy-done | bytes 88
  14.4 0.1 copy.7.skip_ref
  14.5 0.0 copy-done
  14.5 1.0 %shard_map.64 = (bf16[2,256,128]{2,1,0:T(8,128)(2,1)S(1)}, bf16[2,256,128]{2,1,0:T(8,128)(2,1)S(1)}, f32[2,128]{1,0:T(2,128)S(1)}, f32[16,2,8,128]{3,2,1,0:T(8,1...) custom-call(s32[1]{0:T(128)} %bitcast.place_ref, ...), custom_call_target="tpu_custom_call" | custom-call | flops 6553600 | bytes 1048576 | tf_op jit(solution)/shard_map/pallas_call | solution.py:206
  15.5 4.1 %all-to-all-done.4.z_ref = bf16[16,16,256]{2,1,0:T(8,128)(2,1)S(1)} async-done(((bf16[16,16,256]{2,1,0:T(8,128)(2,1)}), bf16[16,16,256]{2,1,0:T(8,128)(2,1)S(1)}, u32[]{:S(2)}, u32[]{:S(2)}) %all-to-all-start.4) | async-done | bytes 131104 | tf_op jit(solution)/shard_map/all_to_all | solution.py:201
  19.6 0.5 %shard_map.66 = (f32[16,2,128]{2,1,0:T(2,128)S(1)}, f32[16,2,8,256]{3,2,1,0:T(8,128)S(1)}) custom-call(bf16[16,16,256]{2,1,0:T(8,128)(2,1)S(1)} %all-to-all-done.4.z_ref, bf16[2,256,128]{2,1,0:T(8,128)(2,1)S(1)} %get-tuple-element.72.high_ref, bf16[2,256,128]{2,1,0:T(8,128)(2,1)S(1)} %get-tuple-element.73.low_ref, f32[2,128]{1,0:T(2,128)S(1)} %get-tuple-element.74.step_ref, ...), custom_call_target="tpu_custom_call" | custom-call | flops 134217728 | bytes 1048576 | tf_op jit(solution)/shard_map/pallas_call | solution.py:217
  20.1 16.4 %conditional.3 = (f32[16,2,128]{2,1,0:T(2,128)S(1)}) conditional(s32[]{:T(128)} %convert_element_type.8, f32[16,2,128]{2,1,0:T(2,128)S(1)} %get-tuple-element.78, f32[16,2,128]{2,1,0:T(2,128)S(1)} %get-tuple-element.78), branch_computations={%region_0.0_spmd, %region_1.0_spmd} | conditional | bytes 65544 | solution.py:226
  20.2 16.3 %all_to_all.21 = f32[16,2,128]{2,1,0:T(2,128)S(1)} all-to-all(f32[16,2,128]{2,1,0:T(2,128)S(1)} %copy.16), channel_id=1, replica_groups=mesh['zh'=2,'yc'=16,'chan'=16] {'yc'}, dimensions={0} | all-to-all | bytes 32768 | tf_op jit(solution)/shard_map/cond/branch_1_fun/all_to_all | solution.py:225
  36.5 1.3 %collective-permute-start = (f32[2,128]{1,0:T(2,128)S(1)}, f32[2,128]{1,0:T(2,128)S(1)}, u32[]{:S(2)}, u32[]{:S(2)}) collective-permute-start(f32[2,128]{1,0:T(2,128)S(1)} %shard_map.67), channel_id=1, source_target_pairs={{0,256},{1,257},{2,258},{3,259},{4,260},{5,261},{6,262},{7,263},{8... | collective-permute-start | bytes 3080 | tf_op jit(solution)/shard_map/ppermute | solution.py:228
  37.8 10.2 %conditional.4 = (f32[16,2,128]{2,1,0:T(2,128)S(1)}, bf16[16,16,256]{2,1,0:T(8,128)(2,1)S(1)}) conditional(s32[]{:T(128)} %convert_element_type.8, (f32[16,2,128]{2,1,0:T(2,128)S(1)}, bf16[16,16,256]{2,1,0:T(8,128)(2,1)S(1)}) %tuple.25, (f32[16,2,128]{2,1,0:T(2,128)S(1)}, f32[16,2,128]{2,1,0:T(2,128)S(1)}, f32[16,2,8,128]{3,2,1,0:T(8,128)S(1)}, ...), branch_computations={%region_2.0_spmd, %region_3.0_spmd} | conditional | flops 100663296 | bytes 786448 | solution.py:243
  37.8 0.4 branch_1_fun.2
  38.2 9.8 %all_to_all.24 = bf16[16,16,256]{2,1,0:T(8,128)(2,1)S(1)} all-to-all(bf16[16,16,256]{2,1,0:T(8,128)(2,1)S(1)} %branch_1_fun.2), channel_id=1, replica_groups=mesh['zh'=2,'yc'=16,'chan'=16] {'chan'}, dimensions={0} | all-to-all | bytes 262144 | tf_op jit(solution)/shard_map/cond/branch_1_fun/all_to_all | solution.py:235
  48.1 0.0 collective-permute-done
  48.1 0.8 %shard_map.68 = bf16[256,256]{1,0:T(8,128)(2,1)} custom-call(bf16[256,256]{1,0:T(8,128)(2,1)S(1)} %get-tuple-element.71.query_ref, bf16[16,16,256]{2,1,0:T(8,128)(2,1)S(1)} %get-tuple-element.91.mixed_ref), custom_call_target="tpu_custom_call" | custom-call | flops 65536 | bytes 393216 | tf_op jit(solution)/shard_map/pallas_call | solution.py:250
  (5 shorter events, 0.0 us)
Async XLA Ops:
  1.8 12.7 %copy-start = (bf16[256,256]{1,0:T(8,128)(2,1)S(1)}, bf16[256,256]{1,0:T(8,128)(2,1)}, u32[]{:S(2)}) copy-start(bf16[256,256]{1,0:T(8,128)(2,1)} %query_ref.1) | copy-start | bytes 393220
  1.8 17.8 %all-to-all-start.4 = ((bf16[16,16,256]{2,1,0:T(8,128)(2,1)}), bf16[16,16,256]{2,1,0:T(8,128)(2,1)S(1)}, u32[]{:S(2)}, u32[]{:S(2)}) async-start(bf16[16,16,256]{2,1,0:T(8,128)(2,1)} %shard_map.65), calls=%async_computation.4 | async-start | bytes 262144 | tf_op jit(solution)/shard_map/all_to_all | solution.py:201
  12.3 0.7 %copy-start.1 = (f32[2,16]{1,0:T(2,128)S(1)}, f32[2,16]{1,0:T(2,128)}, u32[]{:S(2)}) copy-start(f32[2,16]{1,0:T(2,128)} %param.16) | copy-start | bytes 388
  13.0 0.7 %copy-start.2 = (f32[2,16]{1,0:T(2,128)S(1)}, f32[2,16]{1,0:T(2,128)}, u32[]{:S(2)}) copy-start(f32[2,16]{1,0:T(2,128)} %param.15) | copy-start | bytes 388
  13.8 0.7 %copy-start.3 = (f32[16]{0:T(128)S(1)}, f32[16]{0:T(128)}, u32[]{:S(2)}) copy-start(f32[16]{0:T(128)} %param.17) | copy-start | bytes 196
  36.5 11.5 %collective-permute-start = (f32[2,128]{1,0:T(2,128)S(1)}, f32[2,128]{1,0:T(2,128)S(1)}, u32[]{:S(2)}, u32[]{:S(2)}) collective-permute-start(f32[2,128]{1,0:T(2,128)S(1)} %shard_map.67), channel_id=1, source_target_pairs={{0,256},{1,257},{2,258},{3,259},{4,260},{5,261},{6,262},{7,263},{8... | collective-permute-start | bytes 3080 | tf_op jit(solution)/shard_map/ppermute | solution.py:228

commit v7 on v6

--- a/solution.py
+++ b/solution.py
@@ -15,6 +15,10 @@
 HBM = pl.BlockSpec(memory_space=pltpu.HBM)
 NT = (((1,), (1,)), ((), ()))
 HALVES = 2
+
+TOKENS_IN = [10, 11, 12, 0, 4, 3, 13, 2, 1, 7, 9, 15, 8, 14, 5, 6]
+STATES = ([11, 8, 0, 4, 5, 15, 6, 7, 3, 12, 9, 1, 13, 2, 10, 14], [9, 8, 7, 13, 4, 0, 14, 12, 1, 3, 10, 11, 5, 6, 15, 2])
+TOKENS_OUT = ([10, 13, 6, 0, 9, 8, 3, 12, 5, 11, 2, 1, 4, 15, 7, 14], [9, 3, 7, 14, 10, 13, 8, 1, 6, 15, 2, 5, 4, 11, 0, 12])
 
 
 def call(body, out_shape, in_specs, flops, nbytes, vmem=16, **kw):
@@ -50,7 +54,15 @@
     return row == lane // modes
 
 
-def gate_in_kernel(keys_ref, values_ref, out_ref, keys_buf, values_buf, sems):
+def take(data, order):
+    return jnp.stack([data[i] for i in order], axis=0)
+
+
+def inverse(order):
+    return [order.index(i) for i in range(len(order))]
+
+
+def gate_in_kernel(order, keys_ref, values_ref, out_ref, keys_buf, values_buf, sems):
     half = keys_buf.shape[1]
     copies = []
     for h in range(2):
@@ -68,11 +80,12 @@
         for copy in copies[h]:
             copy.wait()
         z = keys_buf[h].astype(F32) * values_buf[h].astype(F32)
-        out_ref[:, :, h * half : (h + 1) * half] = z.T.astype(BF16).reshape(blocks, rows, half)
+        z = take(z.T.reshape(blocks, rows, half), order)
+        out_ref[:, :, h * half : (h + 1) * half] = z.astype(BF16)
 
 
 def table_kernel(
-    dims, place_ref, decay_ref, residue_ref, query_ref,
+    dims, orders, place_ref, decay_ref, residue_ref, query_ref,
     high_ref, low_ref, step_ref, grow_ref, inside_ref, whole_ref, cross_ref,
     conv_high_ref, conv_low_ref, after_ref, query_out_ref, sem,
 ):
@@ -105,7 +118,10 @@
     shape = inside_ref.shape
     span = blocks * length
     place = place_ref[0]
-    index = lax.broadcasted_iota(jnp.int32, shape, 0)
+    message = lax.broadcasted_iota(jnp.int32, shape, 0)
+    index = jnp.zeros(shape, jnp.int32)
+    for b, members in enumerate(zip(*orders)):
+        index = jnp.where(message == b, jnp.where(place_ref[1] == 0, *members), index)
     gap = place - 1 - index
     away = jnp.maximum(gap, 0) * span
     inside_ref[...] = jnp.where(gap >= 0, jnp.exp(-decay[None] * away.astype(F32)), 0.0)
@@ -116,12 +132,12 @@
 
 
 def block_kernel(
-    dims, z_ref, high_ref, low_ref, step_ref, conv_high_ref, conv_low_ref, after_ref, skip_ref,
+    dims, order, z_ref, high_ref, low_ref, step_ref, conv_high_ref, conv_low_ref, after_ref, skip_ref,
     end_ref, out_ref, state_ref,
 ):
     blocks, groups, size, length, modes = dims
     lanes = step_ref.shape[1]
-    z = z_ref[...].astype(F32)
+    z = take(z_ref[...].astype(F32), inverse(order))
     skipped = (skip_ref[...][None] * z).reshape(blocks, groups, size, length)
     z = z.reshape(blocks, groups, size, length)
     mine = own_lanes((size, lanes), modes)
@@ -146,7 +162,7 @@
     total_ref[...] = jnp.sum(ends_ref[...] * whole_ref[...], axis=0)
 
 
-def add_carried(dims, enter, grow_ref, after_ref, local_ref, out_ref):
+def add_carried(dims, order, enter, grow_ref, after_ref, local_ref, out_ref):
     blocks, groups, size, length, modes = dims
     lanes = enter.shape[1]
     mixed = []
@@ -155,22 +171,27 @@
         carried = dot_nt(state, after_ref[g]).reshape(blocks, size, length)
         mixed.append(local_ref[:, g] + carried)
     mixed = jnp.stack(mixed, axis=1).reshape(blocks, groups * size, length)
-    out_ref[...] = mixed.astype(BF16)
-
-
-def carry_first_kernel(dims, ends_ref, inside_ref, *refs):
-    add_carried(dims, jnp.sum(ends_ref[...] * inside_ref[...], axis=0), *refs)
-
-
-def carry_second_kernel(dims, ends_ref, inside_ref, before_ref, cross_ref, *refs):
+    out_ref[...] = take(mixed, order).astype(BF16)
+
+
+def carry_first_kernel(dims, order, ends_ref, inside_ref, *refs):
+    add_carried(dims, order, jnp.sum(ends_ref[...] * inside_ref[...], axis=0), *refs)
+
+
+def carry_second_kernel(dims, order, ends_ref, inside_ref, before_ref, cross_ref, *refs):
     enter = jnp.sum(ends_ref[...] * inside_ref[...], axis=0)
-    add_carried(dims, enter + before_ref[...] * cross_ref[...], *refs)
-
-
-def gate_out_kernel(query_ref, mixed_ref, out_ref):
+    add_carried(dims, order, enter + before_ref[...] * cross_ref[...], *refs)
+
+
+def gate_out_kernel(orders, place_ref, query_ref, mixed_ref, out_ref):
     chan, length = out_ref.shape[1], out_ref.shape[0]
-    mixed = mixed_ref[...].reshape(chan, length).astype(F32).T
-    out_ref[...] = (query_ref[...].astype(F32) * mixed).astype(BF16)
+
+    def gate(order):
+        mixed = take(mixed_ref[...].astype(F32), inverse(order)).reshape(chan, length).T
+        out_ref[...] = (query_ref[...].astype(F32) * mixed).astype(BF16)
+
+    for half, order in enumerate(orders):
+        pl.when(place_ref[1] == half)(functools.partial(gate, order))
 
 
 def on_device(query, keys, values, decay, residue, skip):
@@ -188,23 +209,29 @@
     decay_row = jnp.tile(decay, (1, size))
     residue_row = jnp.tile(residue, (1, size))
     skip_col = skip.reshape(rows, 1)
-    place = lax.axis_index("yc").astype(jnp.int32).reshape(1)
+    place = jnp.stack([lax.axis_index("yc"), lax.axis_index("zh")]).astype(jnp.int32)
+
+    def exchange(axis, order):
+        return lambda a: lax.all_to_all(
+            a, axis, 0, 0, tiled=True, axis_index_groups=[list(order)]
+        )
 
     gated = call(
-        gate_in_kernel, shape((blocks, rows, length), BF16), [HBM] * 2, whole, 6 * whole, 60,
+        functools.partial(gate_in_kernel, TOKENS_IN), shape((blocks, rows, length), BF16),
+        [HBM] * 2, whole, 6 * whole, 60,
         scratch_shapes=[
             pltpu.VMEM((2, length // 2, chan), BF16),
             pltpu.VMEM((2, length // 2, chan), BF16),
             pltpu.SemaphoreType.DMA((2, 2)),
         ],
     )(keys, values)
-    z = lax.all_to_all(gated, "chan", 0, 0, tiled=True)
+    z = exchange("chan", TOKENS_IN)(gated)
     table = shape((groups, length, lanes), BF16)
     conv_table = shape((groups, length, length), BF16)
     weights = shape((seq_count, groups, lanes), F32)
     vector = shape((groups, lanes), F32)
     high, low, step, grow, inside, total_w, cross, conv_high, conv_low, after, query_in = call(
-        functools.partial(table_kernel, dims),
+        functools.partial(table_kernel, dims, STATES),
         (
             table, table, vector, shape((blocks, groups, size, lanes), F32),
             weights, weights, vector,
@@ -215,41 +242,39 @@
         scratch_shapes=[pltpu.SemaphoreType.DMA],
     )(place, decay_row, residue_row, query)
     ends, local = call(
-        functools.partial(block_kernel, dims),
+        functools.partial(block_kernel, dims, TOKENS_IN),
         (weights, shape((blocks, groups, size, length), F32)),
         [VMEM] * 8, 8 * length * whole, 16 * whole,
         scratch_shapes=[pltpu.VMEM((blocks, size, lanes), F32)],
     )(z, high, low, step, conv_high, conv_low, after, skip_col)
 
     half = lax.axis_index("zh")
-    exchange = lambda a: lax.all_to_all(a, "yc", 0, 0, tiled=True)
-    ends = lax.cond(half == 0, exchange, lambda a: a, ends)
+    ends = lax.cond(half == 0, exchange("yc", STATES[0]), lambda a: a, ends)
     total = call(total_kernel, vector, [VMEM] * 2, whole, whole)(ends, total_w)
     before = lax.ppermute(total, "zh", [(0, 1)])
 
-    def finish(kernel, args):
+    def finish(kernel, order, args):
         mixed = call(
-            functools.partial(kernel, dims), shape((blocks, rows, length), BF16),
+            functools.partial(kernel, dims, order), shape((blocks, rows, length), BF16),
             [VMEM] * (len(args) + 3), 12 * lanes * whole, 8 * whole,
         )(*args, grow, after, local)
-        return lax.all_to_all(mixed, "chan", 0, 0, tiled=True)
+        return exchange("chan", order)(mixed)
 
     def first_half(ends, mixed):
-        return ends, finish(carry_first_kernel, (ends, inside))
+        return ends, finish(carry_first_kernel, TOKENS_OUT[0], (ends, inside))
 
     def second_half(ends, mixed):
-        return exchange(ends), mixed
+        return exchange("yc", STATES[1])(ends), mixed
+
+    def second_finish(mixed, before):
+        return finish(carry_second_kernel, TOKENS_OUT[1], (ends, inside, before, cross))
 
     ends, mixed = lax.cond(half == 0, first_half, second_half, ends, z)
-    mixed = lax.cond(
-        half == 1,
-        lambda mixed, before: finish(carry_second_kernel, (ends, inside, before, cross)),
-        lambda mixed, before: mixed,
-        mixed, before,
-    )
+    mixed = lax.cond(half == 1, second_finish, lambda mixed, before: mixed, mixed, before)
     return call(
-        gate_out_kernel, shape((length, chan), BF16), [VMEM] * 2, whole, 6 * whole
-    )(query_in, mixed)
+        functools.partial(gate_out_kernel, TOKENS_OUT), shape((length, chan), BF16),
+        [SMEM] + [VMEM] * 2, whole, 6 * whole,
+    )(place, query_in, mixed)
 
 
 def solution(mesh):

time: 49.2 us -> 42.8 us (0.87)
  blocking collectives: 26.2 us -> 21.6 us
  waiting for transfers between devices: 4.09 us -> 0.01 us
  Pallas kernels: 4.44 us -> 5.55 us
  starting transfers between devices: 11.8 us -> 12.6 us
    all_to_all x2, blocking collectives: 26.2 us -> 21.6 us  [exchange(): lax.all_to_all(a, axis, 0, 0, tiled=True, axis_index_groups=[list(order)])]
    all_to_all x1, waiting for transfers between devices: 4.09 us -> 0.01 us  [exchange(): lax.all_to_all(a, axis, 0, 0, tiled=True, axis_index_groups=[list(order)])]
    pallas_call x5, Pallas kernels: 4.42 us -> 5.53 us  [the longest x1 1.77 us: on_device(): call(functools.partial(gate_in_kernel, TOKENS_IN), shape((blocks, rows, l...]
    all_to_all x1, starting transfers between devices: 10.5 us -> 11.3 us  [exchange(): lax.all_to_all(a, axis, 0, 0, tiled=True, axis_index_groups=[list(order)])]
  transfers between devices with their start and end apart: 2 -> 2, of which waited for: 1 -> 0; matrix products, arithmetic and copies ran while one was open for 1% -> 1% of each run, Pallas kernels for 3% -> 5%
where the time goes in v7:
time: 42.8 us; the launch traced here: 42.1 us
  blocking collectives  21.6 us (50%)
  starting transfers between devices  12.6 us (29%)
  Pallas kernels  5.55 us (13%)
  local copies, waits for them, and re-layouts  2.19 us (5%)
    all_to_all x2, blocking collectives, exchange(): lax.all_to_all(a, axis, 0, 0, tiled=True, axis_index_groups=[list(order)])  21.6 us
    all_to_all x1, starting transfers between devices, exchange(): lax.all_to_all(a, axis, 0, 0, tiled=True, axis_index_groups=[list(order)])  11.3 us
    unnamed x8, local copies, waits for them, and re-layouts  1.93 us
    pallas_call x1, Pallas kernels, on_device(): call(functools.partial(gate_in_kernel, TOKENS_IN), shape((blocks, rows, l...  1.77 us
    pallas_call x1, Pallas kernels, on_device(): call(functools.partial(table_kernel, dims, STATES), (table, table, vector...  1.52 us
    pallas_call x1, Pallas kernels, on_device(): call(functools.partial(gate_out_kernel, TOKENS_OUT), shape((length, chan)...  1.31 us
    ppermute x1, starting transfers between devices, on_device(): before = lax.ppermute(total, 'zh', [(0, 1)])  1.29 us
  transfers between devices with their start and end apart: 2, of which 0 were waited for; matrix products, arithmetic and copies ran while one was open for 1% of the time, Pallas kernels for 5%

profile of v7, /device:TPU:1, one launch (start us, length us, event | category | flops | bytes accessed | tf_op | source)
XLA Modules:
  0.0 42.1 jit_solution(5816959107577561456)
XLA Ops:
  0.0 1.8 %shard_map.65 = bf16[16,16,256]{2,1,0:T(8,128)(2,1)} custom-call(bf16[256,256]{1,0:T(8,128)(2,1)} %keys_ref.1, bf16[256,256]{1,0:T(8,128)(2,1)} %values_ref.1), custom_call_target="tpu_custom_call" | custom-call | flops 65536 | bytes 393216 | tf_op jit(solution)/shard_map/pallas_call | solution.py:219
  1.8 0.0 copy-start
  1.8 11.3 %all-to-all-start.4 = ((bf16[16,16,256]{2,1,0:T(8,128)(2,1)}), bf16[16,16,256]{2,1,0:T(8,128)(2,1)S(1)}, u32[]{:S(2)}, u32[]{:S(2)}) async-start(bf16[16,16,256]{2,1,0:T(8,128)(2,1)} %shard_map.65), calls=%async_computation.4 | async-start | bytes 262144 | tf_op jit(solution)/shard_map/all_to_all | solution.py:215
  13.1 0.0 copy-start.1
  13.1 0.7 %copy-done.1 = f32[2,16]{1,0:T(2,128)S(1)} copy-done((f32[2,16]{1,0:T(2,128)S(1)}, f32[2,16]{1,0:T(2,128)}, u32[]{:S(2)}) %copy-start.1) | copy-done | bytes 152
  13.8 0.0 copy-start.2
  13.8 0.1 tile.21.residue_ref
  13.9 0.6 %copy-done.2 = f32[2,16]{1,0:T(2,128)S(1)} copy-done((f32[2,16]{1,0:T(2,128)S(1)}, f32[2,16]{1,0:T(2,128)}, u32[]{:S(2)}) %copy-start.2) | copy-done | bytes 152
  14.5 0.1 tile.9.decay_ref
  14.6 0.7 %copy-done.3 = f32[16]{0:T(128)S(1)} copy-done((f32[16]{0:T(128)S(1)}, f32[16]{0:T(128)}, u32[]{:S(2)}) %copy-start.3) | copy-done | bytes 88
  15.2 0.1 copy.7.skip_ref
  15.3 0.1 pad_add_fusion.place_ref
  15.4 0.0 copy-done
  15.4 1.5 %shard_map.64 = (bf16[2,256,128]{2,1,0:T(8,128)(2,1)S(1)}, bf16[2,256,128]{2,1,0:T(8,128)(2,1)S(1)}, f32[2,128]{1,0:T(2,128)S(1)}, f32[16,2,8,128]{3,2,1,0:T(8,1...) custom-call(s32[2]{0:T(128)S(1)} %pad_add_fusion.place_ref, ...), custom_call_target="tpu_custom_call" | custom-call | flops 6553600 | bytes 1048576 | tf_op jit(solution)/shard_map/pallas_call | solution.py:233
  16.9 0.0 all-to-all-done.4.z_ref
  16.9 0.5 %shard_map.66 = (f32[16,2,128]{2,1,0:T(2,128)S(1)}, f32[16,2,8,256]{3,2,1,0:T(8,128)S(1)}) custom-call(bf16[16,16,256]{2,1,0:T(8,128)(2,1)S(1)} %all-to-all-done.4.z_ref, bf16[2,256,128]{2,1,0:T(8,128)(2,1)S(1)} %get-tuple-element.72.high_ref, bf16[2,256,128]{2,1,0:T(8,128)(2,1)S(1)} %get-tuple-element.73.low_ref, f32[2,128]{1,0:T(2,128)S(1)} %get-tuple-element.74.step_ref, ...), custom_call_target="tpu_custom_call" | custom-call | flops 134217728 | bytes 1048576 | tf_op jit(solution)/shard_map/pallas_call | solution.py:244
  17.5 11.8 %conditional.3 = (f32[16,2,128]{2,1,0:T(2,128)S(1)}) conditional(s32[]{:T(128)} %convert_element_type.8, f32[16,2,128]{2,1,0:T(2,128)S(1)} %get-tuple-element.78, f32[16,2,128]{2,1,0:T(2,128)S(1)} %get-tuple-element.78), branch_computations={%region_0.0_spmd, %region_1.0_spmd} | conditional | bytes 65544 | solution.py:252
  17.5 11.8 %all_to_all.21 = f32[16,2,128]{2,1,0:T(2,128)S(1)} all-to-all(f32[16,2,128]{2,1,0:T(2,128)S(1)} %copy.16), channel_id=1, replica_groups={{176,128,0,64,80,240,96,112,48,192,144,16,208,32,160,224},{177,129,1,65..., dimensions={0} | all-to-all | bytes 32768 | tf_op jit(solution)/shard_map/cond/branch_1_fun/all_to_all | solution.py:215
  29.3 1.3 %collective-permute-start = (f32[2,128]{1,0:T(2,128)S(1)}, f32[2,128]{1,0:T(2,128)S(1)}, u32[]{:S(2)}, u32[]{:S(2)}) collective-permute-start(f32[2,128]{1,0:T(2,128)S(1)} %shard_map.67), channel_id=1, source_target_pairs={{0,256},{1,257},{2,258},{3,259},{4,260},{5,261},{6,262},{7,263},{8... | collective-permute-start | bytes 3080 | tf_op jit(solution)/shard_map/ppermute | solution.py:254
  30.6 10.2 %conditional.4 = (f32[16,2,128]{2,1,0:T(2,128)S(1)}, bf16[16,16,256]{2,1,0:T(8,128)(2,1)S(1)}) conditional(s32[]{:T(128)} %convert_element_type.8, (f32[16,2,128]{2,1,0:T(2,128)S(1)}, bf16[16,16,256]{2,1,0:T(8,128)(2,1)S(1)}) %tuple.25, (f32[16,2,128]{2,1,0:T(2,128)S(1)}, f32[16,2,128]{2,1,0:T(2,128)S(1)}, f32[16,2,8,128]{3,2,1,0:T(8,128)S(1)}, ...), branch_computations={%region_2.0_spmd, %region_3.0_spmd} | conditional | flops 100663296 | bytes 786448 | solution.py:272
  30.6 0.4 branch_1_fun.2
  31.0 9.8 %all_to_all.24 = bf16[16,16,256]{2,1,0:T(8,128)(2,1)S(1)} all-to-all(bf16[16,16,256]{2,1,0:T(8,128)(2,1)S(1)} %branch_1_fun.2), channel_id=1, replica_groups={{10,13,6,0,9,8,3,12,5,11,2,1,4,15,7,14},{26,29,22,16,25,24,19,28,21,27,..., dimensions={0} | all-to-all | bytes 262144 | tf_op jit(solution)/shard_map/cond/branch_1_fun/all_to_all | solution.py:215
  40.8 0.0 collective-permute-done
  40.8 1.3 %shard_map.68 = bf16[256,256]{1,0:T(8,128)(2,1)} custom-call(s32[2]{0:T(128)S(1)} %pad_add_fusion.place_ref, bf16[256,256]{1,0:T(8,128)(2,1)S(1)} %get-tuple-element.71.query_ref, bf16[16,16,256]{2,1,0:T(8,128)(2,1)S(1)} %get-tuple-element.91.mixed_ref), custom_call_target="tpu_custom_call" | custom-call | flops 65536 | bytes 393216 | tf_op jit(solution)/shard_map/pallas_call | solution.py:274
  (6 shorter events, 0.0 us)
Async XLA Ops:
  1.8 13.6 %copy-start = (bf16[256,256]{1,0:T(8,128)(2,1)S(1)}, bf16[256,256]{1,0:T(8,128)(2,1)}, u32[]{:S(2)}) copy-start(bf16[256,256]{1,0:T(8,128)(2,1)} %query_ref.1) | copy-start | bytes 393220
  1.8 15.1 %all-to-all-start.4 = ((bf16[16,16,256]{2,1,0:T(8,128)(2,1)}), bf16[16,16,256]{2,1,0:T(8,128)(2,1)S(1)}, u32[]{:S(2)}, u32[]{:S(2)}) async-start(bf16[16,16,256]{2,1,0:T(8,128)(2,1)} %shard_map.65), calls=%async_computation.4 | async-start | bytes 262144 | tf_op jit(solution)/shard_map/all_to_all | solution.py:215
  13.1 0.7 %copy-start.1 = (f32[2,16]{1,0:T(2,128)S(1)}, f32[2,16]{1,0:T(2,128)}, u32[]{:S(2)}) copy-start(f32[2,16]{1,0:T(2,128)} %param.16) | copy-start | bytes 388
  13.8 0.7 %copy-start.2 = (f32[2,16]{1,0:T(2,128)S(1)}, f32[2,16]{1,0:T(2,128)}, u32[]{:S(2)}) copy-start(f32[2,16]{1,0:T(2,128)} %param.15) | copy-start | bytes 388
  14.6 0.7 %copy-start.3 = (f32[16]{0:T(128)S(1)}, f32[16]{0:T(128)}, u32[]{:S(2)}) copy-start(f32[16]{0:T(128)} %param.17) | copy-start | bytes 196
  29.3 11.5 %collective-permute-start = (f32[2,128]{1,0:T(2,128)S(1)}, f32[2,128]{1,0:T(2,128)S(1)}, u32[]{:S(2)}, u32[]{:S(2)}) collective-permute-start(f32[2,128]{1,0:T(2,128)S(1)} %shard_map.67), channel_id=1, source_target_pairs={{0,256},{1,257},{2,258},{3,259},{4,260},{5,261},{6,262},{7,263},{8... | collective-permute-start | bytes 3080 | tf_op jit(solution)/shard_map/ppermute | solution.py:254

commit v8 on v7

--- a/solution.py
+++ b/solution.py
@@ -17,8 +17,8 @@
 HALVES = 2
 
 TOKENS_IN = [10, 11, 12, 0, 4, 3, 13, 2, 1, 7, 9, 15, 8, 14, 5, 6]
-STATES = ([11, 8, 0, 4, 5, 15, 6, 7, 3, 12, 9, 1, 13, 2, 10, 14], [9, 8, 7, 13, 4, 0, 14, 12, 1, 3, 10, 11, 5, 6, 15, 2])
-TOKENS_OUT = ([10, 13, 6, 0, 9, 8, 3, 12, 5, 11, 2, 1, 4, 15, 7, 14], [9, 3, 7, 14, 10, 13, 8, 1, 6, 15, 2, 5, 4, 11, 0, 12])
+STATES = [9, 8, 7, 13, 4, 0, 14, 12, 1, 3, 10, 11, 5, 6, 15, 2]
+TOKENS_OUT = [10, 11, 12, 0, 4, 3, 13, 2, 1, 7, 9, 15, 8, 14, 5, 6]
 
 
 def call(body, out_shape, in_specs, flops, nbytes, vmem=16, **kw):
@@ -85,7 +85,7 @@
 
 
 def table_kernel(
-    dims, orders, place_ref, decay_ref, residue_ref, query_ref,
+    dims, order, place_ref, decay_ref, residue_ref, query_ref,
     high_ref, low_ref, step_ref, grow_ref, inside_ref, whole_ref, cross_ref,
     conv_high_ref, conv_low_ref, after_ref, query_out_ref, sem,
 ):
@@ -118,15 +118,13 @@
     shape = inside_ref.shape
     span = blocks * length
     place = place_ref[0]
-    message = lax.broadcasted_iota(jnp.int32, shape, 0)
-    index = jnp.zeros(shape, jnp.int32)
-    for b, members in enumerate(zip(*orders)):
-        index = jnp.where(message == b, jnp.where(place_ref[1] == 0, *members), index)
+    index = lax.broadcasted_iota(jnp.int32, shape, 0)
     gap = place - 1 - index
     away = jnp.maximum(gap, 0) * span
-    inside_ref[...] = jnp.where(gap >= 0, jnp.exp(-decay[None] * away.astype(F32)), 0.0)
+    inside = jnp.where(gap >= 0, jnp.exp(-decay[None] * away.astype(F32)), 0.0)
+    inside_ref[...] = take(inside, order)
     left = (shape[0] - 1 - index) * span
-    whole_ref[...] = jnp.exp(-decay[None] * left.astype(F32))
+    whole_ref[...] = take(jnp.exp(-decay[None] * left.astype(F32)), order)
     cross_ref[...] = jnp.exp(-decay * (place * span).astype(F32))
     fetch.wait()
 
@@ -183,15 +181,10 @@
     add_carried(dims, order, enter + before_ref[...] * cross_ref[...], *refs)
 
 
-def gate_out_kernel(orders, place_ref, query_ref, mixed_ref, out_ref):
+def gate_out_kernel(order, query_ref, mixed_ref, out_ref):
     chan, length = out_ref.shape[1], out_ref.shape[0]
-
-    def gate(order):
-        mixed = take(mixed_ref[...].astype(F32), inverse(order)).reshape(chan, length).T
-        out_ref[...] = (query_ref[...].astype(F32) * mixed).astype(BF16)
-
-    for half, order in enumerate(orders):
-        pl.when(place_ref[1] == half)(functools.partial(gate, order))
+    mixed = take(mixed_ref[...].astype(F32), inverse(order)).reshape(chan, length).T
+    out_ref[...] = (query_ref[...].astype(F32) * mixed).astype(BF16)
 
 
 def on_device(query, keys, values, decay, residue, skip):
@@ -209,7 +202,7 @@
     decay_row = jnp.tile(decay, (1, size))
     residue_row = jnp.tile(residue, (1, size))
     skip_col = skip.reshape(rows, 1)
-    place = jnp.stack([lax.axis_index("yc"), lax.axis_index("zh")]).astype(jnp.int32)
+    place = lax.axis_index("yc").astype(jnp.int32).reshape(1)
 
     def exchange(axis, order):
         return lambda a: lax.all_to_all(
@@ -249,32 +242,32 @@
     )(z, high, low, step, conv_high, conv_low, after, skip_col)
 
     half = lax.axis_index("zh")
-    ends = lax.cond(half == 0, exchange("yc", STATES[0]), lambda a: a, ends)
+    ends = lax.cond(half == 0, exchange("yc", STATES), lambda a: a, ends)
     total = call(total_kernel, vector, [VMEM] * 2, whole, whole)(ends, total_w)
     before = lax.ppermute(total, "zh", [(0, 1)])
 
-    def finish(kernel, order, args):
+    def finish(kernel, args):
         mixed = call(
-            functools.partial(kernel, dims, order), shape((blocks, rows, length), BF16),
+            functools.partial(kernel, dims, TOKENS_OUT), shape((blocks, rows, length), BF16),
             [VMEM] * (len(args) + 3), 12 * lanes * whole, 8 * whole,
         )(*args, grow, after, local)
-        return exchange("chan", order)(mixed)
+        return exchange("chan", TOKENS_OUT)(mixed)
 
     def first_half(ends, mixed):
-        return ends, finish(carry_first_kernel, TOKENS_OUT[0], (ends, inside))
+        return ends, finish(carry_first_kernel, (ends, inside))
 
     def second_half(ends, mixed):
-        return exchange("yc", STATES[1])(ends), mixed
+        return exchange("yc", STATES)(ends), mixed
 
     def second_finish(mixed, before):
-        return finish(carry_second_kernel, TOKENS_OUT[1], (ends, inside, before, cross))
+        return finish(carry_second_kernel, (ends, inside, before, cross))
 
     ends, mixed = lax.cond(half == 0, first_half, second_half, ends, z)
     mixed = lax.cond(half == 1, second_finish, lambda mixed, before: mixed, mixed, before)
     return call(
         functools.partial(gate_out_kernel, TOKENS_OUT), shape((length, chan), BF16),
-        [SMEM] + [VMEM] * 2, whole, 6 * whole,
-    )(place, query_in, mixed)
+        [VMEM] * 2, whole, 6 * whole,
+    )(query_in, mixed)
 
 
 def solution(mesh):

time: 42.8 us -> 41.9 us (0.979)
  Pallas kernels: 5.55 us -> 4.43 us
    pallas_call x1, Pallas kernels: 1.52 us -> 0.95 us  [on_device(): call(functools.partial(table_kernel, dims, STATES), (table, table, vector...]
    pallas_call x1, Pallas kernels: 1.31 us -> 0.76 us  [on_device(): call(functools.partial(gate_out_kernel, TOKENS_OUT), shape((length, chan)...]
  transfers between devices with their start and end apart: 2 -> 2, of which waited for: 0 -> 1; matrix products, arithmetic and copies ran while one was open for 1% -> 1% of each run, Pallas kernels for 5% -> 3%
where the time goes in v8:
time: 41.9 us; the launch traced here: 41.2 us
  blocking collectives  21.6 us (52%)
  starting transfers between devices  12.6 us (30%)
  Pallas kernels  4.43 us (11%)
  local copies, waits for them, and re-layouts  2.19 us (5%)
    all_to_all x2, blocking collectives, exchange(): lax.all_to_all(a, axis, 0, 0, tiled=True, axis_index_groups=[list(order)])  21.6 us
    all_to_all x1, starting transfers between devices, exchange(): lax.all_to_all(a, axis, 0, 0, tiled=True, axis_index_groups=[list(order)])  11.3 us
    unnamed x8, local copies, waits for them, and re-layouts  1.93 us
    pallas_call x1, Pallas kernels, on_device(): call(functools.partial(gate_in_kernel, TOKENS_IN), shape((blocks, rows, l...  1.77 us
    ppermute x1, starting transfers between devices, on_device(): before = lax.ppermute(total, 'zh', [(0, 1)])  1.29 us
    pallas_call x1, Pallas kernels, on_device(): call(functools.partial(table_kernel, dims, STATES), (table, table, vector...  0.95 us
  transfers between devices with their start and end apart: 2, of which 1 were waited for; matrix products, arithmetic and copies ran while one was open for 1% of the time, Pallas kernels for 3%

profile of v8, /device:TPU:1, one launch (start us, length us, event | category | flops | bytes accessed | tf_op | source)
XLA Modules:
  0.0 41.2 jit_solution(14801679804746334370)
XLA Ops:
  0.0 1.8 %shard_map.65 = bf16[16,16,256]{2,1,0:T(8,128)(2,1)} custom-call(bf16[256,256]{1,0:T(8,128)(2,1)} %keys_ref.1, bf16[256,256]{1,0:T(8,128)(2,1)} %values_ref.1), custom_call_target="tpu_custom_call" | custom-call | flops 65536 | bytes 393216 | tf_op jit(solution)/shard_map/pallas_call | solution.py:212
  1.8 0.0 copy-start
  1.8 11.3 %all-to-all-start.4 = ((bf16[16,16,256]{2,1,0:T(8,128)(2,1)}), bf16[16,16,256]{2,1,0:T(8,128)(2,1)S(1)}, u32[]{:S(2)}, u32[]{:S(2)}) async-start(bf16[16,16,256]{2,1,0:T(8,128)(2,1)} %shard_map.65), calls=%async_computation.4 | async-start | bytes 262144 | tf_op jit(solution)/shard_map/all_to_all | solution.py:208
  13.1 0.0 copy-start.1
  13.1 0.7 %copy-done.1 = f32[2,16]{1,0:T(2,128)S(1)} copy-done((f32[2,16]{1,0:T(2,128)S(1)}, f32[2,16]{1,0:T(2,128)}, u32[]{:S(2)}) %copy-start.1) | copy-done | bytes 152
  13.8 0.0 copy-start.2
  13.8 0.1 tile.21.residue_ref
  13.9 0.6 %copy-done.2 = f32[2,16]{1,0:T(2,128)S(1)} copy-done((f32[2,16]{1,0:T(2,128)S(1)}, f32[2,16]{1,0:T(2,128)}, u32[]{:S(2)}) %copy-start.2) | copy-done | bytes 152
  14.5 0.1 tile.9.decay_ref
  14.6 0.0 copy-start.3
  14.6 0.7 %copy-done.3 = f32[16]{0:T(128)S(1)} copy-done((f32[16]{0:T(128)S(1)}, f32[16]{0:T(128)}, u32[]{:S(2)}) %copy-start.3) | copy-done | bytes 88
  15.2 0.1 copy.7.skip_ref
  15.3 0.0 copy-done
  15.3 1.0 %shard_map.64 = (bf16[2,256,128]{2,1,0:T(8,128)(2,1)S(1)}, bf16[2,256,128]{2,1,0:T(8,128)(2,1)S(1)}, f32[2,128]{1,0:T(2,128)S(1)}, f32[16,2,8,128]{3,2,1,0:T(8,1...) custom-call(s32[1]{0:T(128)} %bitcast.place_ref, ...), custom_call_target="tpu_custom_call" | custom-call | flops 6553600 | bytes 1048576 | tf_op jit(solution)/shard_map/pallas_call | solution.py:226
  16.3 0.2 all-to-all-done.4.z_ref
  16.5 0.5 %shard_map.66 = (f32[16,2,128]{2,1,0:T(2,128)S(1)}, f32[16,2,8,256]{3,2,1,0:T(8,128)S(1)}) custom-call(bf16[16,16,256]{2,1,0:T(8,128)(2,1)S(1)} %all-to-all-done.4.z_ref, bf16[2,256,128]{2,1,0:T(8,128)(2,1)S(1)} %get-tuple-element.72.high_ref, bf16[2,256,128]{2,1,0:T(8,128)(2,1)S(1)} %get-tuple-element.73.low_ref, f32[2,128]{1,0:T(2,128)S(1)} %get-tuple-element.74.step_ref, ...), custom_call_target="tpu_custom_call" | custom-call | flops 134217728 | bytes 1048576 | tf_op jit(solution)/shard_map/pallas_call | solution.py:237
  17.1 12.0 %conditional.3 = (f32[16,2,128]{2,1,0:T(2,128)S(1)}) conditional(s32[]{:T(128)} %convert_element_type.8, f32[16,2,128]{2,1,0:T(2,128)S(1)} %get-tuple-element.78, f32[16,2,128]{2,1,0:T(2,128)S(1)} %get-tuple-element.78), branch_computations={%region_0.0_spmd, %region_1.0_spmd} | conditional | bytes 65544 | solution.py:245
  17.1 11.9 %all_to_all.21 = f32[16,2,128]{2,1,0:T(2,128)S(1)} all-to-all(f32[16,2,128]{2,1,0:T(2,128)S(1)} %copy.16), channel_id=1, replica_groups={{144,128,112,208,64,0,224,192,16,48,160,176,80,96,240,32},{145,129,113,..., dimensions={0} | all-to-all | bytes 32768 | tf_op jit(solution)/shard_map/cond/branch_1_fun/all_to_all | solution.py:208
  29.1 1.3 %collective-permute-start = (f32[2,128]{1,0:T(2,128)S(1)}, f32[2,128]{1,0:T(2,128)S(1)}, u32[]{:S(2)}, u32[]{:S(2)}) collective-permute-start(f32[2,128]{1,0:T(2,128)S(1)} %shard_map.67), channel_id=1, source_target_pairs={{0,256},{1,257},{2,258},{3,259},{4,260},{5,261},{6,262},{7,263},{8... | collective-permute-start | bytes 3080 | tf_op jit(solution)/shard_map/ppermute | solution.py:247
  30.4 10.1 %conditional.4 = (f32[16,2,128]{2,1,0:T(2,128)S(1)}, bf16[16,16,256]{2,1,0:T(8,128)(2,1)S(1)}) conditional(s32[]{:T(128)} %convert_element_type.8, (f32[16,2,128]{2,1,0:T(2,128)S(1)}, bf16[16,16,256]{2,1,0:T(8,128)(2,1)S(1)}) %tuple.25, (f32[16,2,128]{2,1,0:T(2,128)S(1)}, f32[16,2,128]{2,1,0:T(2,128)S(1)}, f32[16,2,8,128]{3,2,1,0:T(8,128)S(1)}, ...), branch_computations={%region_2.0_spmd, %region_3.0_spmd} | conditional | flops 100663296 | bytes 786448 | solution.py:265
  30.4 0.4 branch_1_fun.2
  30.8 9.7 %all_to_all.24 = bf16[16,16,256]{2,1,0:T(8,128)(2,1)S(1)} all-to-all(bf16[16,16,256]{2,1,0:T(8,128)(2,1)S(1)} %branch_1_fun.2), channel_id=1, replica_groups={{10,11,12,0,4,3,13,2,1,7,9,15,8,14,5,6},{26,27,28,16,20,19,29,18,17,23,..., dimensions={0} | all-to-all | bytes 262144 | tf_op jit(solution)/shard_map/cond/branch_1_fun/all_to_all | solution.py:208
  40.5 0.0 collective-permute-done
  40.5 0.8 %shard_map.68 = bf16[256,256]{1,0:T(8,128)(2,1)} custom-call(bf16[256,256]{1,0:T(8,128)(2,1)S(1)} %get-tuple-element.71.query_ref, bf16[16,16,256]{2,1,0:T(8,128)(2,1)S(1)} %get-tuple-element.91.mixed_ref), custom_call_target="tpu_custom_call" | custom-call | flops 65536 | bytes 393216 | tf_op jit(solution)/shard_map/pallas_call | solution.py:267
  (5 shorter events, 0.0 us)
Async XLA Ops:
  1.8 13.6 %copy-start = (bf16[256,256]{1,0:T(8,128)(2,1)S(1)}, bf16[256,256]{1,0:T(8,128)(2,1)}, u32[]{:S(2)}) copy-start(bf16[256,256]{1,0:T(8,128)(2,1)} %query_ref.1) | copy-start | bytes 393220
  1.8 14.7 %all-to-all-start.4 = ((bf16[16,16,256]{2,1,0:T(8,128)(2,1)}), bf16[16,16,256]{2,1,0:T(8,128)(2,1)S(1)}, u32[]{:S(2)}, u32[]{:S(2)}) async-start(bf16[16,16,256]{2,1,0:T(8,128)(2,1)} %shard_map.65), calls=%async_computation.4 | async-start | bytes 262144 | tf_op jit(solution)/shard_map/all_to_all | solution.py:208
  13.1 0.7 %copy-start.1 = (f32[2,16]{1,0:T(2,128)S(1)}, f32[2,16]{1,0:T(2,128)}, u32[]{:S(2)}) copy-start(f32[2,16]{1,0:T(2,128)} %param.16) | copy-start | bytes 388
  13.8 0.7 %copy-start.2 = (f32[2,16]{1,0:T(2,128)S(1)}, f32[2,16]{1,0:T(2,128)}, u32[]{:S(2)}) copy-start(f32[2,16]{1,0:T(2,128)} %param.15) | copy-start | bytes 388
  14.6 0.7 %copy-start.3 = (f32[16]{0:T(128)S(1)}, f32[16]{0:T(128)}, u32[]{:S(2)}) copy-start(f32[16]{0:T(128)} %param.17) | copy-start | bytes 196
  29.1 11.4 %collective-permute-start = (f32[2,128]{1,0:T(2,128)S(1)}, f32[2,128]{1,0:T(2,128)S(1)}, u32[]{:S(2)}, u32[]{:S(2)}) collective-permute-start(f32[2,128]{1,0:T(2,128)S(1)} %shard_map.67), channel_id=1, source_target_pairs={{0,256},{1,257},{2,258},{3,259},{4,260},{5,261},{6,262},{7,263},{8... | collective-permute-start | bytes 3080 | tf_op jit(solution)/shard_map/ppermute | solution.py:247

commit v9 on v8

--- a/solution.py
+++ b/solution.py
@@ -16,7 +16,7 @@
 NT = (((1,), (1,)), ((), ()))
 HALVES = 2
 
-TOKENS_IN = [10, 11, 12, 0, 4, 3, 13, 2, 1, 7, 9, 15, 8, 14, 5, 6]
+TOKENS_IN = [10, 13, 2, 4, 0, 14, 3, 5, 1, 8, 15, 6, 9, 7, 12, 11]
 STATES = [9, 8, 7, 13, 4, 0, 14, 12, 1, 3, 10, 11, 5, 6, 15, 2]
 TOKENS_OUT = [10, 11, 12, 0, 4, 3, 13, 2, 1, 7, 9, 15, 8, 14, 5, 6]
 
@@ -46,6 +46,12 @@
     return lax.dot_general(
         a, b, NT, precision=lax.Precision.HIGHEST, preferred_element_type=F32
     )
+
+
+def dot_nt_split(a, high, low):
+    a_high, a_low = split(a)
+    one = functools.partial(lax.dot_general, dimension_numbers=NT, preferred_element_type=F32)
+    return one(a_high, high) + (one(a_high, low) + one(a_low, high))
 
 
 def own_lanes(shape, modes):
@@ -80,8 +86,8 @@
         for copy in copies[h]:
             copy.wait()
         z = keys_buf[h].astype(F32) * values_buf[h].astype(F32)
-        z = take(z.T.reshape(blocks, rows, half), order)
-        out_ref[:, :, h * half : (h + 1) * half] = z.astype(BF16)
+        z = z.astype(BF16).T.reshape(blocks, rows, half)
+        out_ref[:, :, h * half : (h + 1) * half] = take(z, order)
 
 
 def table_kernel(
@@ -113,7 +119,9 @@
         high, low = split(jnp.where(row <= col, dot_nt(rise, fall), 0.0))
         conv_high_ref[g] = high
         conv_low_ref[g] = low
-        after_ref[g] = amplitude * jnp.exp(-rate * (position + 1.0))
+        high, low = split(amplitude * jnp.exp(-rate * (position + 1.0)))
+        after_ref[0, g] = high
+        after_ref[1, g] = low
     step_ref[...] = jnp.exp(-decay * float(length))
     shape = inside_ref.shape
     span = blocks * length
@@ -150,7 +158,8 @@
             state = state * step + jnp.where(mine, ends[b], 0.0)
         packed.append(jnp.sum(state, axis=0, keepdims=True))
         conv = dot(rows, conv_high_ref[g]) + dot(rows, conv_low_ref[g])
-        carried = dot_nt(state_ref[...].reshape(blocks * size, lanes), after_ref[g])
+        states = state_ref[...].reshape(blocks * size, lanes)
+        carried = dot_nt_split(states, after_ref[0, g], after_ref[1, g])
         out_ref[:, g] = (conv + carried).reshape(blocks, size, length) + skipped[:, g]
     packed = jnp.concatenate(packed, axis=0)
     end_ref[...] = jnp.broadcast_to(packed[None], end_ref.shape)
@@ -166,7 +175,8 @@
     mixed = []
     for g in range(groups):
         state = (grow_ref[:, g] * enter[g : g + 1][None]).reshape(blocks * size, lanes)
-        carried = dot_nt(state, after_ref[g]).reshape(blocks, size, length)
+        carried = dot_nt_split(state, after_ref[0, g], after_ref[1, g])
+        carried = carried.reshape(blocks, size, length)
         mixed.append(local_ref[:, g] + carried)
     mixed = jnp.stack(mixed, axis=1).reshape(blocks, groups * size, length)
     out_ref[...] = take(mixed, order).astype(BF16)
@@ -183,8 +193,8 @@
 
 def gate_out_kernel(order, query_ref, mixed_ref, out_ref):
     chan, length = out_ref.shape[1], out_ref.shape[0]
-    mixed = take(mixed_ref[...].astype(F32), inverse(order)).reshape(chan, length).T
-    out_ref[...] = (query_ref[...].astype(F32) * mixed).astype(BF16)
+    mixed = take(mixed_ref[...], inverse(order)).reshape(chan, length).T
+    out_ref[...] = (query_ref[...].astype(F32) * mixed.astype(F32)).astype(BF16)
 
 
 def on_device(query, keys, values, decay, residue, skip):
@@ -228,7 +238,7 @@
         (
             table, table, vector, shape((blocks, groups, size, lanes), F32),
             weights, weights, vector,
-            conv_table, conv_table, shape((groups, length, lanes), F32),
+            conv_table, conv_table, shape((2, groups, length, lanes), BF16),
             shape((length, chan), BF16),
         ),
         [SMEM, VMEM, VMEM, HBM], 100 * whole, 16 * whole,

time: 41.9 us -> 41.1 us (0.981)
  transfers between devices with their start and end apart: 2 -> 2, of which waited for: 1 -> 0; matrix products, arithmetic and copies ran while one was open for 1% -> 1% of each run, Pallas kernels for 3% -> 3%
where the time goes in v9:
time: 41.1 us; the launch traced here: 40.5 us
  blocking collectives  21.4 us (52%)
  starting transfers between devices  12.6 us (31%)
  Pallas kernels  4.16 us (10%)
  local copies, waits for them, and re-layouts  2.19 us (5%)
    all_to_all x2, blocking collectives, exchange(): lax.all_to_all(a, axis, 0, 0, tiled=True, axis_index_groups=[list(order)])  21.4 us
    all_to_all x1, starting transfers between devices, exchange(): lax.all_to_all(a, axis, 0, 0, tiled=True, axis_index_groups=[list(order)])  11.3 us
    unnamed x8, local copies, waits for them, and re-layouts  1.93 us
    pallas_call x1, Pallas kernels, on_device(): call(functools.partial(gate_in_kernel, TOKENS_IN), shape((blocks, rows, l...  1.71 us
    ppermute x1, starting transfers between devices, on_device(): before = lax.ppermute(total, 'zh', [(0, 1)])  1.29 us
    pallas_call x1, Pallas kernels, on_device(): call(functools.partial(table_kernel, dims, STATES), (table, table, vector...  0.97 us
  transfers between devices with their start and end apart: 2, of which 0 were waited for; matrix products, arithmetic and copies ran while one was open for 1% of the time, Pallas kernels for 3%

profile of v9, /device:TPU:1, one launch (start us, length us, event | category | flops | bytes accessed | tf_op | source)
XLA Modules:
  0.0 40.5 jit_solution(12204422864783817554)
XLA Ops:
  0.0 1.7 %shard_map.65 = bf16[16,16,256]{2,1,0:T(8,128)(2,1)} custom-call(bf16[256,256]{1,0:T(8,128)(2,1)} %keys_ref.1, bf16[256,256]{1,0:T(8,128)(2,1)} %values_ref.1), custom_call_target="tpu_custom_call" | custom-call | flops 65536 | bytes 393216 | tf_op jit(solution)/shard_map/pallas_call | solution.py:222
  1.7 0.0 copy-start
  1.7 11.3 %all-to-all-start.4 = ((bf16[16,16,256]{2,1,0:T(8,128)(2,1)}), bf16[16,16,256]{2,1,0:T(8,128)(2,1)S(1)}, u32[]{:S(2)}, u32[]{:S(2)}) async-start(bf16[16,16,256]{2,1,0:T(8,128)(2,1)} %shard_map.65), calls=%async_computation.4 | async-start | bytes 262144 | tf_op jit(solution)/shard_map/all_to_all | solution.py:218
  13.1 0.0 copy-start.1
  13.1 0.7 %copy-done.1 = f32[2,16]{1,0:T(2,128)S(1)} copy-done((f32[2,16]{1,0:T(2,128)S(1)}, f32[2,16]{1,0:T(2,128)}, u32[]{:S(2)}) %copy-start.1) | copy-done | bytes 152
  13.8 0.0 copy-start.2
  13.8 0.1 tile.21.residue_ref
  13.8 0.6 %copy-done.2 = f32[2,16]{1,0:T(2,128)S(1)} copy-done((f32[2,16]{1,0:T(2,128)S(1)}, f32[2,16]{1,0:T(2,128)}, u32[]{:S(2)}) %copy-start.2) | copy-done | bytes 152
  14.4 0.1 tile.9.decay_ref
  14.5 0.0 copy-start.3
  14.5 0.7 %copy-done.3 = f32[16]{0:T(128)S(1)} copy-done((f32[16]{0:T(128)S(1)}, f32[16]{0:T(128)}, u32[]{:S(2)}) %copy-start.3) | copy-done | bytes 88
  15.2 0.1 copy.7.skip_ref
  15.3 0.0 copy-done
  15.3 1.0 %shard_map.64 = (bf16[2,256,128]{2,1,0:T(8,128)(2,1)S(1)}, bf16[2,256,128]{2,1,0:T(8,128)(2,1)S(1)}, f32[2,128]{1,0:T(2,128)S(1)}, f32[16,2,8,128]{3,2,1,0:T(8,1...) custom-call(s32[1]{0:T(128)} %bitcast.place_ref, ...), custom_call_target="tpu_custom_call" | custom-call | flops 6553600 | bytes 1048576 | tf_op jit(solution)/shard_map/pallas_call | solution.py:236
  16.3 0.0 all-to-all-done.4.z_ref
  16.3 0.4 %shard_map.66 = (f32[16,2,128]{2,1,0:T(2,128)S(1)}, f32[16,2,8,256]{3,2,1,0:T(8,128)S(1)}) custom-call(bf16[16,16,256]{2,1,0:T(8,128)(2,1)S(1)} %all-to-all-done.4.z_ref, bf16[2,256,128]{2,1,0:T(8,128)(2,1)S(1)} %get-tuple-element.72.high_ref, bf16[2,256,128]{2,1,0:T(8,128)(2,1)S(1)} %get-tuple-element.73.low_ref, f32[2,128]{1,0:T(2,128)S(1)} %get-tuple-element.74.step_ref, ...), custom_call_target="tpu_custom_call" | custom-call | flops 134217728 | bytes 1048576 | tf_op jit(solution)/shard_map/pallas_call | solution.py:247
  16.7 11.8 %conditional.3 = (f32[16,2,128]{2,1,0:T(2,128)S(1)}) conditional(s32[]{:T(128)} %convert_element_type.8, f32[16,2,128]{2,1,0:T(2,128)S(1)} %get-tuple-element.78, f32[16,2,128]{2,1,0:T(2,128)S(1)} %get-tuple-element.78), branch_computations={%region_0.0_spmd, %region_1.0_spmd} | conditional | bytes 65544 | solution.py:255
  16.7 11.8 %all_to_all.21 = f32[16,2,128]{2,1,0:T(2,128)S(1)} all-to-all(f32[16,2,128]{2,1,0:T(2,128)S(1)} %copy.16), channel_id=1, replica_groups={{144,128,112,208,64,0,224,192,16,48,160,176,80,96,240,32},{145,129,113,..., dimensions={0} | all-to-all | bytes 32768 | tf_op jit(solution)/shard_map/cond/branch_1_fun/all_to_all | solution.py:218
  28.5 1.3 %collective-permute-start = (f32[2,128]{1,0:T(2,128)S(1)}, f32[2,128]{1,0:T(2,128)S(1)}, u32[]{:S(2)}, u32[]{:S(2)}) collective-permute-start(f32[2,128]{1,0:T(2,128)S(1)} %shard_map.67), channel_id=1, source_target_pairs={{0,256},{1,257},{2,258},{3,259},{4,260},{5,261},{6,262},{7,263},{8... | collective-permute-start | bytes 3080 | tf_op jit(solution)/shard_map/ppermute | solution.py:257
  29.8 9.9 %conditional.4 = (f32[16,2,128]{2,1,0:T(2,128)S(1)}, bf16[16,16,256]{2,1,0:T(8,128)(2,1)S(1)}) conditional(s32[]{:T(128)} %convert_element_type.8, (f32[16,2,128]{2,1,0:T(2,128)S(1)}, bf16[16,16,256]{2,1,0:T(8,128)(2,1)S(1)}) %tuple.25, (f32[16,2,128]{2,1,0:T(2,128)S(1)}, f32[16,2,128]{2,1,0:T(2,128)S(1)}, f32[16,2,8,128]{3,2,1,0:T(8,128)S(1)}, ...), branch_computations={%region_2.0_spmd, %region_3.0_spmd} | conditional | flops 100663296 | bytes 786448 | solution.py:275
  29.9 0.3 branch_1_fun.2
  30.1 9.6 %all_to_all.24 = bf16[16,16,256]{2,1,0:T(8,128)(2,1)S(1)} all-to-all(bf16[16,16,256]{2,1,0:T(8,128)(2,1)S(1)} %branch_1_fun.2), channel_id=1, replica_groups={{10,11,12,0,4,3,13,2,1,7,9,15,8,14,5,6},{26,27,28,16,20,19,29,18,17,23,..., dimensions={0} | all-to-all | bytes 262144 | tf_op jit(solution)/shard_map/cond/branch_1_fun/all_to_all | solution.py:218
  39.7 0.0 collective-permute-done
  39.7 0.8 %shard_map.68 = bf16[256,256]{1,0:T(8,128)(2,1)} custom-call(bf16[256,256]{1,0:T(8,128)(2,1)S(1)} %get-tuple-element.71.query_ref, bf16[16,16,256]{2,1,0:T(8,128)(2,1)S(1)} %get-tuple-element.91.mixed_ref), custom_call_target="tpu_custom_call" | custom-call | flops 65536 | bytes 393216 | tf_op jit(solution)/shard_map/pallas_call | solution.py:277
  (5 shorter events, 0.0 us)
Async XLA Ops:
  1.7 13.6 %copy-start = (bf16[256,256]{1,0:T(8,128)(2,1)S(1)}, bf16[256,256]{1,0:T(8,128)(2,1)}, u32[]{:S(2)}) copy-start(bf16[256,256]{1,0:T(8,128)(2,1)} %query_ref.1) | copy-start | bytes 393220
  1.7 14.5 %all-to-all-start.4 = ((bf16[16,16,256]{2,1,0:T(8,128)(2,1)}), bf16[16,16,256]{2,1,0:T(8,128)(2,1)S(1)}, u32[]{:S(2)}, u32[]{:S(2)}) async-start(bf16[16,16,256]{2,1,0:T(8,128)(2,1)} %shard_map.65), calls=%async_computation.4 | async-start | bytes 262144 | tf_op jit(solution)/shard_map/all_to_all | solution.py:218
  13.1 0.7 %copy-start.1 = (f32[2,16]{1,0:T(2,128)S(1)}, f32[2,16]{1,0:T(2,128)}, u32[]{:S(2)}) copy-start(f32[2,16]{1,0:T(2,128)} %param.16) | copy-start | bytes 388
  13.8 0.7 %copy-start.2 = (f32[2,16]{1,0:T(2,128)S(1)}, f32[2,16]{1,0:T(2,128)}, u32[]{:S(2)}) copy-start(f32[2,16]{1,0:T(2,128)} %param.15) | copy-start | bytes 388
  14.5 0.7 %copy-start.3 = (f32[16]{0:T(128)S(1)}, f32[16]{0:T(128)}, u32[]{:S(2)}) copy-start(f32[16]{0:T(128)} %param.17) | copy-start | bytes 196
  28.5 11.2 %collective-permute-start = (f32[2,128]{1,0:T(2,128)S(1)}, f32[2,128]{1,0:T(2,128)S(1)}, u32[]{:S(2)}, u32[]{:S(2)}) collective-permute-start(f32[2,128]{1,0:T(2,128)S(1)} %shard_map.67), channel_id=1, source_target_pairs={{0,256},{1,257},{2,258},{3,259},{4,260},{5,261},{6,262},{7,263},{8... | collective-permute-start | bytes 3080 | tf_op jit(solution)/shard_map/ppermute | solution.py:257

commit v10 on v9

--- a/solution.py
+++ b/solution.py
@@ -51,7 +51,8 @@
 def dot_nt_split(a, high, low):
     a_high, a_low = split(a)
     one = functools.partial(lax.dot_general, dimension_numbers=NT, preferred_element_type=F32)
-    return one(a_high, high) + (one(a_high, low) + one(a_low, high))
+    both = one(jnp.concatenate([a_high, a_low], axis=1), jnp.concatenate([high, high], axis=1))
+    return both + one(a_high, low)
 
 
 def own_lanes(shape, modes):
@@ -150,7 +151,8 @@
     packed = []
     for g in range(groups):
         rows = z[:, g].reshape(blocks * size, length).astype(BF16)
-        ends = (dot(rows, high_ref[g]) + dot(rows, low_ref[g])).reshape(blocks, size, lanes)
+        ends = dot(rows, jnp.concatenate([high_ref[g], low_ref[g]], axis=1))
+        ends = (ends[:, :lanes] + ends[:, lanes:]).reshape(blocks, size, lanes)
         step = step_ref[g : g + 1]
         state = jnp.zeros((size, lanes), F32)
         for b in range(blocks):

time: 41.1 us -> 41.1 us (level)
  no operation moved by 1% of the time
where the time goes in v10:
time: 41.1 us; the launch traced here: 40.5 us
  blocking collectives  21.4 us (52%)
  starting transfers between devices  12.6 us (31%)
  Pallas kernels  4.13 us (10%)
  local copies, waits for them, and re-layouts  2.19 us (5%)
    all_to_all x2, blocking collectives, exchange(): lax.all_to_all(a, axis, 0, 0, tiled=True, axis_index_groups=[list(order)])  21.4 us
    all_to_all x1, starting transfers between devices, exchange(): lax.all_to_all(a, axis, 0, 0, tiled=True, axis_index_groups=[list(order)])  11.3 us
    unnamed x8, local copies, waits for them, and re-layouts  1.93 us
    pallas_call x1, Pallas kernels, on_device(): call(functools.partial(gate_in_kernel, TOKENS_IN), shape((blocks, rows, l...  1.71 us
    ppermute x1, starting transfers between devices, on_device(): before = lax.ppermute(total, 'zh', [(0, 1)])  1.29 us
    pallas_call x1, Pallas kernels, on_device(): call(functools.partial(table_kernel, dims, STATES), (table, table, vector...  0.97 us
  transfers between devices with their start and end apart: 2, of which 0 were waited for; matrix products, arithmetic and copies ran while one was open for 1% of the time, Pallas kernels for 3%

profile of v10, /device:TPU:1, one launch (start us, length us, event | category | flops | bytes accessed | tf_op | source)
XLA Modules:
  0.0 40.5 jit_solution(2045681791620290131)
XLA Ops:
  0.0 1.7 %shard_map.65 = bf16[16,16,256]{2,1,0:T(8,128)(2,1)} custom-call(bf16[256,256]{1,0:T(8,128)(2,1)} %keys_ref.1, bf16[256,256]{1,0:T(8,128)(2,1)} %values_ref.1), custom_call_target="tpu_custom_call" | custom-call | flops 65536 | bytes 393216 | tf_op jit(solution)/shard_map/pallas_call | solution.py:224
  1.7 0.0 copy-start
  1.7 11.3 %all-to-all-start.4 = ((bf16[16,16,256]{2,1,0:T(8,128)(2,1)}), bf16[16,16,256]{2,1,0:T(8,128)(2,1)S(1)}, u32[]{:S(2)}, u32[]{:S(2)}) async-start(bf16[16,16,256]{2,1,0:T(8,128)(2,1)} %shard_map.65), calls=%async_computation.4 | async-start | bytes 262144 | tf_op jit(solution)/shard_map/all_to_all | solution.py:220
  13.1 0.0 copy-start.1
  13.1 0.7 %copy-done.1 = f32[2,16]{1,0:T(2,128)S(1)} copy-done((f32[2,16]{1,0:T(2,128)S(1)}, f32[2,16]{1,0:T(2,128)}, u32[]{:S(2)}) %copy-start.1) | copy-done | bytes 152
  13.8 0.0 copy-start.2
  13.8 0.1 tile.21.residue_ref
  13.8 0.6 %copy-done.2 = f32[2,16]{1,0:T(2,128)S(1)} copy-done((f32[2,16]{1,0:T(2,128)S(1)}, f32[2,16]{1,0:T(2,128)}, u32[]{:S(2)}) %copy-start.2) | copy-done | bytes 152
  14.4 0.1 tile.9.decay_ref
  14.5 0.0 copy-start.3
  14.5 0.7 %copy-done.3 = f32[16]{0:T(128)S(1)} copy-done((f32[16]{0:T(128)S(1)}, f32[16]{0:T(128)}, u32[]{:S(2)}) %copy-start.3) | copy-done | bytes 88
  15.2 0.1 copy.7.skip_ref
  15.3 0.0 copy-done
  15.3 1.0 %shard_map.64 = (bf16[2,256,128]{2,1,0:T(8,128)(2,1)S(1)}, bf16[2,256,128]{2,1,0:T(8,128)(2,1)S(1)}, f32[2,128]{1,0:T(2,128)S(1)}, f32[16,2,8,128]{3,2,1,0:T(8,1...) custom-call(s32[1]{0:T(128)} %bitcast.place_ref, ...), custom_call_target="tpu_custom_call" | custom-call | flops 6553600 | bytes 1048576 | tf_op jit(solution)/shard_map/pallas_call | solution.py:238
  16.3 0.0 all-to-all-done.4.z_ref
  16.3 0.4 shard_map.66
  16.7 11.8 %conditional.3 = (f32[16,2,128]{2,1,0:T(2,128)S(1)}) conditional(s32[]{:T(128)} %convert_element_type.8, f32[16,2,128]{2,1,0:T(2,128)S(1)} %get-tuple-element.78, f32[16,2,128]{2,1,0:T(2,128)S(1)} %get-tuple-element.78), branch_computations={%region_0.0_spmd, %region_1.0_spmd} | conditional | bytes 65544 | solution.py:257
  16.7 11.8 %all_to_all.21 = f32[16,2,128]{2,1,0:T(2,128)S(1)} all-to-all(f32[16,2,128]{2,1,0:T(2,128)S(1)} %copy.16), channel_id=1, replica_groups={{144,128,112,208,64,0,224,192,16,48,160,176,80,96,240,32},{145,129,113,..., dimensions={0} | all-to-all | bytes 32768 | tf_op jit(solution)/shard_map/cond/branch_1_fun/all_to_all | solution.py:220
  28.5 1.3 %collective-permute-start = (f32[2,128]{1,0:T(2,128)S(1)}, f32[2,128]{1,0:T(2,128)S(1)}, u32[]{:S(2)}, u32[]{:S(2)}) collective-permute-start(f32[2,128]{1,0:T(2,128)S(1)} %shard_map.67), channel_id=1, source_target_pairs={{0,256},{1,257},{2,258},{3,259},{4,260},{5,261},{6,262},{7,263},{8... | collective-permute-start | bytes 3080 | tf_op jit(solution)/shard_map/ppermute | solution.py:259
  29.8 9.9 %conditional.4 = (f32[16,2,128]{2,1,0:T(2,128)S(1)}, bf16[16,16,256]{2,1,0:T(8,128)(2,1)S(1)}) conditional(s32[]{:T(128)} %convert_element_type.8, (f32[16,2,128]{2,1,0:T(2,128)S(1)}, bf16[16,16,256]{2,1,0:T(8,128)(2,1)S(1)}) %tuple.25, (f32[16,2,128]{2,1,0:T(2,128)S(1)}, f32[16,2,128]{2,1,0:T(2,128)S(1)}, f32[16,2,8,128]{3,2,1,0:T(8,128)S(1)}, ...), branch_computations={%region_2.0_spmd, %region_3.0_spmd} | conditional | flops 100663296 | bytes 786448 | solution.py:277
  29.8 0.3 branch_1_fun.2
  30.1 9.6 %all_to_all.24 = bf16[16,16,256]{2,1,0:T(8,128)(2,1)S(1)} all-to-all(bf16[16,16,256]{2,1,0:T(8,128)(2,1)S(1)} %branch_1_fun.2), channel_id=1, replica_groups={{10,11,12,0,4,3,13,2,1,7,9,15,8,14,5,6},{26,27,28,16,20,19,29,18,17,23,..., dimensions={0} | all-to-all | bytes 262144 | tf_op jit(solution)/shard_map/cond/branch_1_fun/all_to_all | solution.py:220
  39.7 0.0 collective-permute-done
  39.7 0.8 %shard_map.68 = bf16[256,256]{1,0:T(8,128)(2,1)} custom-call(bf16[256,256]{1,0:T(8,128)(2,1)S(1)} %get-tuple-element.71.query_ref, bf16[16,16,256]{2,1,0:T(8,128)(2,1)S(1)} %get-tuple-element.91.mixed_ref), custom_call_target="tpu_custom_call" | custom-call | flops 65536 | bytes 393216 | tf_op jit(solution)/shard_map/pallas_call | solution.py:279
  (5 shorter events, 0.0 us)
Async XLA Ops:
  1.7 13.6 %copy-start = (bf16[256,256]{1,0:T(8,128)(2,1)S(1)}, bf16[256,256]{1,0:T(8,128)(2,1)}, u32[]{:S(2)}) copy-start(bf16[256,256]{1,0:T(8,128)(2,1)} %query_ref.1) | copy-start | bytes 393220
  1.7 14.5 %all-to-all-start.4 = ((bf16[16,16,256]{2,1,0:T(8,128)(2,1)}), bf16[16,16,256]{2,1,0:T(8,128)(2,1)S(1)}, u32[]{:S(2)}, u32[]{:S(2)}) async-start(bf16[16,16,256]{2,1,0:T(8,128)(2,1)} %shard_map.65), calls=%async_computation.4 | async-start | bytes 262144 | tf_op jit(solution)/shard_map/all_to_all | solution.py:220
  13.1 0.7 %copy-start.1 = (f32[2,16]{1,0:T(2,128)S(1)}, f32[2,16]{1,0:T(2,128)}, u32[]{:S(2)}) copy-start(f32[2,16]{1,0:T(2,128)} %param.16) | copy-start | bytes 388
  13.8 0.7 %copy-start.2 = (f32[2,16]{1,0:T(2,128)S(1)}, f32[2,16]{1,0:T(2,128)}, u32[]{:S(2)}) copy-start(f32[2,16]{1,0:T(2,128)} %param.15) | copy-start | bytes 388
  14.5 0.7 %copy-start.3 = (f32[16]{0:T(128)S(1)}, f32[16]{0:T(128)}, u32[]{:S(2)}) copy-start(f32[16]{0:T(128)} %param.17) | copy-start | bytes 196
  28.5 11.2 %collective-permute-start = (f32[2,128]{1,0:T(2,128)S(1)}, f32[2,128]{1,0:T(2,128)S(1)}, u32[]{:S(2)}, u32[]{:S(2)}) collective-permute-start(f32[2,128]{1,0:T(2,128)S(1)} %shard_map.67), channel_id=1, source_target_pairs={{0,256},{1,257},{2,258},{3,259},{4,260},{5,261},{6,262},{7,263},{8... | collective-permute-start | bytes 3080 | tf_op jit(solution)/shard_map/ppermute | solution.py:259

commit v11 on v10

--- a/solution.py
+++ b/solution.py
@@ -156,11 +156,11 @@
         step = step_ref[g : g + 1]
         state = jnp.zeros((size, lanes), F32)
         for b in range(blocks):
-            state_ref[b] = state
+            state_ref[g, b] = state
             state = state * step + jnp.where(mine, ends[b], 0.0)
         packed.append(jnp.sum(state, axis=0, keepdims=True))
         conv = dot(rows, conv_high_ref[g]) + dot(rows, conv_low_ref[g])
-        states = state_ref[...].reshape(blocks * size, lanes)
+        states = state_ref[g].reshape(blocks * size, lanes)
         carried = dot_nt_split(states, after_ref[0, g], after_ref[1, g])
         out_ref[:, g] = (conv + carried).reshape(blocks, size, length) + skipped[:, g]
     packed = jnp.concatenate(packed, axis=0)
@@ -250,7 +250,7 @@
         functools.partial(block_kernel, dims, TOKENS_IN),
         (weights, shape((blocks, groups, size, length), F32)),
         [VMEM] * 8, 8 * length * whole, 16 * whole,
-        scratch_shapes=[pltpu.VMEM((blocks, size, lanes), F32)],
+        scratch_shapes=[pltpu.VMEM((groups, blocks, size, lanes), F32)],
     )(z, high, low, step, conv_high, conv_low, after, skip_col)
 
     half = lax.axis_index("zh")

time: 41.1 us -> 41.1 us (level)
  no operation moved by 1% of the time
where the time goes in v11:
time: 41.1 us; the launch traced here: 40.5 us
  blocking collectives  21.4 us (52%)
  starting transfers between devices  12.6 us (31%)
  Pallas kernels  4.13 us (10%)
  local copies, waits for them, and re-layouts  2.19 us (5%)
    all_to_all x2, blocking collectives, exchange(): lax.all_to_all(a, axis, 0, 0, tiled=True, axis_index_groups=[list(order)])  21.4 us
    all_to_all x1, starting transfers between devices, exchange(): lax.all_to_all(a, axis, 0, 0, tiled=True, axis_index_groups=[list(order)])  11.3 us
    unnamed x8, local copies, waits for them, and re-layouts  1.93 us
    pallas_call x1, Pallas kernels, on_device(): call(functools.partial(gate_in_kernel, TOKENS_IN), shape((blocks, rows, l...  1.71 us
    ppermute x1, starting transfers between devices, on_device(): before = lax.ppermute(total, 'zh', [(0, 1)])  1.29 us
    pallas_call x1, Pallas kernels, on_device(): call(functools.partial(table_kernel, dims, STATES), (table, table, vector...  0.97 us
  transfers between devices with their start and end apart: 2, of which 0 were waited for; matrix products, arithmetic and copies ran while one was open for 1% of the time, Pallas kernels for 3%

profile of v11, /device:TPU:1, one launch (start us, length us, event | category | flops | bytes accessed | tf_op | source)
XLA Modules:
  0.0 40.5 jit_solution(2045681791620290131)
XLA Ops:
  0.0 1.7 %shard_map.65 = bf16[16,16,256]{2,1,0:T(8,128)(2,1)} custom-call(bf16[256,256]{1,0:T(8,128)(2,1)} %keys_ref.1, bf16[256,256]{1,0:T(8,128)(2,1)} %values_ref.1), custom_call_target="tpu_custom_call" | custom-call | flops 65536 | bytes 393216 | tf_op jit(solution)/shard_map/pallas_call | solution.py:224
  1.7 0.0 copy-start
  1.7 11.3 %all-to-all-start.4 = ((bf16[16,16,256]{2,1,0:T(8,128)(2,1)}), bf16[16,16,256]{2,1,0:T(8,128)(2,1)S(1)}, u32[]{:S(2)}, u32[]{:S(2)}) async-start(bf16[16,16,256]{2,1,0:T(8,128)(2,1)} %shard_map.65), calls=%async_computation.4 | async-start | bytes 262144 | tf_op jit(solution)/shard_map/all_to_all | solution.py:220
  13.1 0.0 copy-start.1
  13.1 0.7 %copy-done.1 = f32[2,16]{1,0:T(2,128)S(1)} copy-done((f32[2,16]{1,0:T(2,128)S(1)}, f32[2,16]{1,0:T(2,128)}, u32[]{:S(2)}) %copy-start.1) | copy-done | bytes 152
  13.8 0.0 copy-start.2
  13.8 0.1 tile.21.residue_ref
  13.8 0.6 %copy-done.2 = f32[2,16]{1,0:T(2,128)S(1)} copy-done((f32[2,16]{1,0:T(2,128)S(1)}, f32[2,16]{1,0:T(2,128)}, u32[]{:S(2)}) %copy-start.2) | copy-done | bytes 152
  14.4 0.1 tile.9.decay_ref
  14.5 0.0 copy-start.3
  14.5 0.7 %copy-done.3 = f32[16]{0:T(128)S(1)} copy-done((f32[16]{0:T(128)S(1)}, f32[16]{0:T(128)}, u32[]{:S(2)}) %copy-start.3) | copy-done | bytes 88
  15.2 0.1 copy.7.skip_ref
  15.3 0.0 copy-done
  15.3 1.0 %shard_map.64 = (bf16[2,256,128]{2,1,0:T(8,128)(2,1)S(1)}, bf16[2,256,128]{2,1,0:T(8,128)(2,1)S(1)}, f32[2,128]{1,0:T(2,128)S(1)}, f32[16,2,8,128]{3,2,1,0:T(8,1...) custom-call(s32[1]{0:T(128)} %bitcast.place_ref, ...), custom_call_target="tpu_custom_call" | custom-call | flops 6553600 | bytes 1048576 | tf_op jit(solution)/shard_map/pallas_call | solution.py:238
  16.3 0.0 all-to-all-done.4.z_ref
  16.3 0.4 shard_map.66
  16.7 11.8 %conditional.3 = (f32[16,2,128]{2,1,0:T(2,128)S(1)}) conditional(s32[]{:T(128)} %convert_element_type.8, f32[16,2,128]{2,1,0:T(2,128)S(1)} %get-tuple-element.78, f32[16,2,128]{2,1,0:T(2,128)S(1)} %get-tuple-element.78), branch_computations={%region_0.0_spmd, %region_1.0_spmd} | conditional | bytes 65544 | solution.py:257
  16.7 11.8 %all_to_all.21 = f32[16,2,128]{2,1,0:T(2,128)S(1)} all-to-all(f32[16,2,128]{2,1,0:T(2,128)S(1)} %copy.16), channel_id=1, replica_groups={{144,128,112,208,64,0,224,192,16,48,160,176,80,96,240,32},{145,129,113,..., dimensions={0} | all-to-all | bytes 32768 | tf_op jit(solution)/shard_map/cond/branch_1_fun/all_to_all | solution.py:220
  28.5 1.3 %collective-permute-start = (f32[2,128]{1,0:T(2,128)S(1)}, f32[2,128]{1,0:T(2,128)S(1)}, u32[]{:S(2)}, u32[]{:S(2)}) collective-permute-start(f32[2,128]{1,0:T(2,128)S(1)} %shard_map.67), channel_id=1, source_target_pairs={{0,256},{1,257},{2,258},{3,259},{4,260},{5,261},{6,262},{7,263},{8... | collective-permute-start | bytes 3080 | tf_op jit(solution)/shard_map/ppermute | solution.py:259
  29.8 9.9 %conditional.4 = (f32[16,2,128]{2,1,0:T(2,128)S(1)}, bf16[16,16,256]{2,1,0:T(8,128)(2,1)S(1)}) conditional(s32[]{:T(128)} %convert_element_type.8, (f32[16,2,128]{2,1,0:T(2,128)S(1)}, bf16[16,16,256]{2,1,0:T(8,128)(2,1)S(1)}) %tuple.25, (f32[16,2,128]{2,1,0:T(2,128)S(1)}, f32[16,2,128]{2,1,0:T(2,128)S(1)}, f32[16,2,8,128]{3,2,1,0:T(8,128)S(1)}, ...), branch_computations={%region_2.0_spmd, %region_3.0_spmd} | conditional | flops 100663296 | bytes 786448 | solution.py:277
  29.8 0.3 branch_1_fun.2
  30.1 9.6 %all_to_all.24 = bf16[16,16,256]{2,1,0:T(8,128)(2,1)S(1)} all-to-all(bf16[16,16,256]{2,1,0:T(8,128)(2,1)S(1)} %branch_1_fun.2), channel_id=1, replica_groups={{10,11,12,0,4,3,13,2,1,7,9,15,8,14,5,6},{26,27,28,16,20,19,29,18,17,23,..., dimensions={0} | all-to-all | bytes 262144 | tf_op jit(solution)/shard_map/cond/branch_1_fun/all_to_all | solution.py:220
  39.7 0.0 collective-permute-done
  39.7 0.8 %shard_map.68 = bf16[256,256]{1,0:T(8,128)(2,1)} custom-call(bf16[256,256]{1,0:T(8,128)(2,1)S(1)} %get-tuple-element.71.query_ref, bf16[16,16,256]{2,1,0:T(8,128)(2,1)S(1)} %get-tuple-element.91.mixed_ref), custom_call_target="tpu_custom_call" | custom-call | flops 65536 | bytes 393216 | tf_op jit(solution)/shard_map/pallas_call | solution.py:279
  (5 shorter events, 0.0 us)
Async XLA Ops:
  1.7 13.6 %copy-start = (bf16[256,256]{1,0:T(8,128)(2,1)S(1)}, bf16[256,256]{1,0:T(8,128)(2,1)}, u32[]{:S(2)}) copy-start(bf16[256,256]{1,0:T(8,128)(2,1)} %query_ref.1) | copy-start | bytes 393220
  1.7 14.5 %all-to-all-start.4 = ((bf16[16,16,256]{2,1,0:T(8,128)(2,1)}), bf16[16,16,256]{2,1,0:T(8,128)(2,1)S(1)}, u32[]{:S(2)}, u32[]{:S(2)}) async-start(bf16[16,16,256]{2,1,0:T(8,128)(2,1)} %shard_map.65), calls=%async_computation.4 | async-start | bytes 262144 | tf_op jit(solution)/shard_map/all_to_all | solution.py:220
  13.1 0.7 %copy-start.1 = (f32[2,16]{1,0:T(2,128)S(1)}, f32[2,16]{1,0:T(2,128)}, u32[]{:S(2)}) copy-start(f32[2,16]{1,0:T(2,128)} %param.16) | copy-start | bytes 388
  13.8 0.7 %copy-start.2 = (f32[2,16]{1,0:T(2,128)S(1)}, f32[2,16]{1,0:T(2,128)}, u32[]{:S(2)}) copy-start(f32[2,16]{1,0:T(2,128)} %param.15) | copy-start | bytes 388
  14.5 0.7 %copy-start.3 = (f32[16]{0:T(128)S(1)}, f32[16]{0:T(128)}, u32[]{:S(2)}) copy-start(f32[16]{0:T(128)} %param.17) | copy-start | bytes 196
  28.5 11.2 %collective-permute-start = (f32[2,128]{1,0:T(2,128)S(1)}, f32[2,128]{1,0:T(2,128)S(1)}, u32[]{:S(2)}, u32[]{:S(2)}) collective-permute-start(f32[2,128]{1,0:T(2,128)S(1)} %shard_map.67), channel_id=1, source_target_pairs={{0,256},{1,257},{2,258},{3,259},{4,260},{5,261},{6,262},{7,263},{8... | collective-permute-start | bytes 3080 | tf_op jit(solution)/shard_map/ppermute | solution.py:259

commit v12 on v10

--- a/solution.py
+++ b/solution.py
@@ -72,7 +72,7 @@
 def gate_in_kernel(order, keys_ref, values_ref, out_ref, keys_buf, values_buf, sems):
     half = keys_buf.shape[1]
     copies = []
-    for h in range(2):
+    for h in range(keys_buf.shape[0]):
         part = pl.ds(h * half, half)
         copies.append(
             [
@@ -83,7 +83,7 @@
         for copy in copies[h]:
             copy.start()
     blocks, rows, _ = out_ref.shape
-    for h in range(2):
+    for h in range(keys_buf.shape[0]):
         for copy in copies[h]:
             copy.wait()
         z = keys_buf[h].astype(F32) * values_buf[h].astype(F32)
@@ -225,9 +225,9 @@
         functools.partial(gate_in_kernel, TOKENS_IN), shape((blocks, rows, length), BF16),
         [HBM] * 2, whole, 6 * whole, 60,
         scratch_shapes=[
-            pltpu.VMEM((2, length // 2, chan), BF16),
-            pltpu.VMEM((2, length // 2, chan), BF16),
-            pltpu.SemaphoreType.DMA((2, 2)),
+            pltpu.VMEM((1, length, chan), BF16),
+            pltpu.VMEM((1, length, chan), BF16),
+            pltpu.SemaphoreType.DMA((1, 2)),
         ],
     )(keys, values)
     z = exchange("chan", TOKENS_IN)(gated)

time: 41.1 us -> 41.1 us (level)
  no operation moved by 1% of the time
where the time goes in v12:
time: 41.1 us; the launch traced here: 40.5 us
  blocking collectives  21.4 us (52%)
  starting transfers between devices  12.6 us (31%)
  Pallas kernels  4.15 us (10%)
  local copies, waits for them, and re-layouts  2.19 us (5%)
    all_to_all x2, blocking collectives, exchange(): lax.all_to_all(a, axis, 0, 0, tiled=True, axis_index_groups=[list(order)])  21.4 us
    all_to_all x1, starting transfers between devices, exchange(): lax.all_to_all(a, axis, 0, 0, tiled=True, axis_index_groups=[list(order)])  11.3 us
    unnamed x8, local copies, waits for them, and re-layouts  1.93 us
    pallas_call x1, Pallas kernels, on_device(): call(functools.partial(gate_in_kernel, TOKENS_IN), shape((blocks, rows, l...  1.73 us
    ppermute x1, starting transfers between devices, on_device(): before = lax.ppermute(total, 'zh', [(0, 1)])  1.29 us
    pallas_call x1, Pallas kernels, on_device(): call(functools.partial(table_kernel, dims, STATES), (table, table, vector...  0.97 us
  transfers between devices with their start and end apart: 2, of which 0 were waited for; matrix products, arithmetic and copies ran while one was open for 1% of the time, Pallas kernels for 3%

profile of v12, /device:TPU:1, one launch (start us, length us, event | category | flops | bytes accessed | tf_op | source)
XLA Modules:
  0.0 40.5 jit_solution(16360618973724613435)
XLA Ops:
  0.0 1.7 %shard_map.65 = bf16[16,16,256]{2,1,0:T(8,128)(2,1)} custom-call(bf16[256,256]{1,0:T(8,128)(2,1)} %keys_ref.1, bf16[256,256]{1,0:T(8,128)(2,1)} %values_ref.1), custom_call_target="tpu_custom_call" | custom-call | flops 65536 | bytes 393216 | tf_op jit(solution)/shard_map/pallas_call | solution.py:224
  1.7 0.0 copy-start
  1.7 11.3 %all-to-all-start.4 = ((bf16[16,16,256]{2,1,0:T(8,128)(2,1)}), bf16[16,16,256]{2,1,0:T(8,128)(2,1)S(1)}, u32[]{:S(2)}, u32[]{:S(2)}) async-start(bf16[16,16,256]{2,1,0:T(8,128)(2,1)} %shard_map.65), calls=%async_computation.4 | async-start | bytes 262144 | tf_op jit(solution)/shard_map/all_to_all | solution.py:220
  13.1 0.0 copy-start.1
  13.1 0.7 %copy-done.1 = f32[2,16]{1,0:T(2,128)S(1)} copy-done((f32[2,16]{1,0:T(2,128)S(1)}, f32[2,16]{1,0:T(2,128)}, u32[]{:S(2)}) %copy-start.1) | copy-done | bytes 152
  13.8 0.0 copy-start.2
  13.8 0.1 tile.21.residue_ref
  13.9 0.6 %copy-done.2 = f32[2,16]{1,0:T(2,128)S(1)} copy-done((f32[2,16]{1,0:T(2,128)S(1)}, f32[2,16]{1,0:T(2,128)}, u32[]{:S(2)}) %copy-start.2) | copy-done | bytes 152
  14.5 0.1 tile.9.decay_ref
  14.5 0.0 copy-start.3
  14.5 0.7 %copy-done.3 = f32[16]{0:T(128)S(1)} copy-done((f32[16]{0:T(128)S(1)}, f32[16]{0:T(128)}, u32[]{:S(2)}) %copy-start.3) | copy-done | bytes 88
  15.2 0.1 copy.7.skip_ref
  15.3 0.0 copy-done
  15.3 1.0 %shard_map.64 = (bf16[2,256,128]{2,1,0:T(8,128)(2,1)S(1)}, bf16[2,256,128]{2,1,0:T(8,128)(2,1)S(1)}, f32[2,128]{1,0:T(2,128)S(1)}, f32[16,2,8,128]{3,2,1,0:T(8,1...) custom-call(s32[1]{0:T(128)} %bitcast.place_ref, ...), custom_call_target="tpu_custom_call" | custom-call | flops 6553600 | bytes 1048576 | tf_op jit(solution)/shard_map/pallas_call | solution.py:238
  16.3 0.0 all-to-all-done.4.z_ref
  16.3 0.4 shard_map.66
  16.7 11.8 %conditional.3 = (f32[16,2,128]{2,1,0:T(2,128)S(1)}) conditional(s32[]{:T(128)} %convert_element_type.8, f32[16,2,128]{2,1,0:T(2,128)S(1)} %get-tuple-element.78, f32[16,2,128]{2,1,0:T(2,128)S(1)} %get-tuple-element.78), branch_computations={%region_0.0_spmd, %region_1.0_spmd} | conditional | bytes 65544 | solution.py:257
  16.7 11.8 %all_to_all.21 = f32[16,2,128]{2,1,0:T(2,128)S(1)} all-to-all(f32[16,2,128]{2,1,0:T(2,128)S(1)} %copy.16), channel_id=1, replica_groups={{144,128,112,208,64,0,224,192,16,48,160,176,80,96,240,32},{145,129,113,..., dimensions={0} | all-to-all | bytes 32768 | tf_op jit(solution)/shard_map/cond/branch_1_fun/all_to_all | solution.py:220
  28.5 1.3 %collective-permute-start = (f32[2,128]{1,0:T(2,128)S(1)}, f32[2,128]{1,0:T(2,128)S(1)}, u32[]{:S(2)}, u32[]{:S(2)}) collective-permute-start(f32[2,128]{1,0:T(2,128)S(1)} %shard_map.67), channel_id=1, source_target_pairs={{0,256},{1,257},{2,258},{3,259},{4,260},{5,261},{6,262},{7,263},{8... | collective-permute-start | bytes 3080 | tf_op jit(solution)/shard_map/ppermute | solution.py:259
  29.8 9.9 %conditional.4 = (f32[16,2,128]{2,1,0:T(2,128)S(1)}, bf16[16,16,256]{2,1,0:T(8,128)(2,1)S(1)}) conditional(s32[]{:T(128)} %convert_element_type.8, (f32[16,2,128]{2,1,0:T(2,128)S(1)}, bf16[16,16,256]{2,1,0:T(8,128)(2,1)S(1)}) %tuple.25, (f32[16,2,128]{2,1,0:T(2,128)S(1)}, f32[16,2,128]{2,1,0:T(2,128)S(1)}, f32[16,2,8,128]{3,2,1,0:T(8,128)S(1)}, ...), branch_computations={%region_2.0_spmd, %region_3.0_spmd} | conditional | flops 100663296 | bytes 786448 | solution.py:277
  29.8 0.3 branch_1_fun.2
  30.1 9.6 %all_to_all.24 = bf16[16,16,256]{2,1,0:T(8,128)(2,1)S(1)} all-to-all(bf16[16,16,256]{2,1,0:T(8,128)(2,1)S(1)} %branch_1_fun.2), channel_id=1, replica_groups={{10,11,12,0,4,3,13,2,1,7,9,15,8,14,5,6},{26,27,28,16,20,19,29,18,17,23,..., dimensions={0} | all-to-all | bytes 262144 | tf_op jit(solution)/shard_map/cond/branch_1_fun/all_to_all | solution.py:220
  39.7 0.0 collective-permute-done
  39.7 0.8 %shard_map.68 = bf16[256,256]{1,0:T(8,128)(2,1)} custom-call(bf16[256,256]{1,0:T(8,128)(2,1)S(1)} %get-tuple-element.71.query_ref, bf16[16,16,256]{2,1,0:T(8,128)(2,1)S(1)} %get-tuple-element.91.mixed_ref), custom_call_target="tpu_custom_call" | custom-call | flops 65536 | bytes 393216 | tf_op jit(solution)/shard_map/pallas_call | solution.py:279
  (5 shorter events, 0.0 us)
Async XLA Ops:
  1.7 13.6 %copy-start = (bf16[256,256]{1,0:T(8,128)(2,1)S(1)}, bf16[256,256]{1,0:T(8,128)(2,1)}, u32[]{:S(2)}) copy-start(bf16[256,256]{1,0:T(8,128)(2,1)} %query_ref.1) | copy-start | bytes 393220
  1.7 14.5 %all-to-all-start.4 = ((bf16[16,16,256]{2,1,0:T(8,128)(2,1)}), bf16[16,16,256]{2,1,0:T(8,128)(2,1)S(1)}, u32[]{:S(2)}, u32[]{:S(2)}) async-start(bf16[16,16,256]{2,1,0:T(8,128)(2,1)} %shard_map.65), calls=%async_computation.4 | async-start | bytes 262144 | tf_op jit(solution)/shard_map/all_to_all | solution.py:220
  13.1 0.7 %copy-start.1 = (f32[2,16]{1,0:T(2,128)S(1)}, f32[2,16]{1,0:T(2,128)}, u32[]{:S(2)}) copy-start(f32[2,16]{1,0:T(2,128)} %param.16) | copy-start | bytes 388
  13.8 0.7 %copy-start.2 = (f32[2,16]{1,0:T(2,128)S(1)}, f32[2,16]{1,0:T(2,128)}, u32[]{:S(2)}) copy-start(f32[2,16]{1,0:T(2,128)} %param.15) | copy-start | bytes 388
  14.5 0.7 %copy-start.3 = (f32[16]{0:T(128)S(1)}, f32[16]{0:T(128)}, u32[]{:S(2)}) copy-start(f32[16]{0:T(128)} %param.17) | copy-start | bytes 196
  28.5 11.2 %collective-permute-start = (f32[2,128]{1,0:T(2,128)S(1)}, f32[2,128]{1,0:T(2,128)S(1)}, u32[]{:S(2)}, u32[]{:S(2)}) collective-permute-start(f32[2,128]{1,0:T(2,128)S(1)} %shard_map.67), channel_id=1, source_target_pairs={{0,256},{1,257},{2,258},{3,259},{4,260},{5,261},{6,262},{7,263},{8... | collective-permute-start | bytes 3080 | tf_op jit(solution)/shard_map/ppermute | solution.py:259
